TPU v7x, 256 devices: a whole 4x4x8 slice. The times are simulated.
256 devices in a mesh: mod: 16 (over z, y_hi), mode: 16 (over y_lo, x, core).
Axes of the slice: x: 4, y: 4 (y_hi: 2, y_lo: 2; y = y_hi * 2 + y_lo), z: 8, core: 2. Of those that a mesh axis runs over, the one named last changes fastest.
Arguments:
- mod_points: int32 [16], P('mod'), may hold values from 0 to 47
- pupil_mask: int32 [256, 256], P('mode'), may hold values 0 or 1
- phase_offset: float32 [256, 256], P('mode'), may hold values from -6 to 6
- modes: bfloat16 [64, 256, 256], P('mode', 'mod'), may hold values from -6 to 6
- block_map: int32 [16], replicated, may hold values from 0 to 15, each once
Outputs:
- tangent: float32 [512, 64, 512], P('mod', 'mode')
Inputs may be any that keep to these rules, and one draw needn't show every extreme that they name: `mod_points`: indices of points on a circle of 48 equally spaced modulation points; repeats are allowed. `block_map`: each of the 16 detector row blocks appears exactly once.
All inputs are finite; a program needn't handle non-finite values. No bound on the sum of `pupil_mask` on one device may be relied on, other than what follows from the above.
Results may differ from a plain program's by a relative error of at most 0.015.
Values may be sent and summed in bfloat16 or wider, within the bound.
No kernel may reach another device: no remote copies, remote signals or barrier semaphores. Data moves between devices by JAX's collectives and lax.ppermute only.
A program may use at most 64 MiB of HBM per device.

v0:
```python
import math

import jax
import jax.numpy as jnp
from jax import lax
from jax.sharding import PartitionSpec as P

NPTS = 48


radius_cells = 6.0


def dft_table(left, right, length):
    turns = left[:, None] * right[None, :] % length
    angle = turns.astype(jnp.float32) * (2.0 * math.pi / length)
    norm = 1.0 / math.sqrt(length)
    return (
        (jnp.cos(angle) * norm).astype(jnp.bfloat16),
        (-jnp.sin(angle) * norm).astype(jnp.bfloat16),
    )


def complex_product(form, left, right):
    real = jnp.einsum(form, left[0], right[0], preferred_element_type=jnp.float32) - jnp.einsum(
        form, left[1], right[1], preferred_element_type=jnp.float32
    )
    imag = jnp.einsum(form, left[0], right[1], preferred_element_type=jnp.float32) + jnp.einsum(
        form, left[1], right[0], preferred_element_type=jnp.float32
    )
    return (real, imag)


def pyramid_parts(length):
    centred = jnp.arange(length, dtype=jnp.int32) - length // 2
    quarter = (jnp.abs(centred)[:, None] + jnp.abs(centred)[None, :]) % 4
    cos_part = (quarter == 0).astype(jnp.float32) - (quarter == 2).astype(jnp.float32)
    sin_part = (quarter == 1).astype(jnp.float32) - (quarter == 3).astype(jnp.float32)
    return (cos_part, sin_part)


def pupil_field(point, phase, mask):
    pupil = phase.shape[0]
    length = 2 * pupil
    theta = point.astype(jnp.float32) * (2.0 * math.pi / NPTS)
    centred = (jnp.arange(pupil, dtype=jnp.int32) - pupil // 2).astype(jnp.float32)
    tilt = (
        2.0
        * math.pi
        * radius_cells
        / length
        * (jnp.cos(theta) * centred[:, None] + jnp.sin(theta) * centred[None, :])
    )
    total = phase + tilt
    return (
        (mask * jnp.cos(total)).astype(jnp.bfloat16),
        (mask * jnp.sin(total)).astype(jnp.bfloat16),
    )


def tangent_terms(fields_re, fields_im, second):
    d_re, d_im = complex_product("fuv,pv->ufp", (fields_re, fields_im), second)
    return 2.0 * (d_re[:, :1] * d_re[:, 1:] + d_im[:, :1] * d_im[:, 1:])


def local(mod_points, pupil_mask, phase_offset, modes, block_map):
    mod_count = lax.axis_size("mod")
    mode_dev = modes.shape[0]
    point_dev = mod_points.shape[0]
    stacked = jnp.stack([phase_offset, pupil_mask.astype(jnp.float32)])
    whole = lax.all_gather(stacked, "mode", axis=1, tiled=True)
    phase = whole[0]
    mask = whole[1]
    pupil = phase.shape[0]
    length = 2 * pupil
    centred_pad = jnp.arange(length, dtype=jnp.int32) - length // 2
    centred_pupil = jnp.arange(pupil, dtype=jnp.int32) - pupil // 2
    first = dft_table(centred_pad, centred_pupil, length)
    second = dft_table(centred_pad, centred_pad, length)
    cos_part, sin_part = pyramid_parts(length)
    factor = float(length * length) / float(pupil * pupil * point_dev * mod_count)
    field_re, field_im = pupil_field(mod_points[0], phase, mask)
    part_re = field_re.astype(jnp.float32)
    part_im = field_im.astype(jnp.float32)
    values = lax.all_gather(modes, "mod", axis=1, tiled=True).astype(jnp.float32)
    shifted = ((-values * part_im).astype(jnp.bfloat16), (values * part_re).astype(jnp.bfloat16))
    columns = (first[0], first[1])
    real, imag = complex_product("un,fnp->fup", columns, shifted)
    own_re, own_im = complex_product("un,np->up", first, (field_re, field_im))
    a_re = jnp.concatenate([own_re[None], real], axis=0).astype(jnp.bfloat16)
    a_im = jnp.concatenate([own_im[None], imag], axis=0).astype(jnp.bfloat16)
    f_re, f_im = complex_product("fup,vp->fuv", (a_re, a_im), first)
    g_re = (cos_part * f_re - sin_part * f_im).astype(jnp.bfloat16)
    g_im = (cos_part * f_im + sin_part * f_re).astype(jnp.bfloat16)
    b_re, b_im = complex_product("um,fmv->fuv", second, (g_re, g_im))
    b_re = b_re.astype(jnp.bfloat16)
    b_im = b_im.astype(jnp.bfloat16)
    fields = (b_re, b_im)
    block_count = block_map.shape[0]
    block_rows = length // block_count
    b_re, b_im = fields
    total = tangent_terms(b_re, b_im, second)
    ordered = total.reshape(block_count, block_rows, mode_dev, length)[block_map].reshape(
        length, mode_dev, length
    )
    summed = lax.psum_scatter(
        ordered.astype(jnp.bfloat16), "mod", scatter_dimension=0, tiled=True
    ).astype(jnp.float32)
    return summed * factor


def solution(mesh):
    placed = (P("mod"), P("mode", None), P("mode", None), P("mode", "mod", None), P())
    return jax.shard_map(
        local, mesh=mesh, in_specs=placed, out_specs=P("mod", "mode", None), check_vma=False
    )
```

profile of v0, /device:TPU:4, one launch (start us, length us, event | category | flops | bytes accessed | tf_op | source)
XLA Modules:
  0.0 347.5 jit_solution(11544509761328396331)
XLA Ops:
  6.5 0.0 all-reduce.3.cloned.1.call-start
  7.4 0.7 convert_bitcast_fusion
  8.1 0.7 pad_maximum_fusion.6
  8.8 18.0 %all_gather.6 = f32[2,256,256]{2,1,0:T(8,128)S(1)} all-gather(f32[2,16,256]{2,1,0:T(8,128)S(1)} %pad_maximum_fusion.6), channel_id=1, replica_groups=mesh['mod'=16,'mode'=16] {'mode'}, dimensions={1}, use_global_device_ids=true | all-gather | bytes 557056 | tf_op jit(solution)/shard_map/all_gather | solution.py:71
  26.8 1.1 fusion.57
  28.0 1.2 fusion.51
  29.2 47.5 %all_gather.7 = bf16[4,256,256]{2,1,0:T(8,128)(2,1)S(1)} all-gather(bf16[4,16,256]{2,1,0:T(8,128)(2,1)} %param.8), channel_id=1, replica_groups=mesh['mod'=16,'mode'=16] {'mod'}, dimensions={1}, use_global_device_ids=true | all-gather | bytes 557056 | tf_op jit(solution)/shard_map/all_gather | solution.py:85
  76.7 2.4 fusion.40
  79.1 3.9 %fusion.36 = f32[4,256,512]{2,1,0:T(8,128)} fusion(bf16[4,256,256]{2,1,0:T(8,128)(2,1)S(1)} %all_gather.7, f32[256,256]{1,0:T(8,128)S(1)} %get-tuple-element.9, s32[256]{0:T(256)S(1)} %iota_add_fusion.1, s32[512]{0:T(512)S(1)} %iota_add_fusion), kind=kOutput, calls=%fused_computation.70 | convolution fusion | flops 271319040 | bytes 2886656 | tf_op jit(solution)/shard_map/un,fnp->fup/dot_general | solution.py:28
  83.0 2.8 fusion.4
  85.9 2.1 fusion.53
  88.0 2.1 fusion.52
  90.1 2.4 fusion.9
  92.4 0.1 copy.27
  92.6 4.8 %fusion.17 = f32[5,512,512]{2,1,0:T(8,128)} fusion(bf16[4,512,256]{1,2,0:T(8,128)(2,1)S(1)} %fusion.4, bf16[1,512,256]{1,2,0:T(8,128)(2,1)S(1)} %copy.27, s32[256]{0:T(256)S(1)} %iota_add_fusion.1, s32[512]{0:T(512)S(1)} %iota_add_fusion), kind=kOutput, calls=%fused_computation.55 | convolution fusion | flops 673972224 | bytes 6556672 | tf_op jit(solution)/shard_map/fup,vp->fuv/dot_general | solution.py:28
  97.4 0.0 copy-start.2
  97.4 4.8 %fusion.18 = f32[5,512,512]{2,1,0:T(8,128)} fusion(bf16[4,512,256]{1,2,0:T(8,128)(2,1)S(1)} %fusion.4, bf16[1,512,256]{1,2,0:T(8,128)(2,1)S(1)} %copy.27, s32[256]{0:T(256)S(1)} %iota_add_fusion.1, s32[512]{0:T(512)S(1)} %iota_add_fusion), kind=kOutput, calls=%fused_computation.56 | convolution fusion | flops 673841152 | bytes 6556672 | tf_op jit(solution)/shard_map/fup,vp->fuv/dot_general | solution.py:25
  102.1 0.0 copy-done.2
  102.1 3.1 fusion.5
  105.2 2.4 fusion.8
  107.6 0.1 copy.31
  107.7 0.0 slice-start
  107.7 0.8 convert_subtract_fusion.1
  108.6 0.0 slice-start.1
  108.6 5.6 %convolution_add_fusion = f32[5,512,512]{2,1,0:T(8,128)S(1)} fusion(f32[5,512,512]{2,1,0:T(8,128)} %fusion.17, bf16[4,512,256]{1,2,0:T(8,128)(2,1)S(1)} %fusion.5, bf16[1,512,256]{1,2,0:T(8,128)(2,1)S(1)} %copy.31, s32[256]{0:T(256)S(1)} %iota_add_fusion.1, s32[512]{0:T(512)S(1)} %iota_add_fusion), kind=kOutput, calls=%fused_computation.13 | convolution fusion | flops 675151872 | bytes 11799552 | tf_op jit(solution)/shard_map/fup,vp->fuv/dot_general | solution.py:28
  114.1 0.0 slice-done
  114.1 0.0 slice-done.1
  114.2 5.1 %add_convert_fusion.1 = (bf16[5,512,512]{2,1,0:T(8,128)(2,1)S(1)}, bf16[5,512,512]{2,1,0:T(8,128)(2,1)S(1)}) fusion(f32[5,512,512]{2,1,0:T(8,128)S(1)} %convolution_add_fusion, f32[512,512]{1,0:T(8,128)S(1)} %get-tuple-element.12, f32[512,512]{1,0:T(8,128)S(1)} %get-tuple-element.11, f32[5,512,512]{2,1,0:T(8,128)S(1)} %bitcast.96, ...), kind=kOutput, calls=%fused_computation.5 | convolution fusion | flops 685768704 | bytes 19139584 | tf_op jit(solution)/shard_map/fup,vp->fuv/dot_general | solution.py:25
  119.2 5.3 %fusion.30 = f32[5,512,512]{2,1,0:T(8,128)S(1)} fusion(bf16[5,512,512]{2,1,0:T(8,128)(2,1)S(1)} %get-tuple-element.5, s32[512]{0:T(512)S(1)} %iota_add_fusion), kind=kOutput, calls=%fused_computation.67 | convolution fusion | flops 1346371584 | bytes 7866368 | tf_op jit(solution)/shard_map/um,fmv->fuv/dot_general | solution.py:28
  124.6 5.4 %fusion.34 = f32[5,512,512]{2,1,0:T(8,128)S(1)} fusion(bf16[5,512,512]{2,1,0:T(8,128)(2,1)S(1)} %get-tuple-element.6, s32[512]{0:T(512)S(1)} %iota_add_fusion), kind=kOutput, calls=%fused_computation.69 | convolution fusion | flops 1346371584 | bytes 7866368 | tf_op jit(solution)/shard_map/um,fmv->fuv/dot_general | solution.py:25
  130.0 7.7 %fusion.2 = bf16[5,512,512]{1,2,0:T(8,128)(2,1)S(1)} fusion(f32[5,512,512]{2,1,0:T(8,128)S(1)} %fusion.34, bf16[5,512,512]{2,1,0:T(8,128)(2,1)S(1)} %get-tuple-element.5, s32[512]{0:T(512)S(1)} %iota_add_fusion), kind=kOutput, calls=%fused_computation.11 | convolution fusion | flops 1349255168 | bytes 10487808 | tf_op jit(solution)/shard_map/um,fmv->fuv/dot_general | solution.py:25
  137.7 5.3 %fusion.32 = f32[512,5,512]{0,2,1:T(8,128)S(1)} fusion(bf16[5,512,512]{1,2,0:T(8,128)(2,1)S(1)} %fusion.2, s32[512]{0:T(512)S(1)} %iota_add_fusion), kind=kOutput, calls=%fused_computation.68 | convolution fusion | flops 1346371584 | bytes 7866368 | tf_op jit(solution)/shard_map/fuv,pv->ufp/dot_general | solution.py:25
  143.1 5.4 %fusion.24 = f32[512,5,512]{0,2,1:T(8,128)S(1)} fusion(bf16[5,512,512]{1,2,0:T(8,128)(2,1)S(1)} %fusion.2, s32[512]{0:T(512)S(1)} %iota_add_fusion), kind=kOutput, calls=%fused_computation.66 | convolution fusion | flops 1346633728 | bytes 7866368 | tf_op jit(solution)/shard_map/fuv,pv->ufp/dot_general | solution.py:28
  148.4 7.8 %fusion.3 = bf16[5,512,512]{1,2,0:T(8,128)(2,1)S(1)} fusion(f32[5,512,512]{2,1,0:T(8,128)S(1)} %fusion.30, bf16[5,512,512]{2,1,0:T(8,128)(2,1)S(1)} %get-tuple-element.6, s32[512]{0:T(512)S(1)} %iota_add_fusion), kind=kOutput, calls=%fused_computation.12 | convolution fusion | flops 1349255168 | bytes 10487808 | tf_op jit(solution)/shard_map/um,fmv->fuv/dot_general | solution.py:28
  156.2 5.4 %subtract_bitcast_fusion = f32[512,5,512]{2,0,1:T(8,128)S(1)} fusion(f32[512,5,512]{0,2,1:T(8,128)S(1)} %fusion.32, bf16[5,512,512]{1,2,0:T(8,128)(2,1)S(1)} %fusion.3, s32[512]{0:T(512)S(1)} %iota_add_fusion), kind=kOutput, calls=%fused_computation.2 | convolution fusion | flops 1347944448 | bytes 13109248 | tf_op jit(solution)/shard_map/fuv,pv->ufp/dot_general | solution.py:25
  161.6 0.1 slice_bitcast_fusion.1
  161.7 0.0 copy-start
  161.7 5.3 %add_bitcast_fusion = f32[512,5,512]{2,0,1:T(8,128)S(1)} fusion(f32[512,5,512]{0,2,1:T(8,128)S(1)} %fusion.24, bf16[5,512,512]{1,2,0:T(8,128)(2,1)S(1)} %fusion.3, s32[512]{0:T(512)S(1)} %iota_add_fusion), kind=kOutput, calls=%fused_computation.1 | convolution fusion | flops 1347682304 | bytes 13109248 | tf_op jit(solution)/shard_map/fuv,pv->ufp/dot_general | solution.py:28
  167.0 0.1 slice_bitcast_fusion
  167.1 0.0 copy-done
  167.1 3.0 fusion.1
  170.2 2.3 gather_fusion
  172.4 0.0 copy-start.1
  172.4 3.1 copy.43
  175.5 0.0 all-reduce.3.cloned.1.call-update
  175.5 0.0 copy-done.1
  175.5 0.6 dynamic-slice
  176.8 162.0 %all-reduce.3.cloned.1.call-done = bf16[512,4,512]{2,1,0:T(4,128)(2,1)} async-done(((bf16[512,4,512]{2,1,0:T(4,128)(2,1)}), bf16[512,4,512]{2,1,0:T(4,128)(2,1)}) %all-reduce.3.cloned.1.call-update) | async-done | bytes 2097168
  338.8 1.7 convert_multiply_fusion.1
  (7 shorter events, 0.0 us)
Async XLA Ops:
  6.5 332.2 %all-reduce.3.cloned.1.call-start = ((), (), s32[]{:S(2)}) async-start(), calls=%async_computation | async-start | bytes 4194304
  97.4 4.8 %copy-start.2 = (f32[4,256,512]{2,1,0:T(8,128)S(1)}, f32[4,256,512]{2,1,0:T(8,128)}, u32[]{:S(2)}) copy-start(f32[4,256,512]{2,1,0:T(8,128)} %fusion.36) | copy-start | bytes 6291460
  107.7 6.4 %slice-start = ((s8[5242880]{0:T(1024)(128)(4,1)}), s8[4194304]{0:T(1024)(128)(4,1)S(1)}, s32[]{:S(2)}) async-start(s8[5242880]{0:T(1024)(128)(4,1)} %bitcast.95), calls=%async_computation.1 | async-start | bytes 8388608
  108.6 5.6 %slice-start.1 = ((s8[5242880]{0:T(1024)(128)(4,1)}), s8[1048576]{0:T(1024)(128)(4,1)S(1)}, s32[]{:S(2)}) async-start(s8[5242880]{0:T(1024)(128)(4,1)} %bitcast.95), calls=%async_computation.2 | async-start | bytes 2097152
  161.7 5.4 %copy-start = (s32[16]{0:T(128)S(1)}, s32[16]{0:T(128)}, u32[]{:S(2)}) copy-start(s32[16]{0:T(128)} %param.9) | copy-start | bytes 196
  172.4 3.1 copy-start.1
Sparse Core Ops, SparseCore 0:
  175.6 163.0 all-reduce.2
where the time goes:
time: 351 us; the launch traced here: 348 us
  waiting for transfers between devices  162 us (46%)
  matrix products  89 us (25%)
  blocking collectives  65.5 us (19%)
  between operations  15.4 us (4%)
  other arithmetic  9.27 us (3%)
  local copies, waits for them, and re-layouts  6.36 us (2%)
    unnamed x2, waiting for transfers between devices  162 us
    all_gather x1, blocking collectives, local(): lax.all_gather(modes, 'mod', axis=1, tiled=True).astype(jnp.float32)  47.5 us
    dot_general x5, matrix products, complex_product(): jnp.einsum(form, left[1], right[0], preferred_element_type=jnp.float32)  24.1 us
    dot_general x5, matrix products, complex_product(): jnp.einsum(form, left[1], right[1], preferred_element_type=jnp.float32)  23.4 us
    dot_general x5, matrix products, complex_product(): jnp.einsum(form, left[0], right[1], preferred_element_type=jnp.float32)  21.5 us
    dot_general x5, matrix products, complex_product(): jnp.einsum(form, left[0], right[0], preferred_element_type=jnp.float32)  20 us
    all_gather x1, blocking collectives, local(): whole = lax.all_gather(stacked, 'mode', axis=1, tiled=True)  18 us
  transfers between devices with their start and end apart: 1, of which 1 were waited for; matrix products, arithmetic and copies ran while one was open for 0% of the time, Pallas kernels for 0%

commit v1 on v0

v1 whole, which is shorter than its diff:
```python
import math

import jax
import jax.numpy as jnp
import numpy as np
from jax import lax
from jax.experimental import pallas as pl
from jax.experimental.pallas import tpu as pltpu
from jax.sharding import PartitionSpec as P

NPTS = 48
radius_cells = 6.0
ORDER = (1, 8, 2, 4)


def sensor_table(length, pupil):
    c = np.arange(length) - length // 2
    n = np.arange(pupil) - pupil // 2
    s = c[:, None] + n[None, :]
    odd = s % 2 != 0
    with np.errstate(divide="ignore"):
        kernel = 2.0 / (length * np.cos(2.0 * np.pi * s / length))
    shift = np.abs(s % length - length // 2) == length // 4
    direct = np.where(shift, np.where(n % 2 == 0, 0.5, -0.5)[None, :], 0.0)
    return np.where(odd, kernel, direct)


def tangent_kernel(block_map, ids, modes_ref, field_ref, rows_ref, second_ref, out_ref, left, base, right, mid, own):
    del block_map
    blocks, height, lanes = modes_ref.shape
    rows, pupil = rows_ref.shape
    fields = out_ref.shape[1]
    me = ids[1]
    for place in range(blocks):
        other = sum(bit for t, bit in enumerate(ORDER) if place >> t & 1)
        block = me ^ other
        part = field_ref[place]
        at = pl.multiple_of(block * 16, 16)
        base[pl.ds(at, 16), :pupil] = part[0]
        base[pl.ds(at, 16), pupil:] = part[1]
    last = height - 16
    point = modes_ref[:, last:, :].astype(jnp.float32)[:, 0, :]
    theta = point * (2.0 * math.pi / NPTS)
    scale = 2.0 * math.pi * radius_cells / (2 * pupil)
    column = lax.broadcasted_iota(jnp.int32, (blocks, pupil), 1)
    odd = column % 2 == 1
    centred = (column - pupil // 2).astype(jnp.float32) * scale

    def factor(tilt):
        angle = jnp.concatenate([tilt] * (pupil // lanes), axis=1) * centred
        cos, sin = jnp.cos(angle), jnp.sin(angle)
        return jnp.where(odd, -sin, cos), jnp.where(odd, cos, sin)

    row_re, row_im = factor(jnp.cos(theta))
    col_re, col_im = factor(jnp.sin(theta))
    table = rows_ref[...]
    for k in range(blocks):
        at = slice(k * rows, (k + 1) * rows)
        left[at, :pupil] = (table * row_re[k : k + 1]).astype(left.dtype)
        left[at, pupil:] = (table * row_im[k : k + 1]).astype(left.dtype)
    half = blocks * rows
    for j in range(fields + 1):
        re = base[:, :pupil]
        im = base[:, pupil:]
        if j == 0:
            right[:pupil, :pupil] = re
            right[:pupil, pupil:] = im
            right[pupil:, :pupil] = -im
            right[pupil:, pupil:] = re
        else:
            at = (j - 1) * 32
            value = jnp.concatenate(
                [modes_ref[:, at : at + 16, :].reshape(pupil, lanes), modes_ref[:, at + 16 : at + 32, :].reshape(pupil, lanes)], axis=1
            )
            real = -value * im
            imag = value * re
            right[:pupil, :pupil] = real
            right[:pupil, pupil:] = imag
            right[pupil:, :pupil] = -imag
            right[pupil:, pupil:] = real
        t = jnp.dot(left[...], right[...], preferred_element_type=jnp.float32)
        for k in range(blocks):
            at = slice(k * rows, (k + 1) * rows)
            t_re, t_im = t[at, :pupil], t[at, pupil:]
            c_re, c_im = col_re[k : k + 1], col_im[k : k + 1]
            mid[at] = (t_re * c_re - t_im * c_im).astype(mid.dtype)
            mid[slice(half + k * rows, half + (k + 1) * rows)] = (t_re * c_im + t_im * c_re).astype(mid.dtype)
        d = jnp.dot(mid[...], second_ref[...], preferred_element_type=jnp.float32)
        if j == 0:
            own[...] = d
        else:
            term = (d * own[...]).reshape(2 * blocks, rows, d.shape[1])
            out_ref[:, j - 1, :] = jnp.sum(term, axis=0) * (2.0 * 4.0 / blocks)


def local(mod_points, pupil_mask, phase_offset, modes, block_map):
    count, height, pupil = modes.shape
    blocks = lax.axis_size("mod")
    length = 2 * pupil
    lanes = 128
    flat = modes.reshape(count, height, pupil // lanes, lanes).transpose(0, 2, 1, 3).reshape(-1, lanes)
    mark = jnp.broadcast_to(mod_points.astype(jnp.bfloat16)[:, None], (16, lanes))
    packed = jnp.concatenate([flat, mark], axis=0)
    spread = jnp.broadcast_to(packed[None], (blocks,) + packed.shape)
    gathered = lax.all_to_all(spread, "mod", 0, 0)

    mask = pupil_mask.astype(jnp.float32)
    field = jnp.stack([mask * jnp.cos(phase_offset), mask * jnp.sin(phase_offset)]).astype(jnp.bfloat16)[None]
    group = lax.axis_size("mode")
    for bit in ORDER:
        field = jnp.concatenate([field, lax.ppermute(field, "mode", [(i, i ^ bit) for i in range(group)])])

    table = sensor_table(length, pupil)
    rows = length // blocks
    ids = jnp.stack([lax.axis_index("mod"), lax.axis_index("mode")]).astype(jnp.int32)
    whole = lambda shape: pl.BlockSpec(shape, lambda i, m, d: (0,) * len(shape))
    return pl.pallas_call(
        tangent_kernel,
        grid_spec=pltpu.PrefetchScalarGridSpec(
            num_scalar_prefetch=2,
            grid=(1,),
            in_specs=[
                whole(gathered.shape),
                whole(field.shape),
                pl.BlockSpec((rows, pupil), lambda i, m, d: (m[d[0]], 0)),
                whole((pupil, length)),
            ],
            out_specs=whole((rows, count, length)),
            scratch_shapes=[
                pltpu.VMEM((length, length), jnp.bfloat16),
                pltpu.VMEM((pupil, length), jnp.bfloat16),
                pltpu.VMEM((length, length), jnp.bfloat16),
                pltpu.VMEM((2 * length, pupil), jnp.bfloat16),
                pltpu.VMEM((2 * length, length), jnp.float32),
            ],
        ),
        out_shape=jax.ShapeDtypeStruct((rows, count, length), jnp.float32),
        compiler_params=pltpu.CompilerParams(vmem_limit_bytes=40 * 2**20),
        cost_estimate=pl.CostEstimate(flops=2_700_000_000, bytes_accessed=2_000_000, transcendentals=0),
        name="tangent",
    )(block_map, ids, gathered, field, jnp.asarray(table, jnp.float32), jnp.asarray(table.T, jnp.bfloat16))


def solution(mesh):
    placed = (P("mod"), P("mode", None), P("mode", None), P("mode", "mod", None), P())
    return jax.shard_map(
        local, mesh=mesh, in_specs=placed, out_specs=P("mod", "mode", None), check_vma=False
    )
```

time: 351 us -> 38.8 us (0.11)
  waiting for transfers between devices: 162 us -> 17.3 us
  matrix products: 89 us -> 0 us
  blocking collectives: 65.5 us -> 0 us
  between operations: 15.4 us -> 0.77 us
  starting transfers between devices: 0.01 us -> 14 us
  other arithmetic: 9.27 us -> 0.19 us
  local copies, waits for them, and re-layouts: 6.36 us -> 1.73 us
  Pallas kernels: 0 us -> 4.52 us
    unnamed x2 -> x0, waiting for transfers between devices: 162 us -> none
    dot_general x20 -> x0, matrix products: 89 us -> none  [the longest x5 24.1 us: complex_product(): jnp.einsum(form, left[1], right[0], preferred_element_type=jnp.float32)]
    all_gather x2 -> x0, blocking collectives: 65.5 us -> none  [the longest x1 47.5 us: local(): lax.all_gather(modes, 'mod', axis=1, tiled=True).astype(jnp.float32)]
    ppermute x0 -> x4, waiting for transfers between devices: none -> 13.3 us  [local(): lax.ppermute(field, 'mode', [(i, i ^ bit) for i in range(group)])]
    all_to_all x0 -> x1, starting transfers between devices: none -> 11.3 us  [local(): gathered = lax.all_to_all(spread, 'mod', 0, 0)]
    mul x4 -> x0, other arithmetic: 5.82 us -> none  [the longest x1 3.02 us: tangent_terms(): return 2.0 * (d_re[:, :1] * d_re[:, 1:] + d_im[:, :1] * d_im[:, 1:])]
    pallas_call x0 -> x1, Pallas kernels: none -> 4.52 us  [local(): pl.pallas_call(tangent_kernel, grid_spec=pltpu.PrefetchScalarGridSpec(num...]
    all_to_all x0 -> x1, waiting for transfers between devices: none -> 3.98 us  [local(): gathered = lax.all_to_all(spread, 'mod', 0, 0)]
  transfers between devices with their start and end apart: 1 -> 5, of which waited for: 1 -> 5; matrix products, arithmetic and copies ran while one was open for 0% -> 1% of each run, Pallas kernels for 0% -> 0%
where the time goes in v1:
time: 38.8 us; the launch traced here: 38.5 us
  waiting for transfers between devices  17.3 us (45%)
  starting transfers between devices  14 us (36%)
  Pallas kernels  4.52 us (12%)
  local copies, waits for them, and re-layouts  1.73 us (4%)
  between operations  0.77 us (2%)
    ppermute x4, waiting for transfers between devices, local(): lax.ppermute(field, 'mode', [(i, i ^ bit) for i in range(group)])  13.3 us
    all_to_all x1, starting transfers between devices, local(): gathered = lax.all_to_all(spread, 'mod', 0, 0)  11.3 us
    pallas_call x1, Pallas kernels, local(): pl.pallas_call(tangent_kernel, grid_spec=pltpu.PrefetchScalarGridSpec(num...  4.52 us
    all_to_all x1, waiting for transfers between devices, local(): gathered = lax.all_to_all(spread, 'mod', 0, 0)  3.98 us
    ppermute x4, starting transfers between devices, local(): lax.ppermute(field, 'mode', [(i, i ^ bit) for i in range(group)])  2.65 us
    broadcast_in_dim x1, local copies, waits for them, and re-layouts, local(): spread = jnp.broadcast_to(packed[None], (blocks,) + packed.shape)  0.9 us
  transfers between devices with their start and end apart: 5, of which 5 were waited for; matrix products, arithmetic and copies ran while one was open for 1% of the time, Pallas kernels for 0%

profile of v1, /device:TPU:4, one launch (start us, length us, event | category | flops | bytes accessed | tf_op | source)
XLA Modules:
  0.0 38.5 jit_solution(3988890599827280631)
XLA Ops:
  0.0 0.8 %reshape.41 = bf16[4,16,2,128]{3,2,1,0:T(2,128)(2,1)S(1)} reshape(bf16[4,16,256]{2,1,0:T(8,128)(2,1)} %param.10) | data formatting | bytes 65536 | tf_op jit(solution)/shard_map/reshape | solution.py:101
  1.5 0.9 %broadcast_in_dim.5 = bf16[16,144,128]{2,1,0:T(8,128)(2,1)} broadcast(bf16[144,128]{1,0:T(8,128)(2,1)S(1)} %concatenate.26), dimensions={1,2} | broadcast | bytes 626688 | tf_op jit(solution)/shard_map/broadcast_in_dim | solution.py:104
  2.4 0.0 copy-start.3
  2.4 0.0 copy-start.4
  2.4 11.3 %all-to-all-start = ((bf16[16,144,128]{2,1,0:T(8,128)(2,1)}), bf16[16,144,128]{2,1,0:T(8,128)(2,1)S(1)}, u32[]{:S(2)}, u32[]{:S(2)}) async-start(bf16[16,144,128]{2,1,0:T(8,128)(2,1)} %broadcast_in_dim.5), calls=%async_computation | async-start | bytes 1179648 | tf_op jit(solution)/shard_map/all_to_all | solution.py:105
  13.7 0.0 copy-done.3
  13.7 0.0 copy-done.4
  13.7 0.1 fusion
  13.8 0.0 copy-start.1
  13.8 0.1 collective-permute-start
  13.9 1.2 %collective-permute-done = bf16[1,2,16,256]{3,2,1,0:T(8,128)(2,1)S(1)} collective-permute-done((bf16[1,2,16,256]{3,2,1,0:T(8,128)(2,1)S(1)}, bf16[1,2,16,256]{3,2,1,0:T(8,128)(2,1)S(1)}, u32[]{:S(2)}, u32[]{:S(2)}) %collective-permute-start) | collective-permute-done | bytes 16416 | tf_op jit(solution)/shard_map/ppermute | solution.py:111
  15.1 0.7 %collective-permute-start.1 = (bf16[2,2,16,256]{3,2,1,0:T(8,128)(2,1)S(1)}, bf16[2,2,16,256]{3,2,1,0:T(8,128)(2,1)S(1)}, u32[]{:S(2)}, u32[]{:S(2)}) collective-permute-start(bf16[2,2,16,256]{3,2,1,0:T(8,128)(2,1)S(1)} %pad_maximum_fusion.2), channel_id=1, source_target_pairs={{0,8},{1,9},{2,10},{3,11},{4,12},{5,13},{6,14},{7,15},{8,0},{9,1},... | collective-permute-start | bytes 98312 | tf_op jit(solution)/shard_map/ppermute | solution.py:111
  15.8 0.1 pad_add_fusion.ids
  15.9 3.2 %collective-permute-done.1 = bf16[2,2,16,256]{3,2,1,0:T(8,128)(2,1)S(1)} collective-permute-done((bf16[2,2,16,256]{3,2,1,0:T(8,128)(2,1)S(1)}, bf16[2,2,16,256]{3,2,1,0:T(8,128)(2,1)S(1)}, u32[]{:S(2)}, u32[]{:S(2)}) %collective-permute-start.1) | collective-permute-done | bytes 32800 | tf_op jit(solution)/shard_map/ppermute | solution.py:111
  19.0 1.3 %collective-permute-start.2 = (bf16[4,2,16,256]{3,2,1,0:T(8,128)(2,1)S(1)}, bf16[4,2,16,256]{3,2,1,0:T(8,128)(2,1)S(1)}, u32[]{:S(2)}, u32[]{:S(2)}) collective-permute-start(bf16[4,2,16,256]{3,2,1,0:T(8,128)(2,1)S(1)} %pad_maximum_fusion.1), channel_id=1, source_target_pairs={{0,2},{1,3},{2,0},{3,1},{4,6},{5,7},{6,4},{7,5},{8,10},{9,11},{10,... | collective-permute-start | bytes 196616 | tf_op jit(solution)/shard_map/ppermute | solution.py:111
  20.3 3.1 %collective-permute-done.2 = bf16[4,2,16,256]{3,2,1,0:T(8,128)(2,1)S(1)} collective-permute-done((bf16[4,2,16,256]{3,2,1,0:T(8,128)(2,1)S(1)}, bf16[4,2,16,256]{3,2,1,0:T(8,128)(2,1)S(1)}, u32[]{:S(2)}, u32[]{:S(2)}) %collective-permute-start.2) | collective-permute-done | bytes 65568 | tf_op jit(solution)/shard_map/ppermute | solution.py:111
  23.4 0.0 copy-start.2
  23.4 0.6 %collective-permute-start.3 = (bf16[8,2,16,256]{3,2,1,0:T(8,128)(2,1)S(1)}, bf16[8,2,16,256]{3,2,1,0:T(8,128)(2,1)S(1)}, u32[]{:S(2)}, u32[]{:S(2)}) collective-permute-start(bf16[8,2,16,256]{3,2,1,0:T(8,128)(2,1)S(1)} %pad_maximum_fusion), channel_id=1, source_target_pairs={{0,4},{1,5},{2,6},{3,7},{4,0},{5,1},{6,2},{7,3},{8,12},{9,13},{10,... | collective-permute-start | bytes 393224 | tf_op jit(solution)/shard_map/ppermute | solution.py:111
  24.0 0.0 copy-start
  24.0 5.9 %collective-permute-done.3 = bf16[8,2,16,256]{3,2,1,0:T(8,128)(2,1)S(1)} collective-permute-done((bf16[8,2,16,256]{3,2,1,0:T(8,128)(2,1)S(1)}, bf16[8,2,16,256]{3,2,1,0:T(8,128)(2,1)S(1)}, u32[]{:S(2)}, u32[]{:S(2)}) %collective-permute-start.3) | collective-permute-done | bytes 131104 | tf_op jit(solution)/shard_map/ppermute | solution.py:111
  30.0 4.0 %all-to-all-done.modes_ref = bf16[16,144,128]{2,1,0:T(8,128)(2,1)S(1)} async-done(((bf16[16,144,128]{2,1,0:T(8,128)(2,1)}), bf16[16,144,128]{2,1,0:T(8,128)(2,1)S(1)}, u32[]{:S(2)}, u32[]{:S(2)}) %all-to-all-start) | async-done | bytes 589856 | tf_op jit(solution)/shard_map/all_to_all | solution.py:105
  34.0 0.0 copy-done.1
  34.0 0.0 copy-done.2
  34.0 0.0 copy-done
  34.0 4.5 %tangent.1 = f32[32,4,512]{2,1,0:T(4,128)} custom-call(s32[16]{0:T(128)S(1)} %copy-done, s32[2]{0:T(128)S(1)} %pad_add_fusion.ids, bf16[16,144,128]{2,1,0:T(8,128)(2,1)S(1)} %all-to-all-done.modes_ref, bf16[16,2,16,256]{3,2,1,0:T(8,128)(2,1)S(1)} %constant_dynamic-update-slice_fusion.field_ref, f32[512,256]{1,0:T(8,128)S(1)} %copy-done.1, ...), custom_call_target="tpu_custom_call" | custom-call | flops 2700000000 | bytes 2000000 | tf_op jit(solution)/shard_map/tangent/pallas_call | solution.py:117
  (10 shorter events, 0.1 us)
Async XLA Ops:
  2.4 11.3 %copy-start.3 = (f32[16,256]{1,0:T(8,128)S(1)}, f32[16,256]{1,0:T(8,128)}, u32[]{:S(2)}) copy-start(f32[16,256]{1,0:T(8,128)} %param.9) | copy-start | bytes 49156
  2.4 11.4 %copy-start.4 = (s32[16,256]{1,0:T(8,128)S(1)}, s32[16,256]{1,0:T(8,128)}, u32[]{:S(2)}) copy-start(s32[16,256]{1,0:T(8,128)} %param.8) | copy-start | bytes 49156
  2.4 31.6 %all-to-all-start = ((bf16[16,144,128]{2,1,0:T(8,128)(2,1)}), bf16[16,144,128]{2,1,0:T(8,128)(2,1)S(1)}, u32[]{:S(2)}, u32[]{:S(2)}) async-start(bf16[16,144,128]{2,1,0:T(8,128)(2,1)} %broadcast_in_dim.5), calls=%async_computation | async-start | bytes 1179648 | tf_op jit(solution)/shard_map/all_to_all | solution.py:105
  13.8 20.2 %copy-start.1 = (f32[512,256]{1,0:T(8,128)S(1)}, f32[512,256]{1,0:T(8,128)}, u32[]{:S(2)}) copy-start(f32[512,256]{1,0:T(8,128)} %constant.11.clone.rows_ref) | copy-start | bytes 1572868
  13.8 1.3 %collective-permute-start = (bf16[1,2,16,256]{3,2,1,0:T(8,128)(2,1)S(1)}, bf16[1,2,16,256]{3,2,1,0:T(8,128)(2,1)S(1)}, u32[]{:S(2)}, u32[]{:S(2)}) collective-permute-start(bf16[1,2,16,256]{3,2,1,0:T(8,128)(2,1)S(1)} %get-tuple-element.7), channel_id=1, source_target_pairs={{0,1},{1,0},{2,3},{3,2},{4,5},{5,4},{6,7},{7,6},{8,9},{9,8},{10,11... | collective-permute-start | bytes 49160 | tf_op jit(solution)/shard_map/ppermute | solution.py:111
  15.1 3.9 %collective-permute-start.1 = (bf16[2,2,16,256]{3,2,1,0:T(8,128)(2,1)S(1)}, bf16[2,2,16,256]{3,2,1,0:T(8,128)(2,1)S(1)}, u32[]{:S(2)}, u32[]{:S(2)}) collective-permute-start(bf16[2,2,16,256]{3,2,1,0:T(8,128)(2,1)S(1)} %pad_maximum_fusion.2), channel_id=1, source_target_pairs={{0,8},{1,9},{2,10},{3,11},{4,12},{5,13},{6,14},{7,15},{8,0},{9,1},... | collective-permute-start | bytes 98312 | tf_op jit(solution)/shard_map/ppermute | solution.py:111
  19.0 4.4 %collective-permute-start.2 = (bf16[4,2,16,256]{3,2,1,0:T(8,128)(2,1)S(1)}, bf16[4,2,16,256]{3,2,1,0:T(8,128)(2,1)S(1)}, u32[]{:S(2)}, u32[]{:S(2)}) collective-permute-start(bf16[4,2,16,256]{3,2,1,0:T(8,128)(2,1)S(1)} %pad_maximum_fusion.1), channel_id=1, source_target_pairs={{0,2},{1,3},{2,0},{3,1},{4,6},{5,7},{6,4},{7,5},{8,10},{9,11},{10,... | collective-permute-start | bytes 196616 | tf_op jit(solution)/shard_map/ppermute | solution.py:111
  23.4 10.6 %copy-start.2 = (bf16[256,512]{1,0:T(8,128)(2,1)S(1)}, bf16[256,512]{1,0:T(8,128)(2,1)}, u32[]{:S(2)}) copy-start(bf16[256,512]{1,0:T(8,128)(2,1)} %constant.12.clone.second_ref) | copy-start | bytes 786436
  23.4 6.6 %collective-permute-start.3 = (bf16[8,2,16,256]{3,2,1,0:T(8,128)(2,1)S(1)}, bf16[8,2,16,256]{3,2,1,0:T(8,128)(2,1)S(1)}, u32[]{:S(2)}, u32[]{:S(2)}) collective-permute-start(bf16[8,2,16,256]{3,2,1,0:T(8,128)(2,1)S(1)} %pad_maximum_fusion), channel_id=1, source_target_pairs={{0,4},{1,5},{2,6},{3,7},{4,0},{5,1},{6,2},{7,3},{8,12},{9,13},{10,... | collective-permute-start | bytes 393224 | tf_op jit(solution)/shard_map/ppermute | solution.py:111
  24.0 10.0 %copy-start = (s32[16]{0:T(128)S(1)}, s32[16]{0:T(128)}, u32[]{:S(2)}) copy-start(s32[16]{0:T(128)} %block_map.1) | copy-start | bytes 196

commit v2 on v1

v2 whole, which is shorter than its diff:
```python
import math

import jax
import jax.numpy as jnp
import numpy as np
from jax import lax
from jax.experimental import pallas as pl
from jax.experimental.pallas import tpu as pltpu
from jax.sharding import PartitionSpec as P

NPTS = 48
radius_cells = 6.0
ORDER = (8, 2, 4, 1)


def sensor_tables(length, pupil):
    c = np.arange(length) - length // 2
    n = np.arange(pupil) - pupil // 2
    s = c[:, None] + n[None, :]
    sign = np.where(c % 2 == 0, 1.0, -1.0)[:, None]
    with np.errstate(divide="ignore"):
        kernel = np.where(s % 2 != 0, sign * 2.0 / (length * np.cos(2.0 * np.pi * s / length)), 0.0)
    direct = np.where(np.abs(s % length - length // 2) == length // 4, 0.5, 0.0)
    place = (pupil - np.arange(pupil)) % pupil
    flip = np.zeros((pupil, pupil))
    flip[np.arange(pupil), place] = 1.0
    return kernel + direct, 2.0 * kernel[place].T, flip


def rotated(t_re, t_im, c_re, c_im):
    return t_re * c_re - t_im * c_im, t_re * c_im + t_im * c_re


def point_kernel(block_map, ids, field_ref, table_ref, left, columns, own, right):
    blocks = field_ref.shape[0]
    length, pupil = table_ref.shape
    rows = length // blocks
    height = pupil // blocks
    me = ids[1]
    points = []
    for place in range(blocks):
        other = sum(bit for t, bit in enumerate(ORDER) if place >> t & 1)
        at = pl.multiple_of((me ^ other) * height, height)
        part = field_ref[place]
        left[pl.ds(length + at, height), :pupil] = part[:height]
        left[pl.ds(length + at, height), pupil:] = part[height : 2 * height]
        points.append(part[2 * height :].astype(jnp.float32)[:1])
    theta = jnp.concatenate(points, axis=0) * (2.0 * math.pi / NPTS)
    scale = 2.0 * math.pi * radius_cells / length
    column = lax.broadcasted_iota(jnp.int32, (blocks, pupil), 1)
    odd = column % 2 == 1
    centred = (column - pupil // 2).astype(jnp.float32) * scale

    def factor(tilt):
        cos, sin = jnp.cos(tilt * centred), jnp.sin(tilt * centred)
        return jnp.where(odd, -sin, cos), jnp.where(odd, cos, sin)

    row_re, row_im = factor(jnp.cos(theta))
    col_re, col_im = factor(jnp.sin(theta))
    columns[0] = col_re
    columns[1] = col_im
    table = table_ref[pl.ds(pl.multiple_of(block_map[ids[0]] * rows, rows), rows), :]
    for k in range(blocks):
        at = slice(k * rows, (k + 1) * rows)
        left[at, :pupil] = (table * row_re[k : k + 1]).astype(left.dtype)
        left[at, pupil:] = (table * row_im[k : k + 1]).astype(left.dtype)
    re = left[length:, :pupil]
    im = left[length:, pupil:]
    right[:pupil, :pupil] = re
    right[:pupil, pupil:] = im
    right[pupil:, :pupil] = -im
    right[pupil:, pupil:] = re
    t = jnp.dot(left[:length], right[...], preferred_element_type=jnp.float32)
    half = blocks * rows
    weight = 4.0 / blocks / 2.0
    for k in range(blocks):
        at = slice(k * rows, (k + 1) * rows)
        low = slice(half + k * rows, half + (k + 1) * rows)
        u_re, u_im = rotated(t[at, :pupil], t[at, pupil:], col_re[k : k + 1], col_im[k : k + 1])
        own[at] = u_re * weight
        own[low] = u_im * weight


def mode_kernel(modes_ref, left, columns, own, mixing_ref, flip_ref, out_ref, other, right, mid, sums):
    count = out_ref.shape[1]
    _, blocks, pupil = columns.shape
    rows = out_ref.shape[0]
    half = blocks * rows
    re = left[half:, :pupil]
    im = left[half:, pupil:]
    other[...] = jnp.dot(own[...].astype(mid.dtype), mixing_ref[...], preferred_element_type=jnp.float32)
    for j in range(count):
        value = modes_ref[:, j].reshape(pupil, pupil)
        real = -value * im
        imag = value * re
        right[:pupil, :pupil] = real
        right[:pupil, pupil:] = imag
        right[pupil:, :pupil] = -imag
        right[pupil:, pupil:] = real
        t = jnp.dot(left[:half], right[...], preferred_element_type=jnp.float32)
        even = jnp.zeros((rows, pupil), jnp.float32)
        odd = jnp.zeros((rows, pupil), jnp.float32)
        for k in range(blocks):
            at = slice(k * rows, (k + 1) * rows)
            low = slice(half + k * rows, half + (k + 1) * rows)
            u_re, u_im = rotated(t[at, :pupil], t[at, pupil:], columns[0, k : k + 1], columns[1, k : k + 1])
            mid[at] = u_re.astype(mid.dtype)
            mid[low] = u_im.astype(mid.dtype)
            even += own[at] * u_re + own[low] * u_im
            odd += other[at] * u_re + other[low] * u_im
        d = jnp.dot(mid[...], mixing_ref[...], preferred_element_type=jnp.float32)
        for k in range(2 * blocks):
            at = slice(k * rows, (k + 1) * rows)
            even += other[at] * d[at]
            odd += own[at] * d[at]
        sums[2 * j * rows : (2 * j + 1) * rows] = even + odd
        sums[(2 * j + 1) * rows : (2 * j + 2) * rows] = even - odd
    total = sums[...]
    high = total.astype(jnp.bfloat16)
    low = (total - high.astype(jnp.float32)).astype(jnp.bfloat16)
    flip = flip_ref[...]
    placed = jnp.dot(high, flip, preferred_element_type=jnp.float32) + jnp.dot(low, flip, preferred_element_type=jnp.float32)
    for j in range(count):
        out_ref[:, j, :pupil] = placed[2 * j * rows : (2 * j + 1) * rows]
        out_ref[:, j, pupil:] = placed[(2 * j + 1) * rows : (2 * j + 2) * rows]


def local(mod_points, pupil_mask, phase_offset, modes, block_map):
    count, height, pupil = modes.shape
    blocks = lax.axis_size("mod")
    group = lax.axis_size("mode")
    length = 2 * pupil
    rows = length // blocks
    gathered = lax.all_to_all(jnp.broadcast_to(modes[None], (blocks,) + modes.shape), "mod", 0, 0)

    point = jnp.broadcast_to(mod_points.astype(jnp.bfloat16)[:, None], (8, pupil))
    swap = [(b * group + g, g * group + b) for b in range(blocks) for g in range(group)]
    point = lax.ppermute(point, ("mod", "mode"), swap)
    mask = pupil_mask.astype(jnp.float32)
    field = jnp.concatenate([mask * jnp.cos(phase_offset), mask * jnp.sin(phase_offset)]).astype(jnp.bfloat16)
    field = jnp.concatenate([field, point])[None]
    for bit in ORDER:
        field = jnp.concatenate([field, lax.ppermute(field, "mode", [(i, i ^ bit) for i in range(group)])])

    table, mixing, flip = sensor_tables(length, pupil)
    table = jnp.asarray(table, jnp.float32)
    mixing = jnp.asarray(mixing, jnp.bfloat16)
    flip = jnp.asarray(flip, jnp.bfloat16)
    ids = jnp.stack([lax.axis_index("mod"), lax.axis_index("mode")]).astype(jnp.int32)
    vmem = pl.BlockSpec(memory_space=pltpu.VMEM)
    smem = pl.BlockSpec(memory_space=pltpu.SMEM)
    limit = pltpu.CompilerParams(vmem_limit_bytes=12 * 2**20)
    left, columns, own = pl.pallas_call(
        point_kernel,
        in_specs=[smem, smem, vmem, vmem],
        out_specs=[vmem] * 3,
        out_shape=[
            jax.ShapeDtypeStruct((length + pupil, length), jnp.bfloat16),
            jax.ShapeDtypeStruct((2, blocks, pupil), jnp.float32),
            jax.ShapeDtypeStruct((2 * length, pupil), jnp.float32),
        ],
        scratch_shapes=[pltpu.VMEM((length, length), jnp.bfloat16)],
        compiler_params=limit,
        cost_estimate=pl.CostEstimate(flops=400_000_000, bytes_accessed=4_000_000, transcendentals=0),
        name="point",
    )(block_map, ids, field, table)
    return pl.pallas_call(
        mode_kernel,
        in_specs=[vmem] * 6,
        out_specs=vmem,
        out_shape=jax.ShapeDtypeStruct((rows, count, length), jnp.float32),
        scratch_shapes=[
            pltpu.VMEM((2 * length, pupil), jnp.float32),
            pltpu.VMEM((length, length), jnp.bfloat16),
            pltpu.VMEM((2 * length, pupil), jnp.bfloat16),
            pltpu.VMEM((2 * count * rows, pupil), jnp.float32),
        ],
        compiler_params=limit,
        cost_estimate=pl.CostEstimate(flops=1_700_000_000, bytes_accessed=5_000_000, transcendentals=0),
        name="tangent",
    )(gathered, left, columns, own, mixing, flip)


def solution(mesh):
    placed = (P("mod"), P("mode", None), P("mode", None), P("mode", "mod", None), P())
    return jax.shard_map(
        local, mesh=mesh, in_specs=placed, out_specs=P("mod", "mode", None), check_vma=False
    )
```

time: 38.8 us -> 41.4 us (1.067)
  the two profiles are of different devices: /device:TPU:4 before, /device:TPU:8 now
where the time goes in v2:
time: 41.4 us; the launch traced here: 41.1 us
  starting transfers between devices  17.3 us (42%)
  waiting for transfers between devices  15.9 us (38%)
  Pallas kernels  5.2 us (13%)
  local copies, waits for them, and re-layouts  1.66 us (4%)
  between operations  0.82 us (2%)
    ppermute x4, waiting for transfers between devices, local(): lax.ppermute(field, 'mode', [(i, i ^ bit) for i in range(group)])  13.5 us
    ppermute x1, starting transfers between devices, local(): point = lax.ppermute(point, ('mod', 'mode'), swap)  8.98 us
    all_to_all x1, starting transfers between devices, local(): lax.all_to_all(jnp.broadcast_to(modes[None], (blocks,) + modes.shape), 'm...  6.49 us
    pallas_call x1, Pallas kernels, local(): pl.pallas_call(mode_kernel, in_specs=[vmem] * 6, out_specs=vmem, out_shap...  4.08 us
    all_to_all x1, waiting for transfers between devices, local(): lax.all_to_all(jnp.broadcast_to(modes[None], (blocks,) + modes.shape), 'm...  2.44 us
    ppermute x4, starting transfers between devices, local(): lax.ppermute(field, 'mode', [(i, i ^ bit) for i in range(group)])  1.8 us
    broadcast_in_dim x1, local copies, waits for them, and re-layouts, local(): jnp.broadcast_to(modes[None], (blocks,) + modes.shape)  1.6 us
    pallas_call x1, Pallas kernels, local(): pl.pallas_call(point_kernel, in_specs=[smem, smem, vmem, vmem], out_specs...  1.12 us
  transfers between devices with their start and end apart: 6, of which 5 were waited for; matrix products, arithmetic and copies ran while one was open for 4% of the time, Pallas kernels for 3%

profile of v2, /device:TPU:8, one launch (start us, length us, event | category | flops | bytes accessed | tf_op | source)
XLA Modules:
  0.0 41.1 jit_solution(9452981538741083840)
XLA Ops:
  0.7 9.0 %collective-permute-start = (bf16[8,256]{1,0:T(8,128)(2,1)S(1)}, bf16[8,256]{1,0:T(8,128)(2,1)S(1)}, u32[]{:S(2)}, u32[]{:S(2)}) collective-permute-start(bf16[8,256]{1,0:T(8,128)(2,1)S(1)} %broadcast_in_dim.19), channel_id=1, source_target_pairs={{0,0},{1,16},{2,32},{3,48},{4,64},{5,80},{6,96},{7,112},{8,128},{9... | collective-permute-start | bytes 12296 | tf_op jit(solution)/shard_map/ppermute | solution.py:138
  9.7 1.6 %broadcast_in_dim.8 = bf16[16,4,16,256]{3,2,1,0:T(8,128)(2,1)} broadcast(bf16[4,16,256]{2,1,0:T(8,128)(2,1)} %param.11), dimensions={1,2,3} | broadcast | bytes 557056 | tf_op jit(solution)/shard_map/broadcast_in_dim | solution.py:134
  11.3 0.0 copy-start.4
  11.3 0.0 copy-start.5
  11.3 6.5 %all-to-all-start = ((bf16[16,4,16,256]{3,2,1,0:T(8,128)(2,1)}), bf16[16,4,16,256]{3,2,1,0:T(8,128)(2,1)S(1)}, u32[]{:S(2)}, u32[]{:S(2)}) async-start(bf16[16,4,16,256]{3,2,1,0:T(8,128)(2,1)} %broadcast_in_dim.8), calls=%async_computation | async-start | bytes 1048576 | tf_op jit(solution)/shard_map/all_to_all | solution.py:134
  17.8 0.0 copy-done.4
  17.8 0.0 copy-done.5
  17.8 0.1 multiply_convert_fusion.1
  17.9 0.0 collective-permute-done
  17.9 0.1 collective-permute-start.1
  18.0 0.1 pad_add_fusion.ids
  18.1 3.7 %collective-permute-done.1 = bf16[1,40,256]{2,1,0:T(8,128)(2,1)S(1)} collective-permute-done((bf16[1,40,256]{2,1,0:T(8,128)(2,1)S(1)}, bf16[1,40,256]{2,1,0:T(8,128)(2,1)S(1)}, u32[]{:S(2)}, u32[]{:S(2)}) %collective-permute-start.1) | collective-permute-done | bytes 20512 | tf_op jit(solution)/shard_map/ppermute | solution.py:143
  21.8 0.1 collective-permute-start.2
  21.9 0.0 copy-start.1
  21.9 3.9 %collective-permute-done.2 = bf16[2,40,256]{2,1,0:T(8,128)(2,1)S(1)} collective-permute-done((bf16[2,40,256]{2,1,0:T(8,128)(2,1)S(1)}, bf16[2,40,256]{2,1,0:T(8,128)(2,1)S(1)}, u32[]{:S(2)}, u32[]{:S(2)}) %collective-permute-start.2) | collective-permute-done | bytes 40992 | tf_op jit(solution)/shard_map/ppermute | solution.py:143
  25.8 1.5 %collective-permute-start.3 = (bf16[4,40,256]{2,1,0:T(8,128)(2,1)S(1)}, bf16[4,40,256]{2,1,0:T(8,128)(2,1)S(1)}, u32[]{:S(2)}, u32[]{:S(2)}) collective-permute-start(bf16[4,40,256]{2,1,0:T(8,128)(2,1)S(1)} %pad_maximum_fusion.1), channel_id=1, source_target_pairs={{0,4},{1,5},{2,6},{3,7},{4,0},{5,1},{6,2},{7,3},{8,12},{9,13},{10,... | collective-permute-start | bytes 245768 | tf_op jit(solution)/shard_map/ppermute | solution.py:143
  27.3 4.5 %collective-permute-done.3 = bf16[4,40,256]{2,1,0:T(8,128)(2,1)S(1)} collective-permute-done((bf16[4,40,256]{2,1,0:T(8,128)(2,1)S(1)}, bf16[4,40,256]{2,1,0:T(8,128)(2,1)S(1)}, u32[]{:S(2)}, u32[]{:S(2)}) %collective-permute-start.3) | collective-permute-done | bytes 81952 | tf_op jit(solution)/shard_map/ppermute | solution.py:143
  31.9 0.1 collective-permute-start.4
  32.0 0.0 copy-start
  32.0 1.3 %collective-permute-done.4 = bf16[8,40,256]{2,1,0:T(8,128)(2,1)S(1)} collective-permute-done((bf16[8,40,256]{2,1,0:T(8,128)(2,1)S(1)}, bf16[8,40,256]{2,1,0:T(8,128)(2,1)S(1)}, u32[]{:S(2)}, u32[]{:S(2)}) %collective-permute-start.4) | collective-permute-done | bytes 163872 | tf_op jit(solution)/shard_map/ppermute | solution.py:143
  33.4 0.0 copy-done.1
  33.4 0.0 copy-done
  33.4 0.0 copy-start.2
  33.4 0.0 copy-start.3
  33.4 1.1 %point.1 = (bf16[768,512]{1,0:T(8,128)(2,1)S(1)}, f32[2,16,256]{2,1,0:T(8,128)S(1)}, f32[1024,256]{1,0:T(8,128)S(1)}) custom-call(s32[16]{0:T(128)S(1)} %copy-done, s32[2]{0:T(128)S(1)} %pad_add_fusion.ids, bf16[16,40,256]{2,1,0:T(8,128)(2,1)S(1)} %constant_dynamic-update-slice_fusion.field_ref, f32[512,256]{1,0:T(8,128)S(1)} %copy-done.1), custom_call_target="tpu_custom_call" | custom-call | flops 400000000 | bytes 4000000 | tf_op jit(solution)/shard_map/point/pallas_call | solution.py:153
  34.6 2.4 %all-to-all-done.modes_ref = bf16[16,4,16,256]{3,2,1,0:T(8,128)(2,1)S(1)} async-done(((bf16[16,4,16,256]{3,2,1,0:T(8,128)(2,1)}), bf16[16,4,16,256]{3,2,1,0:T(8,128)(2,1)S(1)}, u32[]{:S(2)}, u32[]{:S(2)}) %all-to-all-start) | async-done | bytes 524320 | tf_op jit(solution)/shard_map/all_to_all | solution.py:134
  37.0 0.0 copy-done.2
  37.0 0.0 copy-done.3
  37.0 4.1 %tangent.1 = f32[32,4,512]{2,1,0:T(4,128)} custom-call(bf16[16,4,16,256]{3,2,1,0:T(8,128)(2,1)S(1)} %all-to-all-done.modes_ref, bf16[768,512]{1,0:T(8,128)(2,1)S(1)} %get-tuple-element.8.left, f32[2,16,256]{2,1,0:T(8,128)S(1)} %get-tuple-element.9.columns, f32[1024,256]{1,0:T(8,128)S(1)} %get-tuple-element.10.own, bf16[256,256]{1,0:T(8,128)(2,1)S(1)} %copy-done.3, ...), custom_call_target="tpu_custom_call" | custom-call | flops 1700000000 | bytes 5000000 | tf_op jit(solution)/shard_map/tangent/pallas_call | solution.py:167
  (10 shorter events, 0.1 us)
Async XLA Ops:
  0.7 17.2 %collective-permute-start = (bf16[8,256]{1,0:T(8,128)(2,1)S(1)}, bf16[8,256]{1,0:T(8,128)(2,1)S(1)}, u32[]{:S(2)}, u32[]{:S(2)}) collective-permute-start(bf16[8,256]{1,0:T(8,128)(2,1)S(1)} %broadcast_in_dim.19), channel_id=1, source_target_pairs={{0,0},{1,16},{2,32},{3,48},{4,64},{5,80},{6,96},{7,112},{8,128},{9... | collective-permute-start | bytes 12296 | tf_op jit(solution)/shard_map/ppermute | solution.py:138
  11.3 6.5 %copy-start.4 = (f32[16,256]{1,0:T(8,128)S(1)}, f32[16,256]{1,0:T(8,128)}, u32[]{:S(2)}) copy-start(f32[16,256]{1,0:T(8,128)} %param.10) | copy-start | bytes 49156
  11.3 6.5 %copy-start.5 = (s32[16,256]{1,0:T(8,128)S(1)}, s32[16,256]{1,0:T(8,128)}, u32[]{:S(2)}) copy-start(s32[16,256]{1,0:T(8,128)} %param.9) | copy-start | bytes 49156
  11.3 25.7 %all-to-all-start = ((bf16[16,4,16,256]{3,2,1,0:T(8,128)(2,1)}), bf16[16,4,16,256]{3,2,1,0:T(8,128)(2,1)S(1)}, u32[]{:S(2)}, u32[]{:S(2)}) async-start(bf16[16,4,16,256]{3,2,1,0:T(8,128)(2,1)} %broadcast_in_dim.8), calls=%async_computation | async-start | bytes 1048576 | tf_op jit(solution)/shard_map/all_to_all | solution.py:134
  17.9 3.9 %collective-permute-start.1 = (bf16[1,40,256]{2,1,0:T(8,128)(2,1)S(1)}, bf16[1,40,256]{2,1,0:T(8,128)(2,1)S(1)}, u32[]{:S(2)}, u32[]{:S(2)}) collective-permute-start(bf16[1,40,256]{2,1,0:T(8,128)(2,1)S(1)} %maximum_bitcast_fusion), channel_id=1, source_target_pairs={{0,8},{1,9},{2,10},{3,11},{4,12},{5,13},{6,14},{7,15},{8,0},{9,1},... | collective-permute-start | bytes 61448 | tf_op jit(solution)/shard_map/ppermute | solution.py:143
  21.8 4.0 %collective-permute-start.2 = (bf16[2,40,256]{2,1,0:T(8,128)(2,1)S(1)}, bf16[2,40,256]{2,1,0:T(8,128)(2,1)S(1)}, u32[]{:S(2)}, u32[]{:S(2)}) collective-permute-start(bf16[2,40,256]{2,1,0:T(8,128)(2,1)S(1)} %pad_maximum_fusion.2), channel_id=1, source_target_pairs={{0,2},{1,3},{2,0},{3,1},{4,6},{5,7},{6,4},{7,5},{8,10},{9,11},{10,... | collective-permute-start | bytes 122888 | tf_op jit(solution)/shard_map/ppermute | solution.py:143
  21.9 11.5 %copy-start.1 = (f32[512,256]{1,0:T(8,128)S(1)}, f32[512,256]{1,0:T(8,128)}, u32[]{:S(2)}) copy-start(f32[512,256]{1,0:T(8,128)} %constant.13.clone.table_ref) | copy-start | bytes 1572868
  25.8 6.0 %collective-permute-start.3 = (bf16[4,40,256]{2,1,0:T(8,128)(2,1)S(1)}, bf16[4,40,256]{2,1,0:T(8,128)(2,1)S(1)}, u32[]{:S(2)}, u32[]{:S(2)}) collective-permute-start(bf16[4,40,256]{2,1,0:T(8,128)(2,1)S(1)} %pad_maximum_fusion.1), channel_id=1, source_target_pairs={{0,4},{1,5},{2,6},{3,7},{4,0},{5,1},{6,2},{7,3},{8,12},{9,13},{10,... | collective-permute-start | bytes 245768 | tf_op jit(solution)/shard_map/ppermute | solution.py:143
  31.9 1.5 %collective-permute-start.4 = (bf16[8,40,256]{2,1,0:T(8,128)(2,1)S(1)}, bf16[8,40,256]{2,1,0:T(8,128)(2,1)S(1)}, u32[]{:S(2)}, u32[]{:S(2)}) collective-permute-start(bf16[8,40,256]{2,1,0:T(8,128)(2,1)S(1)} %pad_maximum_fusion), channel_id=1, source_target_pairs={{0,1},{1,0},{2,3},{3,2},{4,5},{5,4},{6,7},{7,6},{8,9},{9,8},{10,11... | collective-permute-start | bytes 491528 | tf_op jit(solution)/shard_map/ppermute | solution.py:143
  32.0 1.4 %copy-start = (s32[16]{0:T(128)S(1)}, s32[16]{0:T(128)}, u32[]{:S(2)}) copy-start(s32[16]{0:T(128)} %block_map.1) | copy-start | bytes 196
  33.4 3.6 %copy-start.2 = (bf16[256,256]{1,0:T(8,128)(2,1)S(1)}, bf16[256,256]{1,0:T(8,128)(2,1)}, u32[]{:S(2)}) copy-start(bf16[256,256]{1,0:T(8,128)(2,1)} %constant.15.clone.flip_ref) | copy-start | bytes 393220
  33.4 3.6 %copy-start.3 = (bf16[256,256]{1,0:T(8,128)(2,1)S(1)}, bf16[256,256]{1,0:T(8,128)(2,1)}, u32[]{:S(2)}) copy-start(bf16[256,256]{1,0:T(8,128)(2,1)} %constant.14.clone.mixing_ref) | copy-start | bytes 393220

commit v3 on v1

v3 whole, which is shorter than its diff:
```python
import math

import jax
import jax.numpy as jnp
import numpy as np
from jax import lax
from jax.experimental import pallas as pl
from jax.experimental.pallas import tpu as pltpu
from jax.sharding import PartitionSpec as P

NPTS = 48
radius_cells = 6.0


def peer_order(blocks):
    return [2 * (i % (blocks // 2)) + i // (blocks // 2) for i in range(blocks)]


def sensor_table(length, pupil):
    c = np.arange(length) - length // 2
    n = np.arange(pupil) - pupil // 2
    s = c[:, None] + n[None, :]
    odd = s % 2 != 0
    with np.errstate(divide="ignore"):
        kernel = 2.0 / (length * np.cos(2.0 * np.pi * s / length))
    shift = np.abs(s % length - length // 2) == length // 4
    direct = np.where(shift, np.where(n % 2 == 0, 0.5, -0.5)[None, :], 0.0)
    return np.where(odd, kernel, direct)


def tangent_kernel(block_map, ids, modes_ref, near_ref, far_ref, table_ref, second_ref, out_ref, left, base, right, own):
    blocks = modes_ref.shape[0]
    length, pupil = table_ref.shape
    rows = length // blocks
    height = pupil // blocks
    count = out_ref.shape[1]
    half_group = blocks // 2
    for place in range(blocks):
        core, chip = divmod(place, half_group)
        part = (near_ref, far_ref)[core][chip]
        block = ids[1] ^ (2 * chip + core)
        at = pl.multiple_of(((block & 1) * half_group + (block >> 1)) * height, height)
        base[pl.ds(at, height), :pupil] = part[:height]
        base[pl.ds(at, height), pupil:] = part[height:]
    point = jnp.concatenate([modes_ref[i][count * height :].astype(jnp.float32)[:1] for i in range(blocks)], axis=0)
    theta = point * (2.0 * math.pi / NPTS)
    scale = 2.0 * math.pi * radius_cells / length
    place = lax.broadcasted_iota(jnp.int32, (blocks, pupil), 1)
    odd = (place & 1) == 1
    block = place // height
    row = (2 * (block % half_group) + block // half_group) * height + place % height

    def factor(tilt, index):
        angle = tilt * ((index - pupil // 2).astype(jnp.float32) * scale)
        cos, sin = jnp.cos(angle), jnp.sin(angle)
        return jnp.where(odd, -sin, cos), jnp.where(odd, cos, sin)

    row_re, row_im = factor(jnp.cos(theta), row)
    col_re, col_im = factor(jnp.sin(theta), place)
    table = table_ref[pl.ds(pl.multiple_of(block_map[ids[0]] * rows, rows), rows), :]
    for k in range(blocks):
        at = slice(k * rows, (k + 1) * rows)
        left[at, :pupil] = (table * row_re[k : k + 1]).astype(left.dtype)
        left[at, pupil:] = (table * row_im[k : k + 1]).astype(left.dtype)

    def first(j):
        real = base[:, :pupil]
        imag = base[:, pupil:]
        if j >= 0:
            value = modes_ref[:, j * height : (j + 1) * height].reshape(pupil, pupil)
            real, imag = -value * imag, value * real
        slot = right.at[j % 2]
        slot[:pupil, :pupil] = real
        slot[:pupil, pupil:] = imag
        slot[pupil:, :pupil] = -imag
        slot[pupil:, pupil:] = real
        return jnp.dot(left[...], slot[...], preferred_element_type=jnp.float32)

    def second(t):
        parts = ([], [])
        for k in range(blocks):
            t_re, t_im = t[k * rows : (k + 1) * rows, :pupil], t[k * rows : (k + 1) * rows, pupil:]
            c_re, c_im = col_re[k : k + 1], col_im[k : k + 1]
            parts[0].append(t_re * c_re - t_im * c_im)
            parts[1].append(t_re * c_im + t_im * c_re)
        mixed = jnp.concatenate(parts[0] + parts[1], axis=0).astype(jnp.bfloat16)
        return jnp.dot(mixed, second_ref[...], preferred_element_type=jnp.float32)

    def third(j, d):
        if j < 0:
            own[...] = d * (2.0 * 4.0 / blocks)
            return
        total = jnp.zeros((rows, length), jnp.float32)
        for k in range(2 * blocks):
            at = slice(k * rows, (k + 1) * rows)
            total += own[at] * d[at]
        out_ref[:, j, :] = total

    firsts, seconds = {}, {}
    for step in range(count + 3):
        if step <= count:
            firsts[step] = first(step - 1)
        if 0 <= step - 1 <= count:
            seconds[step - 1] = second(firsts.pop(step - 1))
        if 0 <= step - 2 <= count:
            third(step - 3, seconds.pop(step - 2))


def local(mod_points, pupil_mask, phase_offset, modes, block_map):
    count, height, pupil = modes.shape
    blocks = lax.axis_size("mod")
    group = lax.axis_size("mode")
    length = 2 * pupil
    rows = length // blocks
    order = peer_order(blocks)
    mark = jnp.broadcast_to(mod_points.astype(jnp.bfloat16)[:, None], (8, pupil))
    packed = jnp.concatenate([modes.reshape(count * height, pupil), mark])
    spread = jnp.broadcast_to(packed[None], (blocks,) + packed.shape)
    gathered = lax.all_to_all(spread, "mod", 0, 0, axis_index_groups=[order])

    mask = pupil_mask.astype(jnp.float32)
    field = jnp.concatenate([mask * jnp.cos(phase_offset), mask * jnp.sin(phase_offset)]).astype(jnp.bfloat16)
    swap = lambda x, bit: lax.ppermute(x, "mode", [(i, i ^ bit) for i in range(group)])
    near = jnp.stack([field] + [swap(field, 2 * t) for t in range(1, group // 2)])
    far = swap(near, 1)

    table = sensor_table(length, pupil)
    places = np.concatenate([np.arange(height) + b * height for b in order])
    ids = jnp.stack([lax.axis_index("mod"), lax.axis_index("mode")]).astype(jnp.int32)
    vmem = pl.BlockSpec(memory_space=pltpu.VMEM)
    smem = pl.BlockSpec(memory_space=pltpu.SMEM)
    return pl.pallas_call(
        tangent_kernel,
        in_specs=[smem, smem] + [vmem] * 5,
        out_specs=vmem,
        out_shape=jax.ShapeDtypeStruct((rows, count, length), jnp.float32),
        scratch_shapes=[
            pltpu.VMEM((length, length), jnp.bfloat16),
            pltpu.VMEM((pupil, length), jnp.bfloat16),
            pltpu.VMEM((2, length, length), jnp.bfloat16),
            pltpu.VMEM((2 * length, length), jnp.float32),
        ],
        compiler_params=pltpu.CompilerParams(vmem_limit_bytes=24 * 2**20),
        cost_estimate=pl.CostEstimate(flops=2_700_000_000, bytes_accessed=2_000_000, transcendentals=0),
        name="tangent",
    )(
        block_map,
        ids,
        gathered,
        near,
        far,
        jnp.asarray(table[:, places], jnp.float32),
        jnp.asarray(table.T, jnp.bfloat16),
    )


def solution(mesh):
    placed = (P("mod"), P("mode", None), P("mode", None), P("mode", "mod", None), P())
    return jax.shard_map(
        local, mesh=mesh, in_specs=placed, out_specs=P("mod", "mode", None), check_vma=False
    )
```

time: 38.8 us -> 42.4 us (1.093)
  starting transfers between devices: 14 us -> 21.1 us
  waiting for transfers between devices: 17.3 us -> 13.9 us
  local copies, waits for them, and re-layouts: 1.73 us -> 0.91 us
  other arithmetic: 0.19 us -> 0.88 us
    ppermute x4 -> x8, waiting for transfers between devices: 13.3 us -> 5.31 us  [local(): lax.ppermute(x, 'mode', [(i, i ^ bit) for i in range(group)])]
    ppermute x4 -> x8, starting transfers between devices: 2.65 us -> 9.79 us  [local(): lax.ppermute(x, 'mode', [(i, i ^ bit) for i in range(group)])]
    all_to_all x1, waiting for transfers between devices: 3.98 us -> 8.56 us  [local(): gathered = lax.all_to_all(spread, 'mod', 0, 0, axis_index_groups=[order])]
    reshape x1 -> x0, local copies, waits for them, and re-layouts: 0.77 us -> none  [local(): modes.reshape(count, height, pupil // lanes, lanes).transpose(0, 2, 1, 3)]
    another operation x2 -> x1, other arithmetic: 0.08 us -> 0.8 us  [local(): jnp.stack([mask * jnp.cos(phase_offset), mask * jnp.sin(phase_offset)])]
  transfers between devices with their start and end apart: 5 -> 9, of which waited for: 5 -> 3; matrix products, arithmetic and copies ran while one was open for 1% -> 2% of each run, Pallas kernels for 0% -> 0%
where the time goes in v3:
time: 42.4 us; the launch traced here: 42 us
  starting transfers between devices  21.1 us (50%)
  waiting for transfers between devices  13.9 us (33%)
  Pallas kernels  4.41 us (10%)
  local copies, waits for them, and re-layouts  0.91 us (2%)
  other arithmetic  0.88 us (2%)
  between operations  0.82 us (2%)
    all_to_all x1, starting transfers between devices, local(): gathered = lax.all_to_all(spread, 'mod', 0, 0, axis_index_groups=[order])  11.3 us
    ppermute x8, starting transfers between devices, local(): lax.ppermute(x, 'mode', [(i, i ^ bit) for i in range(group)])  9.79 us
    all_to_all x1, waiting for transfers between devices, local(): gathered = lax.all_to_all(spread, 'mod', 0, 0, axis_index_groups=[order])  8.56 us
    ppermute x8, waiting for transfers between devices, local(): lax.ppermute(x, 'mode', [(i, i ^ bit) for i in range(group)])  5.31 us
    pallas_call x1, Pallas kernels, local(): pl.pallas_call(tangent_kernel, in_specs=[smem, smem] + [vmem] * 5, out_sp...  4.41 us
    broadcast_in_dim x1, local copies, waits for them, and re-layouts, local(): spread = jnp.broadcast_to(packed[None], (blocks,) + packed.shape)  0.86 us
  transfers between devices with their start and end apart: 9, of which 3 were waited for; matrix products, arithmetic and copies ran while one was open for 2% of the time, Pallas kernels for 0%

profile of v3, /device:TPU:4, one launch (start us, length us, event | category | flops | bytes accessed | tf_op | source)
XLA Modules:
  0.0 42.0 jit_solution(5582692003640133099)
XLA Ops:
  0.0 0.8 %multiply_convert_fusion.1 = (bf16[16,256]{1,0:T(8,128)(2,1)S(1)}, bf16[16,256]{1,0:T(8,128)(2,1)S(1)}) fusion(f32[16,256]{1,0:T(8,128)} %param.9, s32[16,256]{1,0:T(8,128)} %param.8), kind=kLoop, calls=%fused_computation.10 | loop fusion | flops 20480 | bytes 49152 | tf_op jit(solution)/shard_map/convert.5
  0.8 0.0 copy-start.3
  0.8 1.3 %collective-permute-start = (bf16[32,256]{1,0:T(8,128)(2,1)S(1)}, bf16[32,256]{1,0:T(8,128)(2,1)S(1)}, u32[]{:S(2)}, u32[]{:S(2)}) collective-permute-start(bf16[32,256]{1,0:T(8,128)(2,1)S(1)} %pad_maximum_fusion), channel_id=1, source_target_pairs={{0,2},{1,3},{2,0},{3,1},{4,6},{5,7},{6,4},{7,5},{8,10},{9,11},{10,... | collective-permute-start | bytes 49160 | tf_op jit(solution)/shard_map/ppermute | solution.py:123
  2.1 1.1 %collective-permute-start.1 = (bf16[32,256]{1,0:T(8,128)(2,1)S(1)}, bf16[32,256]{1,0:T(8,128)(2,1)S(1)}, u32[]{:S(2)}, u32[]{:S(2)}) collective-permute-start(bf16[32,256]{1,0:T(8,128)(2,1)S(1)} %pad_maximum_fusion), channel_id=1, source_target_pairs={{0,4},{1,5},{2,6},{3,7},{4,0},{5,1},{6,2},{7,3},{8,12},{9,13},{10,... | collective-permute-start | bytes 49160 | tf_op jit(solution)/shard_map/ppermute | solution.py:123
  3.3 1.1 %collective-permute-start.2 = (bf16[32,256]{1,0:T(8,128)(2,1)S(1)}, bf16[32,256]{1,0:T(8,128)(2,1)S(1)}, u32[]{:S(2)}, u32[]{:S(2)}) collective-permute-start(bf16[32,256]{1,0:T(8,128)(2,1)S(1)} %pad_maximum_fusion), channel_id=1, source_target_pairs={{0,6},{1,7},{2,4},{3,5},{4,2},{5,3},{6,0},{7,1},{8,14},{9,15},{10,... | collective-permute-start | bytes 49160 | tf_op jit(solution)/shard_map/ppermute | solution.py:123
  4.4 1.6 %collective-permute-start.3 = (bf16[32,256]{1,0:T(8,128)(2,1)S(1)}, bf16[32,256]{1,0:T(8,128)(2,1)S(1)}, u32[]{:S(2)}, u32[]{:S(2)}) collective-permute-start(bf16[32,256]{1,0:T(8,128)(2,1)S(1)} %pad_maximum_fusion), channel_id=1, source_target_pairs={{0,8},{1,9},{2,10},{3,11},{4,12},{5,13},{6,14},{7,15},{8,0},{9,1},... | collective-permute-start | bytes 49160 | tf_op jit(solution)/shard_map/ppermute | solution.py:123
  6.0 2.3 %collective-permute-start.4 = (bf16[32,256]{1,0:T(8,128)(2,1)S(1)}, bf16[32,256]{1,0:T(8,128)(2,1)S(1)}, u32[]{:S(2)}, u32[]{:S(2)}) collective-permute-start(bf16[32,256]{1,0:T(8,128)(2,1)S(1)} %pad_maximum_fusion), channel_id=1, source_target_pairs={{0,10},{1,11},{2,8},{3,9},{4,14},{5,15},{6,12},{7,13},{8,2},{9,3},... | collective-permute-start | bytes 49160 | tf_op jit(solution)/shard_map/ppermute | solution.py:123
  8.9 0.0 copy-done.3
  9.0 0.9 %broadcast_in_dim.5 = bf16[16,72,256]{2,1,0:T(8,128)(2,1)} broadcast(bf16[72,256]{1,0:T(8,128)(2,1)S(1)} %concatenate.21), dimensions={1,2} | broadcast | bytes 626688 | tf_op jit(solution)/shard_map/broadcast_in_dim | solution.py:118
  9.8 0.0 copy-start.1
  9.8 11.3 %all-to-all-start = ((bf16[16,72,256]{2,1,0:T(8,128)(2,1)}), bf16[16,72,256]{2,1,0:T(8,128)(2,1)S(1)}, u32[]{:S(2)}, u32[]{:S(2)}) async-start(bf16[16,72,256]{2,1,0:T(8,128)(2,1)} %broadcast_in_dim.5), calls=%async_computation | async-start | bytes 1179648 | tf_op jit(solution)/shard_map/all_to_all | solution.py:119
  21.2 0.0 copy-start.2
  21.2 0.0 collective-permute-done
  21.2 0.1 collective-permute-start.5
  21.3 0.0 collective-permute-done.1
  21.3 2.2 %collective-permute-start.6 = (bf16[32,256]{1,0:T(8,128)(2,1)S(1)}, bf16[32,256]{1,0:T(8,128)(2,1)S(1)}, u32[]{:S(2)}, u32[]{:S(2)}) collective-permute-start(bf16[32,256]{1,0:T(8,128)(2,1)S(1)} %pad_maximum_fusion), channel_id=1, source_target_pairs={{0,14},{1,15},{2,12},{3,13},{4,10},{5,11},{6,8},{7,9},{8,6},{9,7},... | collective-permute-start | bytes 49160 | tf_op jit(solution)/shard_map/ppermute | solution.py:123
  23.5 0.0 collective-permute-done.2
  23.5 0.0 collective-permute-done.3
  23.5 0.0 collective-permute-done.4
  23.5 4.1 %collective-permute-done.5 = bf16[32,256]{1,0:T(8,128)(2,1)S(1)} collective-permute-done((bf16[32,256]{1,0:T(8,128)(2,1)S(1)}, bf16[32,256]{1,0:T(8,128)(2,1)S(1)}, u32[]{:S(2)}, u32[]{:S(2)}) %collective-permute-start.5) | collective-permute-done | bytes 16416 | tf_op jit(solution)/shard_map/ppermute | solution.py:123
  27.6 0.0 collective-permute-done.6
  27.6 0.1 collective-permute-start.7
  27.7 0.0 copy-start
  27.7 0.1 pad_add_fusion.ids
  27.8 1.2 %collective-permute-done.7.far_ref = bf16[8,32,256]{2,1,0:T(8,128)(2,1)S(1)} collective-permute-done((bf16[8,32,256]{2,1,0:T(8,128)(2,1)S(1)}, bf16[8,32,256]{2,1,0:T(8,128)(2,1)S(1)}, u32[]{:S(2)}, u32[]{:S(2)}) %collective-permute-start.7) | collective-permute-done | bytes 131104 | tf_op jit(solution)/shard_map/ppermute | solution.py:123
  29.0 8.6 %all-to-all-done.modes_ref = bf16[16,72,256]{2,1,0:T(8,128)(2,1)S(1)} async-done(((bf16[16,72,256]{2,1,0:T(8,128)(2,1)}), bf16[16,72,256]{2,1,0:T(8,128)(2,1)S(1)}, u32[]{:S(2)}, u32[]{:S(2)}) %all-to-all-start) | async-done | bytes 589856 | tf_op jit(solution)/shard_map/all_to_all | solution.py:119
  37.6 0.0 copy-done.1
  37.6 0.0 copy-done.2
  37.6 0.0 copy-done
  37.6 4.4 %tangent.1 = f32[32,4,512]{2,1,0:T(4,128)} custom-call(s32[16]{0:T(128)S(1)} %copy-done, s32[2]{0:T(128)S(1)} %pad_add_fusion.ids, bf16[16,72,256]{2,1,0:T(8,128)(2,1)S(1)} %all-to-all-done.modes_ref, bf16[8,32,256]{2,1,0:T(8,128)(2,1)S(1)} %constant_dynamic-update-slice_fusion.near_ref, bf16[8,32,256]{2,1,0:T(8,128)(2,1)S(1)} %collective-permute-done.7.far_ref, ...), custom_call_target="tpu_custom_call" | custom-call | flops 2700000000 | bytes 2000000 | tf_op jit(solution)/shard_map/tangent/pallas_call | solution.py:132
  (10 shorter events, 0.0 us)
Async XLA Ops:
  0.8 8.1 %copy-start.3 = (bf16[4,16,256]{2,1,0:T(8,128)(2,1)S(1)}, bf16[4,16,256]{2,1,0:T(8,128)(2,1)}, u32[]{:S(2)}) copy-start(bf16[4,16,256]{2,1,0:T(8,128)(2,1)} %param.10) | copy-start | bytes 98308
  0.8 20.4 %collective-permute-start = (bf16[32,256]{1,0:T(8,128)(2,1)S(1)}, bf16[32,256]{1,0:T(8,128)(2,1)S(1)}, u32[]{:S(2)}, u32[]{:S(2)}) collective-permute-start(bf16[32,256]{1,0:T(8,128)(2,1)S(1)} %pad_maximum_fusion), channel_id=1, source_target_pairs={{0,2},{1,3},{2,0},{3,1},{4,6},{5,7},{6,4},{7,5},{8,10},{9,11},{10,... | collective-permute-start | bytes 49160 | tf_op jit(solution)/shard_map/ppermute | solution.py:123
  2.1 19.2 %collective-permute-start.1 = (bf16[32,256]{1,0:T(8,128)(2,1)S(1)}, bf16[32,256]{1,0:T(8,128)(2,1)S(1)}, u32[]{:S(2)}, u32[]{:S(2)}) collective-permute-start(bf16[32,256]{1,0:T(8,128)(2,1)S(1)} %pad_maximum_fusion), channel_id=1, source_target_pairs={{0,4},{1,5},{2,6},{3,7},{4,0},{5,1},{6,2},{7,3},{8,12},{9,13},{10,... | collective-permute-start | bytes 49160 | tf_op jit(solution)/shard_map/ppermute | solution.py:123
  3.3 20.2 %collective-permute-start.2 = (bf16[32,256]{1,0:T(8,128)(2,1)S(1)}, bf16[32,256]{1,0:T(8,128)(2,1)S(1)}, u32[]{:S(2)}, u32[]{:S(2)}) collective-permute-start(bf16[32,256]{1,0:T(8,128)(2,1)S(1)} %pad_maximum_fusion), channel_id=1, source_target_pairs={{0,6},{1,7},{2,4},{3,5},{4,2},{5,3},{6,0},{7,1},{8,14},{9,15},{10,... | collective-permute-start | bytes 49160 | tf_op jit(solution)/shard_map/ppermute | solution.py:123
  4.4 19.1 %collective-permute-start.3 = (bf16[32,256]{1,0:T(8,128)(2,1)S(1)}, bf16[32,256]{1,0:T(8,128)(2,1)S(1)}, u32[]{:S(2)}, u32[]{:S(2)}) collective-permute-start(bf16[32,256]{1,0:T(8,128)(2,1)S(1)} %pad_maximum_fusion), channel_id=1, source_target_pairs={{0,8},{1,9},{2,10},{3,11},{4,12},{5,13},{6,14},{7,15},{8,0},{9,1},... | collective-permute-start | bytes 49160 | tf_op jit(solution)/shard_map/ppermute | solution.py:123
  6.0 17.5 %collective-permute-start.4 = (bf16[32,256]{1,0:T(8,128)(2,1)S(1)}, bf16[32,256]{1,0:T(8,128)(2,1)S(1)}, u32[]{:S(2)}, u32[]{:S(2)}) collective-permute-start(bf16[32,256]{1,0:T(8,128)(2,1)S(1)} %pad_maximum_fusion), channel_id=1, source_target_pairs={{0,10},{1,11},{2,8},{3,9},{4,14},{5,15},{6,12},{7,13},{8,2},{9,3},... | collective-permute-start | bytes 49160 | tf_op jit(solution)/shard_map/ppermute | solution.py:123
  9.8 27.8 %copy-start.1 = (f32[512,256]{1,0:T(8,128)S(1)}, f32[512,256]{1,0:T(8,128)}, u32[]{:S(2)}) copy-start(f32[512,256]{1,0:T(8,128)} %constant.11.clone.table_ref) | copy-start | bytes 1572868
  9.8 27.8 %all-to-all-start = ((bf16[16,72,256]{2,1,0:T(8,128)(2,1)}), bf16[16,72,256]{2,1,0:T(8,128)(2,1)S(1)}, u32[]{:S(2)}, u32[]{:S(2)}) async-start(bf16[16,72,256]{2,1,0:T(8,128)(2,1)} %broadcast_in_dim.5), calls=%async_computation | async-start | bytes 1179648 | tf_op jit(solution)/shard_map/all_to_all | solution.py:119
  21.2 16.4 %copy-start.2 = (bf16[256,512]{1,0:T(8,128)(2,1)S(1)}, bf16[256,512]{1,0:T(8,128)(2,1)}, u32[]{:S(2)}) copy-start(bf16[256,512]{1,0:T(8,128)(2,1)} %constant.12.clone.second_ref) | copy-start | bytes 786436
  21.2 6.4 %collective-permute-start.5 = (bf16[32,256]{1,0:T(8,128)(2,1)S(1)}, bf16[32,256]{1,0:T(8,128)(2,1)S(1)}, u32[]{:S(2)}, u32[]{:S(2)}) collective-permute-start(bf16[32,256]{1,0:T(8,128)(2,1)S(1)} %pad_maximum_fusion), channel_id=1, source_target_pairs={{0,12},{1,13},{2,14},{3,15},{4,8},{5,9},{6,10},{7,11},{8,4},{9,5},... | collective-permute-start | bytes 49160 | tf_op jit(solution)/shard_map/ppermute | solution.py:123
  21.3 6.3 %collective-permute-start.6 = (bf16[32,256]{1,0:T(8,128)(2,1)S(1)}, bf16[32,256]{1,0:T(8,128)(2,1)S(1)}, u32[]{:S(2)}, u32[]{:S(2)}) collective-permute-start(bf16[32,256]{1,0:T(8,128)(2,1)S(1)} %pad_maximum_fusion), channel_id=1, source_target_pairs={{0,14},{1,15},{2,12},{3,13},{4,10},{5,11},{6,8},{7,9},{8,6},{9,7},... | collective-permute-start | bytes 49160 | tf_op jit(solution)/shard_map/ppermute | solution.py:123
  27.6 1.4 %collective-permute-start.7 = (bf16[8,32,256]{2,1,0:T(8,128)(2,1)S(1)}, bf16[8,32,256]{2,1,0:T(8,128)(2,1)S(1)}, u32[]{:S(2)}, u32[]{:S(2)}) collective-permute-start(bf16[8,32,256]{2,1,0:T(8,128)(2,1)S(1)} %constant_dynamic-update-slice_fusion.near_ref), channel_id=1, source_target_pairs={{0,1},{1,0},{2,3},{3,2},{4,5},{5,4},{6,7},{7,6},{8,9},{9,8},{10,11... | collective-permute-start | bytes 393224 | tf_op jit(solution)/shard_map/ppermute | solution.py:123
  27.7 9.9 %copy-start = (s32[16]{0:T(128)S(1)}, s32[16]{0:T(128)}, u32[]{:S(2)}) copy-start(s32[16]{0:T(128)} %block_map.1) | copy-start | bytes 196

commit v4 on v3

--- a/solution.py
+++ b/solution.py
@@ -28,17 +28,23 @@
     return np.where(odd, kernel, direct)
 
 
-def tangent_kernel(block_map, ids, modes_ref, near_ref, far_ref, table_ref, second_ref, out_ref, left, base, right, own):
+def tangent_kernel(block_map, ids, modes_ref, pair_ref, near_ref, fourth_ref, far_ref, table_ref, second_ref, out_ref, left, base, right, own):
     blocks = modes_ref.shape[0]
     length, pupil = table_ref.shape
     rows = length // blocks
     height = pupil // blocks
     count = out_ref.shape[1]
     half_group = blocks // 2
-    for place in range(blocks):
-        core, chip = divmod(place, half_group)
-        part = (near_ref, far_ref)[core][chip]
-        block = ids[1] ^ (2 * chip + core)
+    me = ids[1]
+    core = me & 1
+    found = []
+    for r in range(2):
+        found.append((pair_ref[r], me ^ r))
+        found.append((fourth_ref[r], me ^ (8 + r)))
+        for i in range(3):
+            found.append((near_ref[i, r], me ^ (2 * (i + 1 + 4 * core) + r)))
+            found.append((far_ref[i, r], me ^ (2 * (i + 5 - 4 * core) + 1 - r)))
+    for part, block in found:
         at = pl.multiple_of(((block & 1) * half_group + (block >> 1)) * height, height)
         base[pl.ds(at, height), :pupil] = part[:height]
         base[pl.ds(at, height), pupil:] = part[height:]
@@ -120,9 +126,12 @@
 
     mask = pupil_mask.astype(jnp.float32)
     field = jnp.concatenate([mask * jnp.cos(phase_offset), mask * jnp.sin(phase_offset)]).astype(jnp.bfloat16)
-    swap = lambda x, bit: lax.ppermute(x, "mode", [(i, i ^ bit) for i in range(group)])
-    near = jnp.stack([field] + [swap(field, 2 * t) for t in range(1, group // 2)])
-    far = swap(near, 1)
+    pairs = lambda t0, t1: [(i, i ^ (2 * (t1 if i & 1 else t0))) for i in range(group)]
+    cores = [(i, i ^ 1) for i in range(group)]
+    pair = jnp.stack([field, lax.ppermute(field, "mode", cores)])
+    near = jnp.stack([lax.ppermute(pair, "mode", pairs(t, t + 4)) for t in range(1, 4)])
+    fourth = lax.ppermute(pair, "mode", pairs(4, 4))
+    far = lax.ppermute(near, "mode", cores)
 
     table = sensor_table(length, pupil)
     places = np.concatenate([np.arange(height) + b * height for b in order])
@@ -131,7 +140,7 @@
     smem = pl.BlockSpec(memory_space=pltpu.SMEM)
     return pl.pallas_call(
         tangent_kernel,
-        in_specs=[smem, smem] + [vmem] * 5,
+        in_specs=[smem, smem] + [vmem] * 7,
         out_specs=vmem,
         out_shape=jax.ShapeDtypeStruct((rows, count, length), jnp.float32),
         scratch_shapes=[
@@ -147,7 +156,9 @@
         block_map,
         ids,
         gathered,
+        pair,
         near,
+        fourth,
         far,
         jnp.asarray(table[:, places], jnp.float32),
         jnp.asarray(table.T, jnp.bfloat16),

time: 42.4 us -> 36.7 us (0.87)
  starting transfers between devices: 21.1 us -> 16.9 us
  waiting for transfers between devices: 13.9 us -> 12.6 us
  local copies, waits for them, and re-layouts: 0.91 us -> 1.64 us
  other arithmetic: 0.88 us -> 0.17 us
    ppermute x8 -> x6, starting transfers between devices: 9.79 us -> 5.53 us  [the longest x3 4.09 us: local(): lax.ppermute(pair, 'mode', pairs(t, t + 4))]
    concatenate x1, local copies, waits for them, and re-layouts: 0.01 us -> 0.76 us  [local(): packed = jnp.concatenate([modes.reshape(count * height, pupil), mark])]
    another operation x1 -> x3, other arithmetic: 0.8 us -> 0.09 us
    all_to_all x1, waiting for transfers between devices: 8.56 us -> 7.89 us  [local(): gathered = lax.all_to_all(spread, 'mod', 0, 0, axis_index_groups=[order])]
    ppermute x8 -> x6, waiting for transfers between devices: 5.31 us -> 4.74 us  [the longest x3 2.41 us: local(): lax.ppermute(pair, 'mode', pairs(t, t + 4))]
  transfers between devices with their start and end apart: 9 -> 7, of which waited for: 3 -> 5; matrix products, arithmetic and copies ran while one was open for 2% -> 0% of each run, Pallas kernels for 0% -> 0%
where the time goes in v4:
time: 36.7 us; the launch traced here: 36.4 us
  starting transfers between devices  16.9 us (46%)
  waiting for transfers between devices  12.6 us (34%)
  Pallas kernels  4.4 us (12%)
  local copies, waits for them, and re-layouts  1.64 us (4%)
  between operations  0.73 us (2%)
    all_to_all x1, starting transfers between devices, local(): gathered = lax.all_to_all(spread, 'mod', 0, 0, axis_index_groups=[order])  11.3 us
    all_to_all x1, waiting for transfers between devices, local(): gathered = lax.all_to_all(spread, 'mod', 0, 0, axis_index_groups=[order])  7.89 us
    pallas_call x1, Pallas kernels, local(): pl.pallas_call(tangent_kernel, in_specs=[smem, smem] + [vmem] * 7, out_sp...  4.4 us
    ppermute x3, starting transfers between devices, local(): lax.ppermute(pair, 'mode', pairs(t, t + 4))  4.09 us
    ppermute x3, waiting for transfers between devices, local(): lax.ppermute(pair, 'mode', pairs(t, t + 4))  2.41 us
    ppermute x1, waiting for transfers between devices, local(): pair = jnp.stack([field, lax.ppermute(field, 'mode', cores)])  1.17 us
    ppermute x1, waiting for transfers between devices, local(): fourth = lax.ppermute(pair, 'mode', pairs(4, 4))  1.16 us
    broadcast_in_dim x1, local copies, waits for them, and re-layouts, local(): spread = jnp.broadcast_to(packed[None], (blocks,) + packed.shape)  0.85 us
  transfers between devices with their start and end apart: 7, of which 5 were waited for; matrix products, arithmetic and copies ran while one was open for 0% of the time, Pallas kernels for 0%

profile of v4, /device:TPU:4, one launch (start us, length us, event | category | flops | bytes accessed | tf_op | source)
XLA Modules:
  0.0 36.4 jit_solution(17282272592521240599)
XLA Ops:
  0.7 0.8 %concatenate.21 = bf16[72,256]{1,0:T(8,128)(2,1)S(1)} pad(bf16[64,256]{1,0:T(8,128)(2,1)} %bitcast.12, bf16[]{:T(256)} %bitcast.3), padding=0_8x0_0 | pad | bytes 69634 | tf_op jit(solution)/shard_map/concatenate | solution.py:123
  1.4 0.9 %broadcast_in_dim.5 = bf16[16,72,256]{2,1,0:T(8,128)(2,1)} broadcast(bf16[72,256]{1,0:T(8,128)(2,1)S(1)} %concatenate.21), dimensions={1,2} | broadcast | bytes 626688 | tf_op jit(solution)/shard_map/broadcast_in_dim | solution.py:124
  2.3 0.0 copy-start.3
  2.3 0.0 copy-start.4
  2.3 0.0 copy-start.1
  2.3 11.3 %all-to-all-start = ((bf16[16,72,256]{2,1,0:T(8,128)(2,1)}), bf16[16,72,256]{2,1,0:T(8,128)(2,1)S(1)}, u32[]{:S(2)}, u32[]{:S(2)}) async-start(bf16[16,72,256]{2,1,0:T(8,128)(2,1)} %broadcast_in_dim.5), calls=%async_computation | async-start | bytes 1179648 | tf_op jit(solution)/shard_map/all_to_all | solution.py:125
  13.6 0.0 copy-done.3
  13.6 0.0 copy-done.4
  13.6 0.0 copy-start.2
  13.7 0.1 multiply_convert_fusion.1
  13.7 0.1 collective-permute-start
  13.8 1.2 %collective-permute-done = bf16[32,256]{1,0:T(8,128)(2,1)S(1)} collective-permute-done((bf16[32,256]{1,0:T(8,128)(2,1)S(1)}, bf16[32,256]{1,0:T(8,128)(2,1)S(1)}, u32[]{:S(2)}, u32[]{:S(2)}) %collective-permute-start) | collective-permute-done | bytes 16416 | tf_op jit(solution)/shard_map/ppermute | solution.py:131
  15.0 0.5 %collective-permute-start.3 = (bf16[2,32,256]{2,1,0:T(8,128)(2,1)S(1)}, bf16[2,32,256]{2,1,0:T(8,128)(2,1)S(1)}, u32[]{:S(2)}, u32[]{:S(2)}) collective-permute-start(bf16[2,32,256]{2,1,0:T(8,128)(2,1)S(1)} %pad_maximum_fusion.1.pair_ref), channel_id=1, source_target_pairs={{0,6},{1,15},{2,4},{3,13},{4,2},{5,11},{6,0},{7,9},{8,14},{9,7},{1... | collective-permute-start | bytes 98312 | tf_op jit(solution)/shard_map/ppermute | solution.py:132
  15.6 2.7 %collective-permute-start.2 = (bf16[2,32,256]{2,1,0:T(8,128)(2,1)S(1)}, bf16[2,32,256]{2,1,0:T(8,128)(2,1)S(1)}, u32[]{:S(2)}, u32[]{:S(2)}) collective-permute-start(bf16[2,32,256]{2,1,0:T(8,128)(2,1)S(1)} %pad_maximum_fusion.1.pair_ref), channel_id=1, source_target_pairs={{0,4},{1,13},{2,6},{3,15},{4,0},{5,9},{6,2},{7,11},{8,12},{9,5},{1... | collective-permute-start | bytes 98312 | tf_op jit(solution)/shard_map/ppermute | solution.py:132
  18.3 0.8 %collective-permute-start.1 = (bf16[2,32,256]{2,1,0:T(8,128)(2,1)S(1)}, bf16[2,32,256]{2,1,0:T(8,128)(2,1)S(1)}, u32[]{:S(2)}, u32[]{:S(2)}) collective-permute-start(bf16[2,32,256]{2,1,0:T(8,128)(2,1)S(1)} %pad_maximum_fusion.1.pair_ref), channel_id=1, source_target_pairs={{0,2},{1,11},{2,0},{3,9},{4,6},{5,15},{6,4},{7,13},{8,10},{9,3},{1... | collective-permute-start | bytes 98312 | tf_op jit(solution)/shard_map/ppermute | solution.py:132
  19.1 0.7 %collective-permute-start.4 = (bf16[2,32,256]{2,1,0:T(8,128)(2,1)S(1)}, bf16[2,32,256]{2,1,0:T(8,128)(2,1)S(1)}, u32[]{:S(2)}, u32[]{:S(2)}) collective-permute-start(bf16[2,32,256]{2,1,0:T(8,128)(2,1)S(1)} %pad_maximum_fusion.1.pair_ref), channel_id=1, source_target_pairs={{0,8},{1,9},{2,10},{3,11},{4,12},{5,13},{6,14},{7,15},{8,0},{9,1},... | collective-permute-start | bytes 98312 | tf_op jit(solution)/shard_map/ppermute | solution.py:133
  19.8 0.0 collective-permute-done.3
  19.8 1.5 %collective-permute-done.2 = bf16[2,32,256]{2,1,0:T(8,128)(2,1)S(1)} collective-permute-done((bf16[2,32,256]{2,1,0:T(8,128)(2,1)S(1)}, bf16[2,32,256]{2,1,0:T(8,128)(2,1)S(1)}, u32[]{:S(2)}, u32[]{:S(2)}) %collective-permute-start.2) | collective-permute-done | bytes 32800 | tf_op jit(solution)/shard_map/ppermute | solution.py:132
  21.3 0.9 %collective-permute-done.1 = bf16[2,32,256]{2,1,0:T(8,128)(2,1)S(1)} collective-permute-done((bf16[2,32,256]{2,1,0:T(8,128)(2,1)S(1)}, bf16[2,32,256]{2,1,0:T(8,128)(2,1)S(1)}, u32[]{:S(2)}, u32[]{:S(2)}) %collective-permute-start.1) | collective-permute-done | bytes 32800 | tf_op jit(solution)/shard_map/ppermute | solution.py:132
  22.2 0.7 %collective-permute-start.5 = (bf16[3,2,32,256]{3,2,1,0:T(8,128)(2,1)S(1)}, bf16[3,2,32,256]{3,2,1,0:T(8,128)(2,1)S(1)}, u32[]{:S(2)}, u32[]{:S(2)}) collective-permute-start(bf16[3,2,32,256]{3,2,1,0:T(8,128)(2,1)S(1)} %pad_maximum_fusion.near_ref), channel_id=1, source_target_pairs={{0,1},{1,0},{2,3},{3,2},{4,5},{5,4},{6,7},{7,6},{8,9},{9,8},{10,11... | collective-permute-start | bytes 294920 | tf_op jit(solution)/shard_map/ppermute | solution.py:134
  22.9 0.0 copy-start
  22.9 0.1 pad_add_fusion.ids
  23.0 1.2 %collective-permute-done.4.fourth_ref = bf16[2,32,256]{2,1,0:T(8,128)(2,1)S(1)} collective-permute-done((bf16[2,32,256]{2,1,0:T(8,128)(2,1)S(1)}, bf16[2,32,256]{2,1,0:T(8,128)(2,1)S(1)}, u32[]{:S(2)}, u32[]{:S(2)}) %collective-permute-start.4) | collective-permute-done | bytes 32800 | tf_op jit(solution)/shard_map/ppermute | solution.py:133
  24.1 0.0 collective-permute-done.5.far_ref
  24.1 7.9 %all-to-all-done.modes_ref = bf16[16,72,256]{2,1,0:T(8,128)(2,1)S(1)} async-done(((bf16[16,72,256]{2,1,0:T(8,128)(2,1)}), bf16[16,72,256]{2,1,0:T(8,128)(2,1)S(1)}, u32[]{:S(2)}, u32[]{:S(2)}) %all-to-all-start) | async-done | bytes 589856 | tf_op jit(solution)/shard_map/all_to_all | solution.py:125
  32.0 0.0 copy-done.1
  32.0 0.0 copy-done.2
  32.0 0.0 copy-done
  32.0 4.4 %tangent.1 = f32[32,4,512]{2,1,0:T(4,128)} custom-call(s32[16]{0:T(128)S(1)} %copy-done, s32[2]{0:T(128)S(1)} %pad_add_fusion.ids, bf16[16,72,256]{2,1,0:T(8,128)(2,1)S(1)} %all-to-all-done.modes_ref, bf16[2,32,256]{2,1,0:T(8,128)(2,1)S(1)} %pad_maximum_fusion.1.pair_ref, bf16[3,2,32,256]{3,2,1,0:T(8,128)(2,1)S(1)} %pad_maximum_fusion.near_ref, ...), custom_call_target="tpu_custom_call" | custom-call | flops 2700000000 | bytes 2000000 | tf_op jit(solution)/shard_map/tangent/pallas_call | solution.py:141
  (3 shorter events, 0.0 us)
Async XLA Ops:
  2.3 11.3 %copy-start.3 = (f32[16,256]{1,0:T(8,128)S(1)}, f32[16,256]{1,0:T(8,128)}, u32[]{:S(2)}) copy-start(f32[16,256]{1,0:T(8,128)} %param.9) | copy-start | bytes 49156
  2.3 11.4 %copy-start.4 = (s32[16,256]{1,0:T(8,128)S(1)}, s32[16,256]{1,0:T(8,128)}, u32[]{:S(2)}) copy-start(s32[16,256]{1,0:T(8,128)} %param.8) | copy-start | bytes 49156
  2.3 29.7 %copy-start.1 = (f32[512,256]{1,0:T(8,128)S(1)}, f32[512,256]{1,0:T(8,128)}, u32[]{:S(2)}) copy-start(f32[512,256]{1,0:T(8,128)} %constant.11.clone.table_ref) | copy-start | bytes 1572868
  2.3 29.7 %all-to-all-start = ((bf16[16,72,256]{2,1,0:T(8,128)(2,1)}), bf16[16,72,256]{2,1,0:T(8,128)(2,1)S(1)}, u32[]{:S(2)}, u32[]{:S(2)}) async-start(bf16[16,72,256]{2,1,0:T(8,128)(2,1)} %broadcast_in_dim.5), calls=%async_computation | async-start | bytes 1179648 | tf_op jit(solution)/shard_map/all_to_all | solution.py:125
  13.6 18.4 %copy-start.2 = (bf16[256,512]{1,0:T(8,128)(2,1)S(1)}, bf16[256,512]{1,0:T(8,128)(2,1)}, u32[]{:S(2)}) copy-start(bf16[256,512]{1,0:T(8,128)(2,1)} %constant.12.clone.second_ref) | copy-start | bytes 786436
  13.7 1.3 %collective-permute-start = (bf16[32,256]{1,0:T(8,128)(2,1)S(1)}, bf16[32,256]{1,0:T(8,128)(2,1)S(1)}, u32[]{:S(2)}, u32[]{:S(2)}) collective-permute-start(bf16[32,256]{1,0:T(8,128)(2,1)S(1)} %pad_maximum_fusion.2), channel_id=1, source_target_pairs={{0,1},{1,0},{2,3},{3,2},{4,5},{5,4},{6,7},{7,6},{8,9},{9,8},{10,11... | collective-permute-start | bytes 49160 | tf_op jit(solution)/shard_map/ppermute | solution.py:131
  15.0 4.8 %collective-permute-start.3 = (bf16[2,32,256]{2,1,0:T(8,128)(2,1)S(1)}, bf16[2,32,256]{2,1,0:T(8,128)(2,1)S(1)}, u32[]{:S(2)}, u32[]{:S(2)}) collective-permute-start(bf16[2,32,256]{2,1,0:T(8,128)(2,1)S(1)} %pad_maximum_fusion.1.pair_ref), channel_id=1, source_target_pairs={{0,6},{1,15},{2,4},{3,13},{4,2},{5,11},{6,0},{7,9},{8,14},{9,7},{1... | collective-permute-start | bytes 98312 | tf_op jit(solution)/shard_map/ppermute | solution.py:132
  15.6 5.8 %collective-permute-start.2 = (bf16[2,32,256]{2,1,0:T(8,128)(2,1)S(1)}, bf16[2,32,256]{2,1,0:T(8,128)(2,1)S(1)}, u32[]{:S(2)}, u32[]{:S(2)}) collective-permute-start(bf16[2,32,256]{2,1,0:T(8,128)(2,1)S(1)} %pad_maximum_fusion.1.pair_ref), channel_id=1, source_target_pairs={{0,4},{1,13},{2,6},{3,15},{4,0},{5,9},{6,2},{7,11},{8,12},{9,5},{1... | collective-permute-start | bytes 98312 | tf_op jit(solution)/shard_map/ppermute | solution.py:132
  18.3 3.9 %collective-permute-start.1 = (bf16[2,32,256]{2,1,0:T(8,128)(2,1)S(1)}, bf16[2,32,256]{2,1,0:T(8,128)(2,1)S(1)}, u32[]{:S(2)}, u32[]{:S(2)}) collective-permute-start(bf16[2,32,256]{2,1,0:T(8,128)(2,1)S(1)} %pad_maximum_fusion.1.pair_ref), channel_id=1, source_target_pairs={{0,2},{1,11},{2,0},{3,9},{4,6},{5,15},{6,4},{7,13},{8,10},{9,3},{1... | collective-permute-start | bytes 98312 | tf_op jit(solution)/shard_map/ppermute | solution.py:132
  19.1 5.0 %collective-permute-start.4 = (bf16[2,32,256]{2,1,0:T(8,128)(2,1)S(1)}, bf16[2,32,256]{2,1,0:T(8,128)(2,1)S(1)}, u32[]{:S(2)}, u32[]{:S(2)}) collective-permute-start(bf16[2,32,256]{2,1,0:T(8,128)(2,1)S(1)} %pad_maximum_fusion.1.pair_ref), channel_id=1, source_target_pairs={{0,8},{1,9},{2,10},{3,11},{4,12},{5,13},{6,14},{7,15},{8,0},{9,1},... | collective-permute-start | bytes 98312 | tf_op jit(solution)/shard_map/ppermute | solution.py:133
  22.2 1.9 %collective-permute-start.5 = (bf16[3,2,32,256]{3,2,1,0:T(8,128)(2,1)S(1)}, bf16[3,2,32,256]{3,2,1,0:T(8,128)(2,1)S(1)}, u32[]{:S(2)}, u32[]{:S(2)}) collective-permute-start(bf16[3,2,32,256]{3,2,1,0:T(8,128)(2,1)S(1)} %pad_maximum_fusion.near_ref), channel_id=1, source_target_pairs={{0,1},{1,0},{2,3},{3,2},{4,5},{5,4},{6,7},{7,6},{8,9},{9,8},{10,11... | collective-permute-start | bytes 294920 | tf_op jit(solution)/shard_map/ppermute | solution.py:134
  22.9 9.1 %copy-start = (s32[16]{0:T(128)S(1)}, s32[16]{0:T(128)}, u32[]{:S(2)}) copy-start(s32[16]{0:T(128)} %block_map.1) | copy-start | bytes 196

commit v5 on v4

--- a/solution.py
+++ b/solution.py
@@ -13,7 +13,9 @@
 
 
 def peer_order(blocks):
-    return [2 * (i % (blocks // 2)) + i // (blocks // 2) for i in range(blocks)]
+    chips = blocks // 2
+    line = [i // 2 if i % 2 == 0 else chips - 1 - i // 2 for i in range(chips)]
+    return [2 * z + y for y in range(2) for z in line]
 
 
 def sensor_table(length, pupil):
@@ -45,7 +47,9 @@
             found.append((near_ref[i, r], me ^ (2 * (i + 1 + 4 * core) + r)))
             found.append((far_ref[i, r], me ^ (2 * (i + 5 - 4 * core) + 1 - r)))
     for part, block in found:
-        at = pl.multiple_of(((block & 1) * half_group + (block >> 1)) * height, height)
+        chip = block >> 1
+        chip = jnp.where(chip < half_group // 2, 2 * chip, 2 * half_group - 1 - 2 * chip)
+        at = pl.multiple_of(((block & 1) * half_group + chip) * height, height)
         base[pl.ds(at, height), :pupil] = part[:height]
         base[pl.ds(at, height), pupil:] = part[height:]
     point = jnp.concatenate([modes_ref[i][count * height :].astype(jnp.float32)[:1] for i in range(blocks)], axis=0)
@@ -54,7 +58,9 @@
     place = lax.broadcasted_iota(jnp.int32, (blocks, pupil), 1)
     odd = (place & 1) == 1
     block = place // height
-    row = (2 * (block % half_group) + block // half_group) * height + place % height
+    chip = block % half_group
+    chip = jnp.where(chip % 2 == 0, chip // 2, half_group - 1 - chip // 2)
+    row = (2 * chip + block // half_group) * height + place % height
 
     def factor(tilt, index):
         angle = tilt * ((index - pupil // 2).astype(jnp.float32) * scale)

time: 36.7 us -> 37.5 us (1.022)
  waiting for transfers between devices: 12.6 us -> 13.4 us
    all_to_all x1, waiting for transfers between devices: 7.89 us -> 8.96 us  [local(): gathered = lax.all_to_all(spread, 'mod', 0, 0, axis_index_groups=[order])]
    ppermute x1, waiting for transfers between devices: 1.16 us -> 0.3 us  [local(): fourth = lax.ppermute(pair, 'mode', pairs(4, 4))]
    ppermute x1, waiting for transfers between devices: 0.01 us -> 0.57 us  [local(): far = lax.ppermute(near, 'mode', cores)]
  transfers between devices with their start and end apart: 7 -> 7, of which waited for: 5 -> 6; matrix products, arithmetic and copies ran while one was open for 0% -> 0% of each run, Pallas kernels for 0% -> 0%
where the time goes in v5:
time: 37.5 us; the launch traced here: 37.2 us
  starting transfers between devices  16.9 us (45%)
  waiting for transfers between devices  13.4 us (36%)
  Pallas kernels  4.42 us (12%)
  local copies, waits for them, and re-layouts  1.64 us (4%)
  between operations  0.73 us (2%)
    all_to_all x1, starting transfers between devices, local(): gathered = lax.all_to_all(spread, 'mod', 0, 0, axis_index_groups=[order])  11.3 us
    all_to_all x1, waiting for transfers between devices, local(): gathered = lax.all_to_all(spread, 'mod', 0, 0, axis_index_groups=[order])  8.96 us
    pallas_call x1, Pallas kernels, local(): pl.pallas_call(tangent_kernel, in_specs=[smem, smem] + [vmem] * 7, out_sp...  4.42 us
    ppermute x3, starting transfers between devices, local(): lax.ppermute(pair, 'mode', pairs(t, t + 4))  4.09 us
    ppermute x3, waiting for transfers between devices, local(): lax.ppermute(pair, 'mode', pairs(t, t + 4))  2.41 us
    ppermute x1, waiting for transfers between devices, local(): pair = jnp.stack([field, lax.ppermute(field, 'mode', cores)])  1.17 us
    broadcast_in_dim x1, local copies, waits for them, and re-layouts, local(): spread = jnp.broadcast_to(packed[None], (blocks,) + packed.shape)  0.85 us
    concatenate x1, local copies, waits for them, and re-layouts, local(): packed = jnp.concatenate([modes.reshape(count * height, pupil), mark])  0.76 us
  transfers between devices with their start and end apart: 7, of which 6 were waited for; matrix products, arithmetic and copies ran while one was open for 0% of the time, Pallas kernels for 0%

profile of v5, /device:TPU:4, one launch (start us, length us, event | category | flops | bytes accessed | tf_op | source)
XLA Modules:
  0.0 37.2 jit_solution(13284084185691981816)
XLA Ops:
  0.7 0.8 %concatenate.21 = bf16[72,256]{1,0:T(8,128)(2,1)S(1)} pad(bf16[64,256]{1,0:T(8,128)(2,1)} %bitcast.12, bf16[]{:T(256)} %bitcast.3), padding=0_8x0_0 | pad | bytes 69634 | tf_op jit(solution)/shard_map/concatenate | solution.py:129
  1.4 0.9 %broadcast_in_dim.5 = bf16[16,72,256]{2,1,0:T(8,128)(2,1)} broadcast(bf16[72,256]{1,0:T(8,128)(2,1)S(1)} %concatenate.21), dimensions={1,2} | broadcast | bytes 626688 | tf_op jit(solution)/shard_map/broadcast_in_dim | solution.py:130
  2.3 0.0 copy-start.3
  2.3 0.0 copy-start.4
  2.3 0.0 copy-start.1
  2.3 11.3 %all-to-all-start = ((bf16[16,72,256]{2,1,0:T(8,128)(2,1)}), bf16[16,72,256]{2,1,0:T(8,128)(2,1)S(1)}, u32[]{:S(2)}, u32[]{:S(2)}) async-start(bf16[16,72,256]{2,1,0:T(8,128)(2,1)} %broadcast_in_dim.5), calls=%async_computation | async-start | bytes 1179648 | tf_op jit(solution)/shard_map/all_to_all | solution.py:131
  13.6 0.0 copy-done.3
  13.6 0.0 copy-done.4
  13.6 0.0 copy-start.2
  13.7 0.1 multiply_convert_fusion.1
  13.7 0.1 collective-permute-start
  13.8 1.2 %collective-permute-done = bf16[32,256]{1,0:T(8,128)(2,1)S(1)} collective-permute-done((bf16[32,256]{1,0:T(8,128)(2,1)S(1)}, bf16[32,256]{1,0:T(8,128)(2,1)S(1)}, u32[]{:S(2)}, u32[]{:S(2)}) %collective-permute-start) | collective-permute-done | bytes 16416 | tf_op jit(solution)/shard_map/ppermute | solution.py:137
  15.0 0.5 %collective-permute-start.3 = (bf16[2,32,256]{2,1,0:T(8,128)(2,1)S(1)}, bf16[2,32,256]{2,1,0:T(8,128)(2,1)S(1)}, u32[]{:S(2)}, u32[]{:S(2)}) collective-permute-start(bf16[2,32,256]{2,1,0:T(8,128)(2,1)S(1)} %pad_maximum_fusion.1.pair_ref), channel_id=1, source_target_pairs={{0,6},{1,15},{2,4},{3,13},{4,2},{5,11},{6,0},{7,9},{8,14},{9,7},{1... | collective-permute-start | bytes 98312 | tf_op jit(solution)/shard_map/ppermute | solution.py:138
  15.6 2.7 %collective-permute-start.2 = (bf16[2,32,256]{2,1,0:T(8,128)(2,1)S(1)}, bf16[2,32,256]{2,1,0:T(8,128)(2,1)S(1)}, u32[]{:S(2)}, u32[]{:S(2)}) collective-permute-start(bf16[2,32,256]{2,1,0:T(8,128)(2,1)S(1)} %pad_maximum_fusion.1.pair_ref), channel_id=1, source_target_pairs={{0,4},{1,13},{2,6},{3,15},{4,0},{5,9},{6,2},{7,11},{8,12},{9,5},{1... | collective-permute-start | bytes 98312 | tf_op jit(solution)/shard_map/ppermute | solution.py:138
  18.3 0.8 %collective-permute-start.1 = (bf16[2,32,256]{2,1,0:T(8,128)(2,1)S(1)}, bf16[2,32,256]{2,1,0:T(8,128)(2,1)S(1)}, u32[]{:S(2)}, u32[]{:S(2)}) collective-permute-start(bf16[2,32,256]{2,1,0:T(8,128)(2,1)S(1)} %pad_maximum_fusion.1.pair_ref), channel_id=1, source_target_pairs={{0,2},{1,11},{2,0},{3,9},{4,6},{5,15},{6,4},{7,13},{8,10},{9,3},{1... | collective-permute-start | bytes 98312 | tf_op jit(solution)/shard_map/ppermute | solution.py:138
  19.1 0.7 %collective-permute-start.4 = (bf16[2,32,256]{2,1,0:T(8,128)(2,1)S(1)}, bf16[2,32,256]{2,1,0:T(8,128)(2,1)S(1)}, u32[]{:S(2)}, u32[]{:S(2)}) collective-permute-start(bf16[2,32,256]{2,1,0:T(8,128)(2,1)S(1)} %pad_maximum_fusion.1.pair_ref), channel_id=1, source_target_pairs={{0,8},{1,9},{2,10},{3,11},{4,12},{5,13},{6,14},{7,15},{8,0},{9,1},... | collective-permute-start | bytes 98312 | tf_op jit(solution)/shard_map/ppermute | solution.py:139
  19.8 0.0 collective-permute-done.3
  19.8 1.5 %collective-permute-done.2 = bf16[2,32,256]{2,1,0:T(8,128)(2,1)S(1)} collective-permute-done((bf16[2,32,256]{2,1,0:T(8,128)(2,1)S(1)}, bf16[2,32,256]{2,1,0:T(8,128)(2,1)S(1)}, u32[]{:S(2)}, u32[]{:S(2)}) %collective-permute-start.2) | collective-permute-done | bytes 32800 | tf_op jit(solution)/shard_map/ppermute | solution.py:138
  21.3 0.9 %collective-permute-done.1 = bf16[2,32,256]{2,1,0:T(8,128)(2,1)S(1)} collective-permute-done((bf16[2,32,256]{2,1,0:T(8,128)(2,1)S(1)}, bf16[2,32,256]{2,1,0:T(8,128)(2,1)S(1)}, u32[]{:S(2)}, u32[]{:S(2)}) %collective-permute-start.1) | collective-permute-done | bytes 32800 | tf_op jit(solution)/shard_map/ppermute | solution.py:138
  22.2 0.7 %collective-permute-start.5 = (bf16[3,2,32,256]{3,2,1,0:T(8,128)(2,1)S(1)}, bf16[3,2,32,256]{3,2,1,0:T(8,128)(2,1)S(1)}, u32[]{:S(2)}, u32[]{:S(2)}) collective-permute-start(bf16[3,2,32,256]{3,2,1,0:T(8,128)(2,1)S(1)} %pad_maximum_fusion.near_ref), channel_id=1, source_target_pairs={{0,1},{1,0},{2,3},{3,2},{4,5},{5,4},{6,7},{7,6},{8,9},{9,8},{10,11... | collective-permute-start | bytes 294920 | tf_op jit(solution)/shard_map/ppermute | solution.py:140
  22.9 0.0 copy-start
  22.9 0.1 pad_add_fusion.ids
  23.0 0.3 collective-permute-done.4.fourth_ref
  23.3 0.6 %collective-permute-done.5.far_ref = bf16[3,2,32,256]{3,2,1,0:T(8,128)(2,1)S(1)} collective-permute-done((bf16[3,2,32,256]{3,2,1,0:T(8,128)(2,1)S(1)}, bf16[3,2,32,256]{3,2,1,0:T(8,128)(2,1)S(1)}, u32[]{:S(2)}, u32[]{:S(2)}) %collective-permute-start.5) | collective-permute-done | bytes 98336 | tf_op jit(solution)/shard_map/ppermute | solution.py:140
  23.8 9.0 %all-to-all-done.modes_ref = bf16[16,72,256]{2,1,0:T(8,128)(2,1)S(1)} async-done(((bf16[16,72,256]{2,1,0:T(8,128)(2,1)}), bf16[16,72,256]{2,1,0:T(8,128)(2,1)S(1)}, u32[]{:S(2)}, u32[]{:S(2)}) %all-to-all-start) | async-done | bytes 589856 | tf_op jit(solution)/shard_map/all_to_all | solution.py:131
  32.8 0.0 copy-done.1
  32.8 0.0 copy-done.2
  32.8 0.0 copy-done
  32.8 4.4 %tangent.1 = f32[32,4,512]{2,1,0:T(4,128)} custom-call(s32[16]{0:T(128)S(1)} %copy-done, s32[2]{0:T(128)S(1)} %pad_add_fusion.ids, bf16[16,72,256]{2,1,0:T(8,128)(2,1)S(1)} %all-to-all-done.modes_ref, bf16[2,32,256]{2,1,0:T(8,128)(2,1)S(1)} %pad_maximum_fusion.1.pair_ref, bf16[3,2,32,256]{3,2,1,0:T(8,128)(2,1)S(1)} %pad_maximum_fusion.near_ref, ...), custom_call_target="tpu_custom_call" | custom-call | flops 2700000000 | bytes 2000000 | tf_op jit(solution)/shard_map/tangent/pallas_call | solution.py:147
  (3 shorter events, 0.0 us)
Async XLA Ops:
  2.3 11.3 %copy-start.3 = (f32[16,256]{1,0:T(8,128)S(1)}, f32[16,256]{1,0:T(8,128)}, u32[]{:S(2)}) copy-start(f32[16,256]{1,0:T(8,128)} %param.9) | copy-start | bytes 49156
  2.3 11.4 %copy-start.4 = (s32[16,256]{1,0:T(8,128)S(1)}, s32[16,256]{1,0:T(8,128)}, u32[]{:S(2)}) copy-start(s32[16,256]{1,0:T(8,128)} %param.8) | copy-start | bytes 49156
  2.3 30.5 %copy-start.1 = (f32[512,256]{1,0:T(8,128)S(1)}, f32[512,256]{1,0:T(8,128)}, u32[]{:S(2)}) copy-start(f32[512,256]{1,0:T(8,128)} %constant.11.clone.table_ref) | copy-start | bytes 1572868
  2.3 30.5 %all-to-all-start = ((bf16[16,72,256]{2,1,0:T(8,128)(2,1)}), bf16[16,72,256]{2,1,0:T(8,128)(2,1)S(1)}, u32[]{:S(2)}, u32[]{:S(2)}) async-start(bf16[16,72,256]{2,1,0:T(8,128)(2,1)} %broadcast_in_dim.5), calls=%async_computation | async-start | bytes 1179648 | tf_op jit(solution)/shard_map/all_to_all | solution.py:131
  13.6 19.2 %copy-start.2 = (bf16[256,512]{1,0:T(8,128)(2,1)S(1)}, bf16[256,512]{1,0:T(8,128)(2,1)}, u32[]{:S(2)}) copy-start(bf16[256,512]{1,0:T(8,128)(2,1)} %constant.12.clone.second_ref) | copy-start | bytes 786436
  13.7 1.3 %collective-permute-start = (bf16[32,256]{1,0:T(8,128)(2,1)S(1)}, bf16[32,256]{1,0:T(8,128)(2,1)S(1)}, u32[]{:S(2)}, u32[]{:S(2)}) collective-permute-start(bf16[32,256]{1,0:T(8,128)(2,1)S(1)} %pad_maximum_fusion.2), channel_id=1, source_target_pairs={{0,1},{1,0},{2,3},{3,2},{4,5},{5,4},{6,7},{7,6},{8,9},{9,8},{10,11... | collective-permute-start | bytes 49160 | tf_op jit(solution)/shard_map/ppermute | solution.py:137
  15.0 4.8 %collective-permute-start.3 = (bf16[2,32,256]{2,1,0:T(8,128)(2,1)S(1)}, bf16[2,32,256]{2,1,0:T(8,128)(2,1)S(1)}, u32[]{:S(2)}, u32[]{:S(2)}) collective-permute-start(bf16[2,32,256]{2,1,0:T(8,128)(2,1)S(1)} %pad_maximum_fusion.1.pair_ref), channel_id=1, source_target_pairs={{0,6},{1,15},{2,4},{3,13},{4,2},{5,11},{6,0},{7,9},{8,14},{9,7},{1... | collective-permute-start | bytes 98312 | tf_op jit(solution)/shard_map/ppermute | solution.py:138
  15.6 5.8 %collective-permute-start.2 = (bf16[2,32,256]{2,1,0:T(8,128)(2,1)S(1)}, bf16[2,32,256]{2,1,0:T(8,128)(2,1)S(1)}, u32[]{:S(2)}, u32[]{:S(2)}) collective-permute-start(bf16[2,32,256]{2,1,0:T(8,128)(2,1)S(1)} %pad_maximum_fusion.1.pair_ref), channel_id=1, source_target_pairs={{0,4},{1,13},{2,6},{3,15},{4,0},{5,9},{6,2},{7,11},{8,12},{9,5},{1... | collective-permute-start | bytes 98312 | tf_op jit(solution)/shard_map/ppermute | solution.py:138
  18.3 3.9 %collective-permute-start.1 = (bf16[2,32,256]{2,1,0:T(8,128)(2,1)S(1)}, bf16[2,32,256]{2,1,0:T(8,128)(2,1)S(1)}, u32[]{:S(2)}, u32[]{:S(2)}) collective-permute-start(bf16[2,32,256]{2,1,0:T(8,128)(2,1)S(1)} %pad_maximum_fusion.1.pair_ref), channel_id=1, source_target_pairs={{0,2},{1,11},{2,0},{3,9},{4,6},{5,15},{6,4},{7,13},{8,10},{9,3},{1... | collective-permute-start | bytes 98312 | tf_op jit(solution)/shard_map/ppermute | solution.py:138
  19.1 4.1 %collective-permute-start.4 = (bf16[2,32,256]{2,1,0:T(8,128)(2,1)S(1)}, bf16[2,32,256]{2,1,0:T(8,128)(2,1)S(1)}, u32[]{:S(2)}, u32[]{:S(2)}) collective-permute-start(bf16[2,32,256]{2,1,0:T(8,128)(2,1)S(1)} %pad_maximum_fusion.1.pair_ref), channel_id=1, source_target_pairs={{0,8},{1,9},{2,10},{3,11},{4,12},{5,13},{6,14},{7,15},{8,0},{9,1},... | collective-permute-start | bytes 98312 | tf_op jit(solution)/shard_map/ppermute | solution.py:139
  22.2 1.6 %collective-permute-start.5 = (bf16[3,2,32,256]{3,2,1,0:T(8,128)(2,1)S(1)}, bf16[3,2,32,256]{3,2,1,0:T(8,128)(2,1)S(1)}, u32[]{:S(2)}, u32[]{:S(2)}) collective-permute-start(bf16[3,2,32,256]{3,2,1,0:T(8,128)(2,1)S(1)} %pad_maximum_fusion.near_ref), channel_id=1, source_target_pairs={{0,1},{1,0},{2,3},{3,2},{4,5},{5,4},{6,7},{7,6},{8,9},{9,8},{10,11... | collective-permute-start | bytes 294920 | tf_op jit(solution)/shard_map/ppermute | solution.py:140
  22.9 9.9 %copy-start = (s32[16]{0:T(128)S(1)}, s32[16]{0:T(128)}, u32[]{:S(2)}) copy-start(s32[16]{0:T(128)} %block_map.1) | copy-start | bytes 196

commit v6 on v4

--- a/solution.py
+++ b/solution.py
@@ -42,8 +42,8 @@
         found.append((pair_ref[r], me ^ r))
         found.append((fourth_ref[r], me ^ (8 + r)))
         for i in range(3):
-            found.append((near_ref[i, r], me ^ (2 * (i + 1 + 4 * core) + r)))
-            found.append((far_ref[i, r], me ^ (2 * (i + 5 - 4 * core) + 1 - r)))
+            found.append((near_ref[i, r], me ^ (2 * (i + 5 - 4 * core) + r)))
+            found.append((far_ref[i, r], me ^ (2 * (i + 1 + 4 * core) + 1 - r)))
     for part, block in found:
         at = pl.multiple_of(((block & 1) * half_group + (block >> 1)) * height, height)
         base[pl.ds(at, height), :pupil] = part[:height]
@@ -129,7 +129,7 @@
     pairs = lambda t0, t1: [(i, i ^ (2 * (t1 if i & 1 else t0))) for i in range(group)]
     cores = [(i, i ^ 1) for i in range(group)]
     pair = jnp.stack([field, lax.ppermute(field, "mode", cores)])
-    near = jnp.stack([lax.ppermute(pair, "mode", pairs(t, t + 4)) for t in range(1, 4)])
+    near = jnp.stack([lax.ppermute(pair, "mode", pairs(t + 4, t)) for t in range(1, 4)])
     fourth = lax.ppermute(pair, "mode", pairs(4, 4))
     far = lax.ppermute(near, "mode", cores)
 

time: 36.7 us -> 36.7 us (level)
  starting transfers between devices: 16.9 us -> 18 us
  waiting for transfers between devices: 12.6 us -> 11.5 us
    all_to_all x1, waiting for transfers between devices: 7.89 us -> 6.5 us  [local(): gathered = lax.all_to_all(spread, 'mod', 0, 0, axis_index_groups=[order])]
    ppermute x3, starting transfers between devices: 4.09 us -> 5.11 us  [local(): lax.ppermute(pair, 'mode', pairs(t + 4, t))]
    ppermute x1, waiting for transfers between devices: 0.01 us -> 0.96 us  [local(): far = lax.ppermute(near, 'mode', cores)]
    ppermute x1, waiting for transfers between devices: 1.16 us -> 0.24 us  [local(): fourth = lax.ppermute(pair, 'mode', pairs(4, 4))]
    ppermute x1, starting transfers between devices: 0.68 us -> 1.35 us  [local(): fourth = lax.ppermute(pair, 'mode', pairs(4, 4))]
    ppermute x1, starting transfers between devices: 0.67 us -> 0.09 us  [local(): far = lax.ppermute(near, 'mode', cores)]
  transfers between devices with their start and end apart: 7 -> 7, of which waited for: 5 -> 6; matrix products, arithmetic and copies ran while one was open for 0% -> 0% of each run, Pallas kernels for 0% -> 0%
where the time goes in v6:
time: 36.7 us; the launch traced here: 36.4 us
  starting transfers between devices  18 us (49%)
  waiting for transfers between devices  11.5 us (31%)
  Pallas kernels  4.4 us (12%)
  local copies, waits for them, and re-layouts  1.64 us (4%)
  between operations  0.74 us (2%)
    all_to_all x1, starting transfers between devices, local(): gathered = lax.all_to_all(spread, 'mod', 0, 0, axis_index_groups=[order])  11.3 us
    all_to_all x1, waiting for transfers between devices, local(): gathered = lax.all_to_all(spread, 'mod', 0, 0, axis_index_groups=[order])  6.5 us
    ppermute x3, starting transfers between devices, local(): lax.ppermute(pair, 'mode', pairs(t + 4, t))  5.11 us
    pallas_call x1, Pallas kernels, local(): pl.pallas_call(tangent_kernel, in_specs=[smem, smem] + [vmem] * 7, out_sp...  4.4 us
    ppermute x3, waiting for transfers between devices, local(): lax.ppermute(pair, 'mode', pairs(t + 4, t))  2.64 us
    ppermute x1, starting transfers between devices, local(): fourth = lax.ppermute(pair, 'mode', pairs(4, 4))  1.35 us
    ppermute x1, waiting for transfers between devices, local(): pair = jnp.stack([field, lax.ppermute(field, 'mode', cores)])  1.17 us
    ppermute x1, waiting for transfers between devices, local(): far = lax.ppermute(near, 'mode', cores)  0.96 us
  transfers between devices with their start and end apart: 7, of which 6 were waited for; matrix products, arithmetic and copies ran while one was open for 0% of the time, Pallas kernels for 0%

profile of v6, /device:TPU:4, one launch (start us, length us, event | category | flops | bytes accessed | tf_op | source)
XLA Modules:
  0.0 36.4 jit_solution(3567613069782966405)
XLA Ops:
  0.7 0.8 %concatenate.21 = bf16[72,256]{1,0:T(8,128)(2,1)S(1)} pad(bf16[64,256]{1,0:T(8,128)(2,1)} %bitcast.12, bf16[]{:T(256)} %bitcast.3), padding=0_8x0_0 | pad | bytes 69634 | tf_op jit(solution)/shard_map/concatenate | solution.py:123
  1.4 0.9 %broadcast_in_dim.5 = bf16[16,72,256]{2,1,0:T(8,128)(2,1)} broadcast(bf16[72,256]{1,0:T(8,128)(2,1)S(1)} %concatenate.21), dimensions={1,2} | broadcast | bytes 626688 | tf_op jit(solution)/shard_map/broadcast_in_dim | solution.py:124
  2.3 0.0 copy-start.3
  2.3 0.0 copy-start.4
  2.3 0.0 copy-start.1
  2.3 11.3 %all-to-all-start = ((bf16[16,72,256]{2,1,0:T(8,128)(2,1)}), bf16[16,72,256]{2,1,0:T(8,128)(2,1)S(1)}, u32[]{:S(2)}, u32[]{:S(2)}) async-start(bf16[16,72,256]{2,1,0:T(8,128)(2,1)} %broadcast_in_dim.5), calls=%async_computation | async-start | bytes 1179648 | tf_op jit(solution)/shard_map/all_to_all | solution.py:125
  13.6 0.0 copy-done.3
  13.6 0.0 copy-done.4
  13.6 0.0 copy-start.2
  13.7 0.1 multiply_convert_fusion.1
  13.7 0.1 collective-permute-start
  13.8 1.2 %collective-permute-done = bf16[32,256]{1,0:T(8,128)(2,1)S(1)} collective-permute-done((bf16[32,256]{1,0:T(8,128)(2,1)S(1)}, bf16[32,256]{1,0:T(8,128)(2,1)S(1)}, u32[]{:S(2)}, u32[]{:S(2)}) %collective-permute-start) | collective-permute-done | bytes 16416 | tf_op jit(solution)/shard_map/ppermute | solution.py:131
  15.0 0.6 %collective-permute-start.3 = (bf16[2,32,256]{2,1,0:T(8,128)(2,1)S(1)}, bf16[2,32,256]{2,1,0:T(8,128)(2,1)S(1)}, u32[]{:S(2)}, u32[]{:S(2)}) collective-permute-start(bf16[2,32,256]{2,1,0:T(8,128)(2,1)S(1)} %pad_maximum_fusion.1.pair_ref), channel_id=1, source_target_pairs={{0,14},{1,7},{2,12},{3,5},{4,10},{5,3},{6,8},{7,1},{8,6},{9,15},{1... | collective-permute-start | bytes 98312 | tf_op jit(solution)/shard_map/ppermute | solution.py:132
  15.7 3.5 %collective-permute-start.2 = (bf16[2,32,256]{2,1,0:T(8,128)(2,1)S(1)}, bf16[2,32,256]{2,1,0:T(8,128)(2,1)S(1)}, u32[]{:S(2)}, u32[]{:S(2)}) collective-permute-start(bf16[2,32,256]{2,1,0:T(8,128)(2,1)S(1)} %pad_maximum_fusion.1.pair_ref), channel_id=1, source_target_pairs={{0,12},{1,5},{2,14},{3,7},{4,8},{5,1},{6,10},{7,3},{8,4},{9,13},{1... | collective-permute-start | bytes 98312 | tf_op jit(solution)/shard_map/ppermute | solution.py:132
  19.2 0.9 %collective-permute-start.1 = (bf16[2,32,256]{2,1,0:T(8,128)(2,1)S(1)}, bf16[2,32,256]{2,1,0:T(8,128)(2,1)S(1)}, u32[]{:S(2)}, u32[]{:S(2)}) collective-permute-start(bf16[2,32,256]{2,1,0:T(8,128)(2,1)S(1)} %pad_maximum_fusion.1.pair_ref), channel_id=1, source_target_pairs={{0,10},{1,3},{2,8},{3,1},{4,14},{5,7},{6,12},{7,5},{8,2},{9,11},{1... | collective-permute-start | bytes 98312 | tf_op jit(solution)/shard_map/ppermute | solution.py:132
  20.1 1.3 %collective-permute-start.4 = (bf16[2,32,256]{2,1,0:T(8,128)(2,1)S(1)}, bf16[2,32,256]{2,1,0:T(8,128)(2,1)S(1)}, u32[]{:S(2)}, u32[]{:S(2)}) collective-permute-start(bf16[2,32,256]{2,1,0:T(8,128)(2,1)S(1)} %pad_maximum_fusion.1.pair_ref), channel_id=1, source_target_pairs={{0,8},{1,9},{2,10},{3,11},{4,12},{5,13},{6,14},{7,15},{8,0},{9,1},... | collective-permute-start | bytes 98312 | tf_op jit(solution)/shard_map/ppermute | solution.py:133
  21.5 0.0 collective-permute-done.3
  21.5 0.7 %collective-permute-done.2 = bf16[2,32,256]{2,1,0:T(8,128)(2,1)S(1)} collective-permute-done((bf16[2,32,256]{2,1,0:T(8,128)(2,1)S(1)}, bf16[2,32,256]{2,1,0:T(8,128)(2,1)S(1)}, u32[]{:S(2)}, u32[]{:S(2)}) %collective-permute-start.2) | collective-permute-done | bytes 32800 | tf_op jit(solution)/shard_map/ppermute | solution.py:132
  22.1 2.0 %collective-permute-done.1 = bf16[2,32,256]{2,1,0:T(8,128)(2,1)S(1)} collective-permute-done((bf16[2,32,256]{2,1,0:T(8,128)(2,1)S(1)}, bf16[2,32,256]{2,1,0:T(8,128)(2,1)S(1)}, u32[]{:S(2)}, u32[]{:S(2)}) %collective-permute-start.1) | collective-permute-done | bytes 32800 | tf_op jit(solution)/shard_map/ppermute | solution.py:132
  24.1 0.1 collective-permute-start.5
  24.2 0.0 copy-start
  24.2 0.1 pad_add_fusion.ids
  24.3 0.2 collective-permute-done.4.fourth_ref
  24.6 1.0 %collective-permute-done.5.far_ref = bf16[3,2,32,256]{3,2,1,0:T(8,128)(2,1)S(1)} collective-permute-done((bf16[3,2,32,256]{3,2,1,0:T(8,128)(2,1)S(1)}, bf16[3,2,32,256]{3,2,1,0:T(8,128)(2,1)S(1)}, u32[]{:S(2)}, u32[]{:S(2)}) %collective-permute-start.5) | collective-permute-done | bytes 98336 | tf_op jit(solution)/shard_map/ppermute | solution.py:134
  25.5 6.5 %all-to-all-done.modes_ref = bf16[16,72,256]{2,1,0:T(8,128)(2,1)S(1)} async-done(((bf16[16,72,256]{2,1,0:T(8,128)(2,1)}), bf16[16,72,256]{2,1,0:T(8,128)(2,1)S(1)}, u32[]{:S(2)}, u32[]{:S(2)}) %all-to-all-start) | async-done | bytes 589856 | tf_op jit(solution)/shard_map/all_to_all | solution.py:125
  32.0 0.0 copy-done.1
  32.0 0.0 copy-done.2
  32.0 0.0 copy-done
  32.0 4.4 %tangent.1 = f32[32,4,512]{2,1,0:T(4,128)} custom-call(s32[16]{0:T(128)S(1)} %copy-done, s32[2]{0:T(128)S(1)} %pad_add_fusion.ids, bf16[16,72,256]{2,1,0:T(8,128)(2,1)S(1)} %all-to-all-done.modes_ref, bf16[2,32,256]{2,1,0:T(8,128)(2,1)S(1)} %pad_maximum_fusion.1.pair_ref, bf16[3,2,32,256]{3,2,1,0:T(8,128)(2,1)S(1)} %pad_maximum_fusion.near_ref, ...), custom_call_target="tpu_custom_call" | custom-call | flops 2700000000 | bytes 2000000 | tf_op jit(solution)/shard_map/tangent/pallas_call | solution.py:141
  (3 shorter events, 0.0 us)
Async XLA Ops:
  2.3 11.3 %copy-start.3 = (f32[16,256]{1,0:T(8,128)S(1)}, f32[16,256]{1,0:T(8,128)}, u32[]{:S(2)}) copy-start(f32[16,256]{1,0:T(8,128)} %param.9) | copy-start | bytes 49156
  2.3 11.4 %copy-start.4 = (s32[16,256]{1,0:T(8,128)S(1)}, s32[16,256]{1,0:T(8,128)}, u32[]{:S(2)}) copy-start(s32[16,256]{1,0:T(8,128)} %param.8) | copy-start | bytes 49156
  2.3 29.7 %copy-start.1 = (f32[512,256]{1,0:T(8,128)S(1)}, f32[512,256]{1,0:T(8,128)}, u32[]{:S(2)}) copy-start(f32[512,256]{1,0:T(8,128)} %constant.11.clone.table_ref) | copy-start | bytes 1572868
  2.3 29.7 %all-to-all-start = ((bf16[16,72,256]{2,1,0:T(8,128)(2,1)}), bf16[16,72,256]{2,1,0:T(8,128)(2,1)S(1)}, u32[]{:S(2)}, u32[]{:S(2)}) async-start(bf16[16,72,256]{2,1,0:T(8,128)(2,1)} %broadcast_in_dim.5), calls=%async_computation | async-start | bytes 1179648 | tf_op jit(solution)/shard_map/all_to_all | solution.py:125
  13.6 18.4 %copy-start.2 = (bf16[256,512]{1,0:T(8,128)(2,1)S(1)}, bf16[256,512]{1,0:T(8,128)(2,1)}, u32[]{:S(2)}) copy-start(bf16[256,512]{1,0:T(8,128)(2,1)} %constant.12.clone.second_ref) | copy-start | bytes 786436
  13.7 1.3 %collective-permute-start = (bf16[32,256]{1,0:T(8,128)(2,1)S(1)}, bf16[32,256]{1,0:T(8,128)(2,1)S(1)}, u32[]{:S(2)}, u32[]{:S(2)}) collective-permute-start(bf16[32,256]{1,0:T(8,128)(2,1)S(1)} %pad_maximum_fusion.2), channel_id=1, source_target_pairs={{0,1},{1,0},{2,3},{3,2},{4,5},{5,4},{6,7},{7,6},{8,9},{9,8},{10,11... | collective-permute-start | bytes 49160 | tf_op jit(solution)/shard_map/ppermute | solution.py:131
  15.0 6.5 %collective-permute-start.3 = (bf16[2,32,256]{2,1,0:T(8,128)(2,1)S(1)}, bf16[2,32,256]{2,1,0:T(8,128)(2,1)S(1)}, u32[]{:S(2)}, u32[]{:S(2)}) collective-permute-start(bf16[2,32,256]{2,1,0:T(8,128)(2,1)S(1)} %pad_maximum_fusion.1.pair_ref), channel_id=1, source_target_pairs={{0,14},{1,7},{2,12},{3,5},{4,10},{5,3},{6,8},{7,1},{8,6},{9,15},{1... | collective-permute-start | bytes 98312 | tf_op jit(solution)/shard_map/ppermute | solution.py:132
  15.7 6.5 %collective-permute-start.2 = (bf16[2,32,256]{2,1,0:T(8,128)(2,1)S(1)}, bf16[2,32,256]{2,1,0:T(8,128)(2,1)S(1)}, u32[]{:S(2)}, u32[]{:S(2)}) collective-permute-start(bf16[2,32,256]{2,1,0:T(8,128)(2,1)S(1)} %pad_maximum_fusion.1.pair_ref), channel_id=1, source_target_pairs={{0,12},{1,5},{2,14},{3,7},{4,8},{5,1},{6,10},{7,3},{8,4},{9,13},{1... | collective-permute-start | bytes 98312 | tf_op jit(solution)/shard_map/ppermute | solution.py:132
  19.2 4.9 %collective-permute-start.1 = (bf16[2,32,256]{2,1,0:T(8,128)(2,1)S(1)}, bf16[2,32,256]{2,1,0:T(8,128)(2,1)S(1)}, u32[]{:S(2)}, u32[]{:S(2)}) collective-permute-start(bf16[2,32,256]{2,1,0:T(8,128)(2,1)S(1)} %pad_maximum_fusion.1.pair_ref), channel_id=1, source_target_pairs={{0,10},{1,3},{2,8},{3,1},{4,14},{5,7},{6,12},{7,5},{8,2},{9,11},{1... | collective-permute-start | bytes 98312 | tf_op jit(solution)/shard_map/ppermute | solution.py:132
  20.1 4.4 %collective-permute-start.4 = (bf16[2,32,256]{2,1,0:T(8,128)(2,1)S(1)}, bf16[2,32,256]{2,1,0:T(8,128)(2,1)S(1)}, u32[]{:S(2)}, u32[]{:S(2)}) collective-permute-start(bf16[2,32,256]{2,1,0:T(8,128)(2,1)S(1)} %pad_maximum_fusion.1.pair_ref), channel_id=1, source_target_pairs={{0,8},{1,9},{2,10},{3,11},{4,12},{5,13},{6,14},{7,15},{8,0},{9,1},... | collective-permute-start | bytes 98312 | tf_op jit(solution)/shard_map/ppermute | solution.py:133
  24.1 1.4 %collective-permute-start.5 = (bf16[3,2,32,256]{3,2,1,0:T(8,128)(2,1)S(1)}, bf16[3,2,32,256]{3,2,1,0:T(8,128)(2,1)S(1)}, u32[]{:S(2)}, u32[]{:S(2)}) collective-permute-start(bf16[3,2,32,256]{3,2,1,0:T(8,128)(2,1)S(1)} %pad_maximum_fusion.near_ref), channel_id=1, source_target_pairs={{0,1},{1,0},{2,3},{3,2},{4,5},{5,4},{6,7},{7,6},{8,9},{9,8},{10,11... | collective-permute-start | bytes 294920 | tf_op jit(solution)/shard_map/ppermute | solution.py:134
  24.2 7.8 %copy-start = (s32[16]{0:T(128)S(1)}, s32[16]{0:T(128)}, u32[]{:S(2)}) copy-start(s32[16]{0:T(128)} %block_map.1) | copy-start | bytes 196

commit v7 on v4

--- a/solution.py
+++ b/solution.py
@@ -10,10 +10,6 @@
 
 NPTS = 48
 radius_cells = 6.0
-
-
-def peer_order(blocks):
-    return [2 * (i % (blocks // 2)) + i // (blocks // 2) for i in range(blocks)]
 
 
 def sensor_table(length, pupil):
@@ -34,7 +30,6 @@
     rows = length // blocks
     height = pupil // blocks
     count = out_ref.shape[1]
-    half_group = blocks // 2
     me = ids[1]
     core = me & 1
     found = []
@@ -45,7 +40,7 @@
             found.append((near_ref[i, r], me ^ (2 * (i + 1 + 4 * core) + r)))
             found.append((far_ref[i, r], me ^ (2 * (i + 5 - 4 * core) + 1 - r)))
     for part, block in found:
-        at = pl.multiple_of(((block & 1) * half_group + (block >> 1)) * height, height)
+        at = pl.multiple_of(block * height, height)
         base[pl.ds(at, height), :pupil] = part[:height]
         base[pl.ds(at, height), pupil:] = part[height:]
     point = jnp.concatenate([modes_ref[i][count * height :].astype(jnp.float32)[:1] for i in range(blocks)], axis=0)
@@ -53,16 +48,14 @@
     scale = 2.0 * math.pi * radius_cells / length
     place = lax.broadcasted_iota(jnp.int32, (blocks, pupil), 1)
     odd = (place & 1) == 1
-    block = place // height
-    row = (2 * (block % half_group) + block // half_group) * height + place % height
 
-    def factor(tilt, index):
-        angle = tilt * ((index - pupil // 2).astype(jnp.float32) * scale)
+    def factor(tilt):
+        angle = tilt * ((place - pupil // 2).astype(jnp.float32) * scale)
         cos, sin = jnp.cos(angle), jnp.sin(angle)
         return jnp.where(odd, -sin, cos), jnp.where(odd, cos, sin)
 
-    row_re, row_im = factor(jnp.cos(theta), row)
-    col_re, col_im = factor(jnp.sin(theta), place)
+    row_re, row_im = factor(jnp.cos(theta))
+    col_re, col_im = factor(jnp.sin(theta))
     table = table_ref[pl.ds(pl.multiple_of(block_map[ids[0]] * rows, rows), rows), :]
     for k in range(blocks):
         at = slice(k * rows, (k + 1) * rows)
@@ -118,11 +111,10 @@
     group = lax.axis_size("mode")
     length = 2 * pupil
     rows = length // blocks
-    order = peer_order(blocks)
     mark = jnp.broadcast_to(mod_points.astype(jnp.bfloat16)[:, None], (8, pupil))
     packed = jnp.concatenate([modes.reshape(count * height, pupil), mark])
     spread = jnp.broadcast_to(packed[None], (blocks,) + packed.shape)
-    gathered = lax.all_to_all(spread, "mod", 0, 0, axis_index_groups=[order])
+    gathered = lax.all_to_all(spread, "mod", 0, 0)
 
     mask = pupil_mask.astype(jnp.float32)
     field = jnp.concatenate([mask * jnp.cos(phase_offset), mask * jnp.sin(phase_offset)]).astype(jnp.bfloat16)
@@ -134,7 +126,6 @@
     far = lax.ppermute(near, "mode", cores)
 
     table = sensor_table(length, pupil)
-    places = np.concatenate([np.arange(height) + b * height for b in order])
     ids = jnp.stack([lax.axis_index("mod"), lax.axis_index("mode")]).astype(jnp.int32)
     vmem = pl.BlockSpec(memory_space=pltpu.VMEM)
     smem = pl.BlockSpec(memory_space=pltpu.SMEM)
@@ -160,7 +151,7 @@
         near,
         fourth,
         far,
-        jnp.asarray(table[:, places], jnp.float32),
+        jnp.asarray(table, jnp.float32),
         jnp.asarray(table.T, jnp.bfloat16),
     )
 

time: 36.7 us -> 38.6 us (1.052)
  waiting for transfers between devices: 12.6 us -> 14.7 us
    all_to_all x1, waiting for transfers between devices: 7.89 us -> 9.89 us  [local(): gathered = lax.all_to_all(spread, 'mod', 0, 0)]
where the time goes in v7:
time: 38.6 us; the launch traced here: 38.3 us
  starting transfers between devices  16.7 us (43%)
  waiting for transfers between devices  14.7 us (38%)
  Pallas kernels  4.4 us (11%)
  local copies, waits for them, and re-layouts  1.64 us (4%)
  between operations  0.73 us (2%)
    all_to_all x1, starting transfers between devices, local(): gathered = lax.all_to_all(spread, 'mod', 0, 0)  11.3 us
    all_to_all x1, waiting for transfers between devices, local(): gathered = lax.all_to_all(spread, 'mod', 0, 0)  9.89 us
    pallas_call x1, Pallas kernels, local(): pl.pallas_call(tangent_kernel, in_specs=[smem, smem] + [vmem] * 7, out_sp...  4.4 us
    ppermute x3, starting transfers between devices, local(): lax.ppermute(pair, 'mode', pairs(t, t + 4))  4.09 us
    ppermute x3, waiting for transfers between devices, local(): lax.ppermute(pair, 'mode', pairs(t, t + 4))  2.41 us
    ppermute x1, waiting for transfers between devices, local(): fourth = lax.ppermute(pair, 'mode', pairs(4, 4))  1.2 us
    ppermute x1, waiting for transfers between devices, local(): pair = jnp.stack([field, lax.ppermute(field, 'mode', cores)])  1.17 us
    broadcast_in_dim x1, local copies, waits for them, and re-layouts, local(): spread = jnp.broadcast_to(packed[None], (blocks,) + packed.shape)  0.85 us
  transfers between devices with their start and end apart: 7, of which 5 were waited for; matrix products, arithmetic and copies ran while one was open for 0% of the time, Pallas kernels for 0%

profile of v7, /device:TPU:4, one launch (start us, length us, event | category | flops | bytes accessed | tf_op | source)
XLA Modules:
  0.0 38.3 jit_solution(16001342631481059558)
XLA Ops:
  0.7 0.8 %concatenate.21 = bf16[72,256]{1,0:T(8,128)(2,1)S(1)} pad(bf16[64,256]{1,0:T(8,128)(2,1)} %bitcast.12, bf16[]{:T(256)} %bitcast.3), padding=0_8x0_0 | pad | bytes 69634 | tf_op jit(solution)/shard_map/concatenate | solution.py:115
  1.4 0.9 %broadcast_in_dim.5 = bf16[16,72,256]{2,1,0:T(8,128)(2,1)} broadcast(bf16[72,256]{1,0:T(8,128)(2,1)S(1)} %concatenate.21), dimensions={1,2} | broadcast | bytes 626688 | tf_op jit(solution)/shard_map/broadcast_in_dim | solution.py:116
  2.3 0.0 copy-start.3
  2.3 0.0 copy-start.4
  2.3 0.0 copy-start.1
  2.3 11.3 %all-to-all-start = ((bf16[16,72,256]{2,1,0:T(8,128)(2,1)}), bf16[16,72,256]{2,1,0:T(8,128)(2,1)S(1)}, u32[]{:S(2)}, u32[]{:S(2)}) async-start(bf16[16,72,256]{2,1,0:T(8,128)(2,1)} %broadcast_in_dim.5), calls=%async_computation | async-start | bytes 1179648 | tf_op jit(solution)/shard_map/all_to_all | solution.py:117
  13.6 0.0 copy-done.3
  13.6 0.0 copy-done.4
  13.6 0.0 copy-start.2
  13.7 0.1 multiply_convert_fusion.1
  13.7 0.1 collective-permute-start
  13.8 1.2 %collective-permute-done = bf16[32,256]{1,0:T(8,128)(2,1)S(1)} collective-permute-done((bf16[32,256]{1,0:T(8,128)(2,1)S(1)}, bf16[32,256]{1,0:T(8,128)(2,1)S(1)}, u32[]{:S(2)}, u32[]{:S(2)}) %collective-permute-start) | collective-permute-done | bytes 16416 | tf_op jit(solution)/shard_map/ppermute | solution.py:123
  15.0 0.5 %collective-permute-start.3 = (bf16[2,32,256]{2,1,0:T(8,128)(2,1)S(1)}, bf16[2,32,256]{2,1,0:T(8,128)(2,1)S(1)}, u32[]{:S(2)}, u32[]{:S(2)}) collective-permute-start(bf16[2,32,256]{2,1,0:T(8,128)(2,1)S(1)} %pad_maximum_fusion.1.pair_ref), channel_id=1, source_target_pairs={{0,6},{1,15},{2,4},{3,13},{4,2},{5,11},{6,0},{7,9},{8,14},{9,7},{1... | collective-permute-start | bytes 98312 | tf_op jit(solution)/shard_map/ppermute | solution.py:124
  15.6 2.7 %collective-permute-start.2 = (bf16[2,32,256]{2,1,0:T(8,128)(2,1)S(1)}, bf16[2,32,256]{2,1,0:T(8,128)(2,1)S(1)}, u32[]{:S(2)}, u32[]{:S(2)}) collective-permute-start(bf16[2,32,256]{2,1,0:T(8,128)(2,1)S(1)} %pad_maximum_fusion.1.pair_ref), channel_id=1, source_target_pairs={{0,4},{1,13},{2,6},{3,15},{4,0},{5,9},{6,2},{7,11},{8,12},{9,5},{1... | collective-permute-start | bytes 98312 | tf_op jit(solution)/shard_map/ppermute | solution.py:124
  18.3 0.8 %collective-permute-start.1 = (bf16[2,32,256]{2,1,0:T(8,128)(2,1)S(1)}, bf16[2,32,256]{2,1,0:T(8,128)(2,1)S(1)}, u32[]{:S(2)}, u32[]{:S(2)}) collective-permute-start(bf16[2,32,256]{2,1,0:T(8,128)(2,1)S(1)} %pad_maximum_fusion.1.pair_ref), channel_id=1, source_target_pairs={{0,2},{1,11},{2,0},{3,9},{4,6},{5,15},{6,4},{7,13},{8,10},{9,3},{1... | collective-permute-start | bytes 98312 | tf_op jit(solution)/shard_map/ppermute | solution.py:124
  19.1 0.7 %collective-permute-start.4 = (bf16[2,32,256]{2,1,0:T(8,128)(2,1)S(1)}, bf16[2,32,256]{2,1,0:T(8,128)(2,1)S(1)}, u32[]{:S(2)}, u32[]{:S(2)}) collective-permute-start(bf16[2,32,256]{2,1,0:T(8,128)(2,1)S(1)} %pad_maximum_fusion.1.pair_ref), channel_id=1, source_target_pairs={{0,8},{1,9},{2,10},{3,11},{4,12},{5,13},{6,14},{7,15},{8,0},{9,1},... | collective-permute-start | bytes 98312 | tf_op jit(solution)/shard_map/ppermute | solution.py:125
  19.8 0.0 collective-permute-done.3
  19.8 1.5 %collective-permute-done.2 = bf16[2,32,256]{2,1,0:T(8,128)(2,1)S(1)} collective-permute-done((bf16[2,32,256]{2,1,0:T(8,128)(2,1)S(1)}, bf16[2,32,256]{2,1,0:T(8,128)(2,1)S(1)}, u32[]{:S(2)}, u32[]{:S(2)}) %collective-permute-start.2) | collective-permute-done | bytes 32800 | tf_op jit(solution)/shard_map/ppermute | solution.py:124
  21.3 0.9 %collective-permute-done.1 = bf16[2,32,256]{2,1,0:T(8,128)(2,1)S(1)} collective-permute-done((bf16[2,32,256]{2,1,0:T(8,128)(2,1)S(1)}, bf16[2,32,256]{2,1,0:T(8,128)(2,1)S(1)}, u32[]{:S(2)}, u32[]{:S(2)}) %collective-permute-start.1) | collective-permute-done | bytes 32800 | tf_op jit(solution)/shard_map/ppermute | solution.py:124
  22.2 0.5 %collective-permute-start.5 = (bf16[3,2,32,256]{3,2,1,0:T(8,128)(2,1)S(1)}, bf16[3,2,32,256]{3,2,1,0:T(8,128)(2,1)S(1)}, u32[]{:S(2)}, u32[]{:S(2)}) collective-permute-start(bf16[3,2,32,256]{3,2,1,0:T(8,128)(2,1)S(1)} %pad_maximum_fusion.near_ref), channel_id=1, source_target_pairs={{0,1},{1,0},{2,3},{3,2},{4,5},{5,4},{6,7},{7,6},{8,9},{9,8},{10,11... | collective-permute-start | bytes 294920 | tf_op jit(solution)/shard_map/ppermute | solution.py:126
  22.7 0.0 copy-start
  22.7 0.1 pad_add_fusion.ids
  22.8 1.2 %collective-permute-done.4.fourth_ref = bf16[2,32,256]{2,1,0:T(8,128)(2,1)S(1)} collective-permute-done((bf16[2,32,256]{2,1,0:T(8,128)(2,1)S(1)}, bf16[2,32,256]{2,1,0:T(8,128)(2,1)S(1)}, u32[]{:S(2)}, u32[]{:S(2)}) %collective-permute-start.4) | collective-permute-done | bytes 32800 | tf_op jit(solution)/shard_map/ppermute | solution.py:125
  24.0 0.0 collective-permute-done.5.far_ref
  24.0 9.9 %all-to-all-done.modes_ref = bf16[16,72,256]{2,1,0:T(8,128)(2,1)S(1)} async-done(((bf16[16,72,256]{2,1,0:T(8,128)(2,1)}), bf16[16,72,256]{2,1,0:T(8,128)(2,1)S(1)}, u32[]{:S(2)}, u32[]{:S(2)}) %all-to-all-start) | async-done | bytes 589856 | tf_op jit(solution)/shard_map/all_to_all | solution.py:117
  33.9 0.0 copy-done.1
  33.9 0.0 copy-done.2
  33.9 0.0 copy-done
  33.9 4.4 %tangent.1 = f32[32,4,512]{2,1,0:T(4,128)} custom-call(s32[16]{0:T(128)S(1)} %copy-done, s32[2]{0:T(128)S(1)} %pad_add_fusion.ids, bf16[16,72,256]{2,1,0:T(8,128)(2,1)S(1)} %all-to-all-done.modes_ref, bf16[2,32,256]{2,1,0:T(8,128)(2,1)S(1)} %pad_maximum_fusion.1.pair_ref, bf16[3,2,32,256]{3,2,1,0:T(8,128)(2,1)S(1)} %pad_maximum_fusion.near_ref, ...), custom_call_target="tpu_custom_call" | custom-call | flops 2700000000 | bytes 2000000 | tf_op jit(solution)/shard_map/tangent/pallas_call | solution.py:132
  (3 shorter events, 0.0 us)
Async XLA Ops:
  2.3 11.3 %copy-start.3 = (f32[16,256]{1,0:T(8,128)S(1)}, f32[16,256]{1,0:T(8,128)}, u32[]{:S(2)}) copy-start(f32[16,256]{1,0:T(8,128)} %param.9) | copy-start | bytes 49156
  2.3 11.4 %copy-start.4 = (s32[16,256]{1,0:T(8,128)S(1)}, s32[16,256]{1,0:T(8,128)}, u32[]{:S(2)}) copy-start(s32[16,256]{1,0:T(8,128)} %param.8) | copy-start | bytes 49156
  2.3 31.6 %copy-start.1 = (f32[512,256]{1,0:T(8,128)S(1)}, f32[512,256]{1,0:T(8,128)}, u32[]{:S(2)}) copy-start(f32[512,256]{1,0:T(8,128)} %constant.11.clone.table_ref) | copy-start | bytes 1572868
  2.3 31.6 %all-to-all-start = ((bf16[16,72,256]{2,1,0:T(8,128)(2,1)}), bf16[16,72,256]{2,1,0:T(8,128)(2,1)S(1)}, u32[]{:S(2)}, u32[]{:S(2)}) async-start(bf16[16,72,256]{2,1,0:T(8,128)(2,1)} %broadcast_in_dim.5), calls=%async_computation | async-start | bytes 1179648 | tf_op jit(solution)/shard_map/all_to_all | solution.py:117
  13.6 20.3 %copy-start.2 = (bf16[256,512]{1,0:T(8,128)(2,1)S(1)}, bf16[256,512]{1,0:T(8,128)(2,1)}, u32[]{:S(2)}) copy-start(bf16[256,512]{1,0:T(8,128)(2,1)} %constant.12.clone.second_ref) | copy-start | bytes 786436
  13.7 1.3 %collective-permute-start = (bf16[32,256]{1,0:T(8,128)(2,1)S(1)}, bf16[32,256]{1,0:T(8,128)(2,1)S(1)}, u32[]{:S(2)}, u32[]{:S(2)}) collective-permute-start(bf16[32,256]{1,0:T(8,128)(2,1)S(1)} %pad_maximum_fusion.2), channel_id=1, source_target_pairs={{0,1},{1,0},{2,3},{3,2},{4,5},{5,4},{6,7},{7,6},{8,9},{9,8},{10,11... | collective-permute-start | bytes 49160 | tf_op jit(solution)/shard_map/ppermute | solution.py:123
  15.0 4.8 %collective-permute-start.3 = (bf16[2,32,256]{2,1,0:T(8,128)(2,1)S(1)}, bf16[2,32,256]{2,1,0:T(8,128)(2,1)S(1)}, u32[]{:S(2)}, u32[]{:S(2)}) collective-permute-start(bf16[2,32,256]{2,1,0:T(8,128)(2,1)S(1)} %pad_maximum_fusion.1.pair_ref), channel_id=1, source_target_pairs={{0,6},{1,15},{2,4},{3,13},{4,2},{5,11},{6,0},{7,9},{8,14},{9,7},{1... | collective-permute-start | bytes 98312 | tf_op jit(solution)/shard_map/ppermute | solution.py:124
  15.6 5.8 %collective-permute-start.2 = (bf16[2,32,256]{2,1,0:T(8,128)(2,1)S(1)}, bf16[2,32,256]{2,1,0:T(8,128)(2,1)S(1)}, u32[]{:S(2)}, u32[]{:S(2)}) collective-permute-start(bf16[2,32,256]{2,1,0:T(8,128)(2,1)S(1)} %pad_maximum_fusion.1.pair_ref), channel_id=1, source_target_pairs={{0,4},{1,13},{2,6},{3,15},{4,0},{5,9},{6,2},{7,11},{8,12},{9,5},{1... | collective-permute-start | bytes 98312 | tf_op jit(solution)/shard_map/ppermute | solution.py:124
  18.3 3.9 %collective-permute-start.1 = (bf16[2,32,256]{2,1,0:T(8,128)(2,1)S(1)}, bf16[2,32,256]{2,1,0:T(8,128)(2,1)S(1)}, u32[]{:S(2)}, u32[]{:S(2)}) collective-permute-start(bf16[2,32,256]{2,1,0:T(8,128)(2,1)S(1)} %pad_maximum_fusion.1.pair_ref), channel_id=1, source_target_pairs={{0,2},{1,11},{2,0},{3,9},{4,6},{5,15},{6,4},{7,13},{8,10},{9,3},{1... | collective-permute-start | bytes 98312 | tf_op jit(solution)/shard_map/ppermute | solution.py:124
  19.1 4.9 %collective-permute-start.4 = (bf16[2,32,256]{2,1,0:T(8,128)(2,1)S(1)}, bf16[2,32,256]{2,1,0:T(8,128)(2,1)S(1)}, u32[]{:S(2)}, u32[]{:S(2)}) collective-permute-start(bf16[2,32,256]{2,1,0:T(8,128)(2,1)S(1)} %pad_maximum_fusion.1.pair_ref), channel_id=1, source_target_pairs={{0,8},{1,9},{2,10},{3,11},{4,12},{5,13},{6,14},{7,15},{8,0},{9,1},... | collective-permute-start | bytes 98312 | tf_op jit(solution)/shard_map/ppermute | solution.py:125
  22.2 1.8 %collective-permute-start.5 = (bf16[3,2,32,256]{3,2,1,0:T(8,128)(2,1)S(1)}, bf16[3,2,32,256]{3,2,1,0:T(8,128)(2,1)S(1)}, u32[]{:S(2)}, u32[]{:S(2)}) collective-permute-start(bf16[3,2,32,256]{3,2,1,0:T(8,128)(2,1)S(1)} %pad_maximum_fusion.near_ref), channel_id=1, source_target_pairs={{0,1},{1,0},{2,3},{3,2},{4,5},{5,4},{6,7},{7,6},{8,9},{9,8},{10,11... | collective-permute-start | bytes 294920 | tf_op jit(solution)/shard_map/ppermute | solution.py:126
  22.7 11.2 %copy-start = (s32[16]{0:T(128)S(1)}, s32[16]{0:T(128)}, u32[]{:S(2)}) copy-start(s32[16]{0:T(128)} %block_map.1) | copy-start | bytes 196

commit v8 on v4

--- a/solution.py
+++ b/solution.py
@@ -13,7 +13,8 @@
 
 
 def peer_order(blocks):
-    return [2 * (i % (blocks // 2)) + i // (blocks // 2) for i in range(blocks)]
+    chips = blocks // 2
+    return [2 * (chips - 1 - i % chips) + i // chips for i in range(blocks)]
 
 
 def sensor_table(length, pupil):
@@ -45,7 +46,7 @@
             found.append((near_ref[i, r], me ^ (2 * (i + 1 + 4 * core) + r)))
             found.append((far_ref[i, r], me ^ (2 * (i + 5 - 4 * core) + 1 - r)))
     for part, block in found:
-        at = pl.multiple_of(((block & 1) * half_group + (block >> 1)) * height, height)
+        at = pl.multiple_of(((block & 1) * half_group + half_group - 1 - (block >> 1)) * height, height)
         base[pl.ds(at, height), :pupil] = part[:height]
         base[pl.ds(at, height), pupil:] = part[height:]
     point = jnp.concatenate([modes_ref[i][count * height :].astype(jnp.float32)[:1] for i in range(blocks)], axis=0)
@@ -54,7 +55,7 @@
     place = lax.broadcasted_iota(jnp.int32, (blocks, pupil), 1)
     odd = (place & 1) == 1
     block = place // height
-    row = (2 * (block % half_group) + block // half_group) * height + place % height
+    row = (2 * (half_group - 1 - block % half_group) + block // half_group) * height + place % height
 
     def factor(tilt, index):
         angle = tilt * ((index - pupil // 2).astype(jnp.float32) * scale)

time: 36.7 us -> 36.6 us (level)
  waiting for transfers between devices: 12.6 us -> 12 us
  starting transfers between devices: 16.9 us -> 17.3 us
    all_to_all x1, waiting for transfers between devices: 7.89 us -> 6.96 us  [local(): gathered = lax.all_to_all(spread, 'mod', 0, 0, axis_index_groups=[order])]
    all_to_all x1, starting transfers between devices: 11.3 us -> 11.8 us  [local(): gathered = lax.all_to_all(spread, 'mod', 0, 0, axis_index_groups=[order])]
where the time goes in v8:
time: 36.6 us; the launch traced here: 36.3 us
  starting transfers between devices  17.3 us (47%)
  waiting for transfers between devices  12 us (33%)
  Pallas kernels  4.4 us (12%)
  local copies, waits for them, and re-layouts  1.64 us (4%)
  between operations  0.71 us (2%)
    all_to_all x1, starting transfers between devices, local(): gathered = lax.all_to_all(spread, 'mod', 0, 0, axis_index_groups=[order])  11.8 us
    all_to_all x1, waiting for transfers between devices, local(): gathered = lax.all_to_all(spread, 'mod', 0, 0, axis_index_groups=[order])  6.96 us
    pallas_call x1, Pallas kernels, local(): pl.pallas_call(tangent_kernel, in_specs=[smem, smem] + [vmem] * 7, out_sp...  4.4 us
    ppermute x3, starting transfers between devices, local(): lax.ppermute(pair, 'mode', pairs(t, t + 4))  4.09 us
    ppermute x3, waiting for transfers between devices, local(): lax.ppermute(pair, 'mode', pairs(t, t + 4))  2.41 us
    ppermute x1, waiting for transfers between devices, local(): fourth = lax.ppermute(pair, 'mode', pairs(4, 4))  1.49 us
    ppermute x1, waiting for transfers between devices, local(): pair = jnp.stack([field, lax.ppermute(field, 'mode', cores)])  1.17 us
    broadcast_in_dim x1, local copies, waits for them, and re-layouts, local(): spread = jnp.broadcast_to(packed[None], (blocks,) + packed.shape)  0.85 us
  transfers between devices with their start and end apart: 7, of which 5 were waited for; matrix products, arithmetic and copies ran while one was open for 0% of the time, Pallas kernels for 0%

profile of v8, /device:TPU:4, one launch (start us, length us, event | category | flops | bytes accessed | tf_op | source)
XLA Modules:
  0.0 36.3 jit_solution(3094724518973698241)
XLA Ops:
  0.7 0.8 %concatenate.21 = bf16[72,256]{1,0:T(8,128)(2,1)S(1)} pad(bf16[64,256]{1,0:T(8,128)(2,1)} %bitcast.12, bf16[]{:T(256)} %bitcast.3), padding=0_8x0_0 | pad | bytes 69634 | tf_op jit(solution)/shard_map/concatenate | solution.py:124
  1.4 0.9 %broadcast_in_dim.5 = bf16[16,72,256]{2,1,0:T(8,128)(2,1)} broadcast(bf16[72,256]{1,0:T(8,128)(2,1)S(1)} %concatenate.21), dimensions={1,2} | broadcast | bytes 626688 | tf_op jit(solution)/shard_map/broadcast_in_dim | solution.py:125
  2.3 0.0 copy-start.3
  2.3 0.0 copy-start.4
  2.3 0.0 copy-start.1
  2.3 11.8 %all-to-all-start = ((bf16[16,72,256]{2,1,0:T(8,128)(2,1)}), bf16[16,72,256]{2,1,0:T(8,128)(2,1)S(1)}, u32[]{:S(2)}, u32[]{:S(2)}) async-start(bf16[16,72,256]{2,1,0:T(8,128)(2,1)} %broadcast_in_dim.5), calls=%async_computation | async-start | bytes 1179648 | tf_op jit(solution)/shard_map/all_to_all | solution.py:126
  14.1 0.0 copy-done.3
  14.1 0.0 copy-done.4
  14.1 0.0 copy-start.2
  14.1 0.1 multiply_convert_fusion.1
  14.2 0.1 collective-permute-start
  14.3 1.2 %collective-permute-done = bf16[32,256]{1,0:T(8,128)(2,1)S(1)} collective-permute-done((bf16[32,256]{1,0:T(8,128)(2,1)S(1)}, bf16[32,256]{1,0:T(8,128)(2,1)S(1)}, u32[]{:S(2)}, u32[]{:S(2)}) %collective-permute-start) | collective-permute-done | bytes 16416 | tf_op jit(solution)/shard_map/ppermute | solution.py:132
  15.5 0.5 %collective-permute-start.3 = (bf16[2,32,256]{2,1,0:T(8,128)(2,1)S(1)}, bf16[2,32,256]{2,1,0:T(8,128)(2,1)S(1)}, u32[]{:S(2)}, u32[]{:S(2)}) collective-permute-start(bf16[2,32,256]{2,1,0:T(8,128)(2,1)S(1)} %pad_maximum_fusion.1.pair_ref), channel_id=1, source_target_pairs={{0,6},{1,15},{2,4},{3,13},{4,2},{5,11},{6,0},{7,9},{8,14},{9,7},{1... | collective-permute-start | bytes 98312 | tf_op jit(solution)/shard_map/ppermute | solution.py:133
  16.0 2.7 %collective-permute-start.2 = (bf16[2,32,256]{2,1,0:T(8,128)(2,1)S(1)}, bf16[2,32,256]{2,1,0:T(8,128)(2,1)S(1)}, u32[]{:S(2)}, u32[]{:S(2)}) collective-permute-start(bf16[2,32,256]{2,1,0:T(8,128)(2,1)S(1)} %pad_maximum_fusion.1.pair_ref), channel_id=1, source_target_pairs={{0,4},{1,13},{2,6},{3,15},{4,0},{5,9},{6,2},{7,11},{8,12},{9,5},{1... | collective-permute-start | bytes 98312 | tf_op jit(solution)/shard_map/ppermute | solution.py:133
  18.7 0.8 %collective-permute-start.1 = (bf16[2,32,256]{2,1,0:T(8,128)(2,1)S(1)}, bf16[2,32,256]{2,1,0:T(8,128)(2,1)S(1)}, u32[]{:S(2)}, u32[]{:S(2)}) collective-permute-start(bf16[2,32,256]{2,1,0:T(8,128)(2,1)S(1)} %pad_maximum_fusion.1.pair_ref), channel_id=1, source_target_pairs={{0,2},{1,11},{2,0},{3,9},{4,6},{5,15},{6,4},{7,13},{8,10},{9,3},{1... | collective-permute-start | bytes 98312 | tf_op jit(solution)/shard_map/ppermute | solution.py:133
  19.6 0.7 %collective-permute-start.4 = (bf16[2,32,256]{2,1,0:T(8,128)(2,1)S(1)}, bf16[2,32,256]{2,1,0:T(8,128)(2,1)S(1)}, u32[]{:S(2)}, u32[]{:S(2)}) collective-permute-start(bf16[2,32,256]{2,1,0:T(8,128)(2,1)S(1)} %pad_maximum_fusion.1.pair_ref), channel_id=1, source_target_pairs={{0,8},{1,9},{2,10},{3,11},{4,12},{5,13},{6,14},{7,15},{8,0},{9,1},... | collective-permute-start | bytes 98312 | tf_op jit(solution)/shard_map/ppermute | solution.py:134
  20.3 0.0 collective-permute-done.3
  20.3 1.5 %collective-permute-done.2 = bf16[2,32,256]{2,1,0:T(8,128)(2,1)S(1)} collective-permute-done((bf16[2,32,256]{2,1,0:T(8,128)(2,1)S(1)}, bf16[2,32,256]{2,1,0:T(8,128)(2,1)S(1)}, u32[]{:S(2)}, u32[]{:S(2)}) %collective-permute-start.2) | collective-permute-done | bytes 32800 | tf_op jit(solution)/shard_map/ppermute | solution.py:133
  21.8 0.9 %collective-permute-done.1 = bf16[2,32,256]{2,1,0:T(8,128)(2,1)S(1)} collective-permute-done((bf16[2,32,256]{2,1,0:T(8,128)(2,1)S(1)}, bf16[2,32,256]{2,1,0:T(8,128)(2,1)S(1)}, u32[]{:S(2)}, u32[]{:S(2)}) %collective-permute-start.1) | collective-permute-done | bytes 32800 | tf_op jit(solution)/shard_map/ppermute | solution.py:133
  22.7 0.7 %collective-permute-start.5 = (bf16[3,2,32,256]{3,2,1,0:T(8,128)(2,1)S(1)}, bf16[3,2,32,256]{3,2,1,0:T(8,128)(2,1)S(1)}, u32[]{:S(2)}, u32[]{:S(2)}) collective-permute-start(bf16[3,2,32,256]{3,2,1,0:T(8,128)(2,1)S(1)} %pad_maximum_fusion.near_ref), channel_id=1, source_target_pairs={{0,1},{1,0},{2,3},{3,2},{4,5},{5,4},{6,7},{7,6},{8,9},{9,8},{10,11... | collective-permute-start | bytes 294920 | tf_op jit(solution)/shard_map/ppermute | solution.py:135
  23.3 0.0 copy-start
  23.3 0.1 pad_add_fusion.ids
  23.4 1.5 %collective-permute-done.4.fourth_ref = bf16[2,32,256]{2,1,0:T(8,128)(2,1)S(1)} collective-permute-done((bf16[2,32,256]{2,1,0:T(8,128)(2,1)S(1)}, bf16[2,32,256]{2,1,0:T(8,128)(2,1)S(1)}, u32[]{:S(2)}, u32[]{:S(2)}) %collective-permute-start.4) | collective-permute-done | bytes 32800 | tf_op jit(solution)/shard_map/ppermute | solution.py:134
  24.9 0.0 collective-permute-done.5.far_ref
  24.9 7.0 %all-to-all-done.modes_ref = bf16[16,72,256]{2,1,0:T(8,128)(2,1)S(1)} async-done(((bf16[16,72,256]{2,1,0:T(8,128)(2,1)}), bf16[16,72,256]{2,1,0:T(8,128)(2,1)S(1)}, u32[]{:S(2)}, u32[]{:S(2)}) %all-to-all-start) | async-done | bytes 589856 | tf_op jit(solution)/shard_map/all_to_all | solution.py:126
  31.9 0.0 copy-done.1
  31.9 0.0 copy-done.2
  31.9 0.0 copy-done
  31.9 4.4 %tangent.1 = f32[32,4,512]{2,1,0:T(4,128)} custom-call(s32[16]{0:T(128)S(1)} %copy-done, s32[2]{0:T(128)S(1)} %pad_add_fusion.ids, bf16[16,72,256]{2,1,0:T(8,128)(2,1)S(1)} %all-to-all-done.modes_ref, bf16[2,32,256]{2,1,0:T(8,128)(2,1)S(1)} %pad_maximum_fusion.1.pair_ref, bf16[3,2,32,256]{3,2,1,0:T(8,128)(2,1)S(1)} %pad_maximum_fusion.near_ref, ...), custom_call_target="tpu_custom_call" | custom-call | flops 2700000000 | bytes 2000000 | tf_op jit(solution)/shard_map/tangent/pallas_call | solution.py:142
  (3 shorter events, 0.0 us)
Async XLA Ops:
  2.3 11.8 %copy-start.3 = (f32[16,256]{1,0:T(8,128)S(1)}, f32[16,256]{1,0:T(8,128)}, u32[]{:S(2)}) copy-start(f32[16,256]{1,0:T(8,128)} %param.9) | copy-start | bytes 49156
  2.3 11.8 %copy-start.4 = (s32[16,256]{1,0:T(8,128)S(1)}, s32[16,256]{1,0:T(8,128)}, u32[]{:S(2)}) copy-start(s32[16,256]{1,0:T(8,128)} %param.8) | copy-start | bytes 49156
  2.3 29.6 %copy-start.1 = (f32[512,256]{1,0:T(8,128)S(1)}, f32[512,256]{1,0:T(8,128)}, u32[]{:S(2)}) copy-start(f32[512,256]{1,0:T(8,128)} %constant.11.clone.table_ref) | copy-start | bytes 1572868
  2.3 29.6 %all-to-all-start = ((bf16[16,72,256]{2,1,0:T(8,128)(2,1)}), bf16[16,72,256]{2,1,0:T(8,128)(2,1)S(1)}, u32[]{:S(2)}, u32[]{:S(2)}) async-start(bf16[16,72,256]{2,1,0:T(8,128)(2,1)} %broadcast_in_dim.5), calls=%async_computation | async-start | bytes 1179648 | tf_op jit(solution)/shard_map/all_to_all | solution.py:126
  14.1 17.8 %copy-start.2 = (bf16[256,512]{1,0:T(8,128)(2,1)S(1)}, bf16[256,512]{1,0:T(8,128)(2,1)}, u32[]{:S(2)}) copy-start(bf16[256,512]{1,0:T(8,128)(2,1)} %constant.12.clone.second_ref) | copy-start | bytes 786436
  14.2 1.3 %collective-permute-start = (bf16[32,256]{1,0:T(8,128)(2,1)S(1)}, bf16[32,256]{1,0:T(8,128)(2,1)S(1)}, u32[]{:S(2)}, u32[]{:S(2)}) collective-permute-start(bf16[32,256]{1,0:T(8,128)(2,1)S(1)} %pad_maximum_fusion.2), channel_id=1, source_target_pairs={{0,1},{1,0},{2,3},{3,2},{4,5},{5,4},{6,7},{7,6},{8,9},{9,8},{10,11... | collective-permute-start | bytes 49160 | tf_op jit(solution)/shard_map/ppermute | solution.py:132
  15.5 4.8 %collective-permute-start.3 = (bf16[2,32,256]{2,1,0:T(8,128)(2,1)S(1)}, bf16[2,32,256]{2,1,0:T(8,128)(2,1)S(1)}, u32[]{:S(2)}, u32[]{:S(2)}) collective-permute-start(bf16[2,32,256]{2,1,0:T(8,128)(2,1)S(1)} %pad_maximum_fusion.1.pair_ref), channel_id=1, source_target_pairs={{0,6},{1,15},{2,4},{3,13},{4,2},{5,11},{6,0},{7,9},{8,14},{9,7},{1... | collective-permute-start | bytes 98312 | tf_op jit(solution)/shard_map/ppermute | solution.py:133
  16.0 5.8 %collective-permute-start.2 = (bf16[2,32,256]{2,1,0:T(8,128)(2,1)S(1)}, bf16[2,32,256]{2,1,0:T(8,128)(2,1)S(1)}, u32[]{:S(2)}, u32[]{:S(2)}) collective-permute-start(bf16[2,32,256]{2,1,0:T(8,128)(2,1)S(1)} %pad_maximum_fusion.1.pair_ref), channel_id=1, source_target_pairs={{0,4},{1,13},{2,6},{3,15},{4,0},{5,9},{6,2},{7,11},{8,12},{9,5},{1... | collective-permute-start | bytes 98312 | tf_op jit(solution)/shard_map/ppermute | solution.py:133
  18.7 3.9 %collective-permute-start.1 = (bf16[2,32,256]{2,1,0:T(8,128)(2,1)S(1)}, bf16[2,32,256]{2,1,0:T(8,128)(2,1)S(1)}, u32[]{:S(2)}, u32[]{:S(2)}) collective-permute-start(bf16[2,32,256]{2,1,0:T(8,128)(2,1)S(1)} %pad_maximum_fusion.1.pair_ref), channel_id=1, source_target_pairs={{0,2},{1,11},{2,0},{3,9},{4,6},{5,15},{6,4},{7,13},{8,10},{9,3},{1... | collective-permute-start | bytes 98312 | tf_op jit(solution)/shard_map/ppermute | solution.py:133
  19.6 5.3 %collective-permute-start.4 = (bf16[2,32,256]{2,1,0:T(8,128)(2,1)S(1)}, bf16[2,32,256]{2,1,0:T(8,128)(2,1)S(1)}, u32[]{:S(2)}, u32[]{:S(2)}) collective-permute-start(bf16[2,32,256]{2,1,0:T(8,128)(2,1)S(1)} %pad_maximum_fusion.1.pair_ref), channel_id=1, source_target_pairs={{0,8},{1,9},{2,10},{3,11},{4,12},{5,13},{6,14},{7,15},{8,0},{9,1},... | collective-permute-start | bytes 98312 | tf_op jit(solution)/shard_map/ppermute | solution.py:134
  22.7 2.2 %collective-permute-start.5 = (bf16[3,2,32,256]{3,2,1,0:T(8,128)(2,1)S(1)}, bf16[3,2,32,256]{3,2,1,0:T(8,128)(2,1)S(1)}, u32[]{:S(2)}, u32[]{:S(2)}) collective-permute-start(bf16[3,2,32,256]{3,2,1,0:T(8,128)(2,1)S(1)} %pad_maximum_fusion.near_ref), channel_id=1, source_target_pairs={{0,1},{1,0},{2,3},{3,2},{4,5},{5,4},{6,7},{7,6},{8,9},{9,8},{10,11... | collective-permute-start | bytes 294920 | tf_op jit(solution)/shard_map/ppermute | solution.py:135
  23.3 8.5 %copy-start = (s32[16]{0:T(128)S(1)}, s32[16]{0:T(128)}, u32[]{:S(2)}) copy-start(s32[16]{0:T(128)} %block_map.1) | copy-start | bytes 196

commit v9 on v8

--- a/solution.py
+++ b/solution.py
@@ -43,8 +43,8 @@
         found.append((pair_ref[r], me ^ r))
         found.append((fourth_ref[r], me ^ (8 + r)))
         for i in range(3):
-            found.append((near_ref[i, r], me ^ (2 * (i + 1 + 4 * core) + r)))
-            found.append((far_ref[i, r], me ^ (2 * (i + 5 - 4 * core) + 1 - r)))
+            found.append((near_ref[i, r], me ^ (2 * (i + 5 - 4 * core) + r)))
+            found.append((far_ref[i, r], me ^ (2 * (i + 1 + 4 * core) + 1 - r)))
     for part, block in found:
         at = pl.multiple_of(((block & 1) * half_group + half_group - 1 - (block >> 1)) * height, height)
         base[pl.ds(at, height), :pupil] = part[:height]
@@ -130,7 +130,7 @@
     pairs = lambda t0, t1: [(i, i ^ (2 * (t1 if i & 1 else t0))) for i in range(group)]
     cores = [(i, i ^ 1) for i in range(group)]
     pair = jnp.stack([field, lax.ppermute(field, "mode", cores)])
-    near = jnp.stack([lax.ppermute(pair, "mode", pairs(t, t + 4)) for t in range(1, 4)])
+    near = jnp.stack([lax.ppermute(pair, "mode", pairs(t + 4, t)) for t in range(1, 4)])
     fourth = lax.ppermute(pair, "mode", pairs(4, 4))
     far = lax.ppermute(near, "mode", cores)
 

time: 36.6 us -> 36.6 us (level)
  waiting for transfers between devices: 12 us -> 10.9 us
  starting transfers between devices: 17.3 us -> 18.4 us
    all_to_all x1, waiting for transfers between devices: 6.96 us -> 5.76 us  [local(): gathered = lax.all_to_all(spread, 'mod', 0, 0, axis_index_groups=[order])]
    ppermute x3, starting transfers between devices: 4.09 us -> 5.11 us  [local(): lax.ppermute(pair, 'mode', pairs(t + 4, t))]
    ppermute x1, waiting for transfers between devices: 1.49 us -> 0.59 us  [local(): fourth = lax.ppermute(pair, 'mode', pairs(4, 4))]
    ppermute x1, starting transfers between devices: 0.68 us -> 1.35 us  [local(): fourth = lax.ppermute(pair, 'mode', pairs(4, 4))]
    ppermute x1, waiting for transfers between devices: 0.01 us -> 0.61 us  [local(): far = lax.ppermute(near, 'mode', cores)]
    ppermute x1, starting transfers between devices: 0.67 us -> 0.09 us  [local(): far = lax.ppermute(near, 'mode', cores)]
  transfers between devices with their start and end apart: 7 -> 7, of which waited for: 5 -> 6; matrix products, arithmetic and copies ran while one was open for 0% -> 0% of each run, Pallas kernels for 0% -> 0%
where the time goes in v9:
time: 36.6 us; the launch traced here: 36.3 us
  starting transfers between devices  18.4 us (50%)
  waiting for transfers between devices  10.9 us (30%)
  Pallas kernels  4.4 us (12%)
  local copies, waits for them, and re-layouts  1.64 us (4%)
  between operations  0.73 us (2%)
    all_to_all x1, starting transfers between devices, local(): gathered = lax.all_to_all(spread, 'mod', 0, 0, axis_index_groups=[order])  11.8 us
    all_to_all x1, waiting for transfers between devices, local(): gathered = lax.all_to_all(spread, 'mod', 0, 0, axis_index_groups=[order])  5.76 us
    ppermute x3, starting transfers between devices, local(): lax.ppermute(pair, 'mode', pairs(t + 4, t))  5.11 us
    pallas_call x1, Pallas kernels, local(): pl.pallas_call(tangent_kernel, in_specs=[smem, smem] + [vmem] * 7, out_sp...  4.4 us
    ppermute x3, waiting for transfers between devices, local(): lax.ppermute(pair, 'mode', pairs(t + 4, t))  2.77 us
    ppermute x1, starting transfers between devices, local(): fourth = lax.ppermute(pair, 'mode', pairs(4, 4))  1.35 us
    ppermute x1, waiting for transfers between devices, local(): pair = jnp.stack([field, lax.ppermute(field, 'mode', cores)])  1.17 us
    broadcast_in_dim x1, local copies, waits for them, and re-layouts, local(): spread = jnp.broadcast_to(packed[None], (blocks,) + packed.shape)  0.85 us
  transfers between devices with their start and end apart: 7, of which 6 were waited for; matrix products, arithmetic and copies ran while one was open for 0% of the time, Pallas kernels for 0%

profile of v9, /device:TPU:4, one launch (start us, length us, event | category | flops | bytes accessed | tf_op | source)
XLA Modules:
  0.0 36.3 jit_solution(4153591209052170002)
XLA Ops:
  0.7 0.8 %concatenate.21 = bf16[72,256]{1,0:T(8,128)(2,1)S(1)} pad(bf16[64,256]{1,0:T(8,128)(2,1)} %bitcast.12, bf16[]{:T(256)} %bitcast.3), padding=0_8x0_0 | pad | bytes 69634 | tf_op jit(solution)/shard_map/concatenate | solution.py:124
  1.4 0.9 %broadcast_in_dim.5 = bf16[16,72,256]{2,1,0:T(8,128)(2,1)} broadcast(bf16[72,256]{1,0:T(8,128)(2,1)S(1)} %concatenate.21), dimensions={1,2} | broadcast | bytes 626688 | tf_op jit(solution)/shard_map/broadcast_in_dim | solution.py:125
  2.3 0.0 copy-start.3
  2.3 0.0 copy-start.4
  2.3 0.0 copy-start.1
  2.3 11.8 %all-to-all-start = ((bf16[16,72,256]{2,1,0:T(8,128)(2,1)}), bf16[16,72,256]{2,1,0:T(8,128)(2,1)S(1)}, u32[]{:S(2)}, u32[]{:S(2)}) async-start(bf16[16,72,256]{2,1,0:T(8,128)(2,1)} %broadcast_in_dim.5), calls=%async_computation | async-start | bytes 1179648 | tf_op jit(solution)/shard_map/all_to_all | solution.py:126
  14.1 0.0 copy-done.3
  14.1 0.0 copy-done.4
  14.1 0.0 copy-start.2
  14.1 0.1 multiply_convert_fusion.1
  14.2 0.1 collective-permute-start
  14.3 1.2 %collective-permute-done = bf16[32,256]{1,0:T(8,128)(2,1)S(1)} collective-permute-done((bf16[32,256]{1,0:T(8,128)(2,1)S(1)}, bf16[32,256]{1,0:T(8,128)(2,1)S(1)}, u32[]{:S(2)}, u32[]{:S(2)}) %collective-permute-start) | collective-permute-done | bytes 16416 | tf_op jit(solution)/shard_map/ppermute | solution.py:132
  15.5 0.6 %collective-permute-start.3 = (bf16[2,32,256]{2,1,0:T(8,128)(2,1)S(1)}, bf16[2,32,256]{2,1,0:T(8,128)(2,1)S(1)}, u32[]{:S(2)}, u32[]{:S(2)}) collective-permute-start(bf16[2,32,256]{2,1,0:T(8,128)(2,1)S(1)} %pad_maximum_fusion.1.pair_ref), channel_id=1, source_target_pairs={{0,14},{1,7},{2,12},{3,5},{4,10},{5,3},{6,8},{7,1},{8,6},{9,15},{1... | collective-permute-start | bytes 98312 | tf_op jit(solution)/shard_map/ppermute | solution.py:133
  16.1 3.5 %collective-permute-start.2 = (bf16[2,32,256]{2,1,0:T(8,128)(2,1)S(1)}, bf16[2,32,256]{2,1,0:T(8,128)(2,1)S(1)}, u32[]{:S(2)}, u32[]{:S(2)}) collective-permute-start(bf16[2,32,256]{2,1,0:T(8,128)(2,1)S(1)} %pad_maximum_fusion.1.pair_ref), channel_id=1, source_target_pairs={{0,12},{1,5},{2,14},{3,7},{4,8},{5,1},{6,10},{7,3},{8,4},{9,13},{1... | collective-permute-start | bytes 98312 | tf_op jit(solution)/shard_map/ppermute | solution.py:133
  19.6 0.9 %collective-permute-start.1 = (bf16[2,32,256]{2,1,0:T(8,128)(2,1)S(1)}, bf16[2,32,256]{2,1,0:T(8,128)(2,1)S(1)}, u32[]{:S(2)}, u32[]{:S(2)}) collective-permute-start(bf16[2,32,256]{2,1,0:T(8,128)(2,1)S(1)} %pad_maximum_fusion.1.pair_ref), channel_id=1, source_target_pairs={{0,10},{1,3},{2,8},{3,1},{4,14},{5,7},{6,12},{7,5},{8,2},{9,11},{1... | collective-permute-start | bytes 98312 | tf_op jit(solution)/shard_map/ppermute | solution.py:133
  20.6 1.3 %collective-permute-start.4 = (bf16[2,32,256]{2,1,0:T(8,128)(2,1)S(1)}, bf16[2,32,256]{2,1,0:T(8,128)(2,1)S(1)}, u32[]{:S(2)}, u32[]{:S(2)}) collective-permute-start(bf16[2,32,256]{2,1,0:T(8,128)(2,1)S(1)} %pad_maximum_fusion.1.pair_ref), channel_id=1, source_target_pairs={{0,8},{1,9},{2,10},{3,11},{4,12},{5,13},{6,14},{7,15},{8,0},{9,1},... | collective-permute-start | bytes 98312 | tf_op jit(solution)/shard_map/ppermute | solution.py:134
  21.9 0.0 collective-permute-done.3
  21.9 0.7 %collective-permute-done.2 = bf16[2,32,256]{2,1,0:T(8,128)(2,1)S(1)} collective-permute-done((bf16[2,32,256]{2,1,0:T(8,128)(2,1)S(1)}, bf16[2,32,256]{2,1,0:T(8,128)(2,1)S(1)}, u32[]{:S(2)}, u32[]{:S(2)}) %collective-permute-start.2) | collective-permute-done | bytes 32800 | tf_op jit(solution)/shard_map/ppermute | solution.py:133
  22.6 2.1 %collective-permute-done.1 = bf16[2,32,256]{2,1,0:T(8,128)(2,1)S(1)} collective-permute-done((bf16[2,32,256]{2,1,0:T(8,128)(2,1)S(1)}, bf16[2,32,256]{2,1,0:T(8,128)(2,1)S(1)}, u32[]{:S(2)}, u32[]{:S(2)}) %collective-permute-start.1) | collective-permute-done | bytes 32800 | tf_op jit(solution)/shard_map/ppermute | solution.py:133
  24.7 0.1 collective-permute-start.5
  24.8 0.0 copy-start
  24.8 0.1 pad_add_fusion.ids
  24.9 0.6 %collective-permute-done.4.fourth_ref = bf16[2,32,256]{2,1,0:T(8,128)(2,1)S(1)} collective-permute-done((bf16[2,32,256]{2,1,0:T(8,128)(2,1)S(1)}, bf16[2,32,256]{2,1,0:T(8,128)(2,1)S(1)}, u32[]{:S(2)}, u32[]{:S(2)}) %collective-permute-start.4) | collective-permute-done | bytes 32800 | tf_op jit(solution)/shard_map/ppermute | solution.py:134
  25.5 0.6 %collective-permute-done.5.far_ref = bf16[3,2,32,256]{3,2,1,0:T(8,128)(2,1)S(1)} collective-permute-done((bf16[3,2,32,256]{3,2,1,0:T(8,128)(2,1)S(1)}, bf16[3,2,32,256]{3,2,1,0:T(8,128)(2,1)S(1)}, u32[]{:S(2)}, u32[]{:S(2)}) %collective-permute-start.5) | collective-permute-done | bytes 98336 | tf_op jit(solution)/shard_map/ppermute | solution.py:135
  26.1 5.8 %all-to-all-done.modes_ref = bf16[16,72,256]{2,1,0:T(8,128)(2,1)S(1)} async-done(((bf16[16,72,256]{2,1,0:T(8,128)(2,1)}), bf16[16,72,256]{2,1,0:T(8,128)(2,1)S(1)}, u32[]{:S(2)}, u32[]{:S(2)}) %all-to-all-start) | async-done | bytes 589856 | tf_op jit(solution)/shard_map/all_to_all | solution.py:126
  31.9 0.0 copy-done.1
  31.9 0.0 copy-done.2
  31.9 0.0 copy-done
  31.9 4.4 %tangent.1 = f32[32,4,512]{2,1,0:T(4,128)} custom-call(s32[16]{0:T(128)S(1)} %copy-done, s32[2]{0:T(128)S(1)} %pad_add_fusion.ids, bf16[16,72,256]{2,1,0:T(8,128)(2,1)S(1)} %all-to-all-done.modes_ref, bf16[2,32,256]{2,1,0:T(8,128)(2,1)S(1)} %pad_maximum_fusion.1.pair_ref, bf16[3,2,32,256]{3,2,1,0:T(8,128)(2,1)S(1)} %pad_maximum_fusion.near_ref, ...), custom_call_target="tpu_custom_call" | custom-call | flops 2700000000 | bytes 2000000 | tf_op jit(solution)/shard_map/tangent/pallas_call | solution.py:142
  (3 shorter events, 0.0 us)
Async XLA Ops:
  2.3 11.8 %copy-start.3 = (f32[16,256]{1,0:T(8,128)S(1)}, f32[16,256]{1,0:T(8,128)}, u32[]{:S(2)}) copy-start(f32[16,256]{1,0:T(8,128)} %param.9) | copy-start | bytes 49156
  2.3 11.8 %copy-start.4 = (s32[16,256]{1,0:T(8,128)S(1)}, s32[16,256]{1,0:T(8,128)}, u32[]{:S(2)}) copy-start(s32[16,256]{1,0:T(8,128)} %param.8) | copy-start | bytes 49156
  2.3 29.6 %copy-start.1 = (f32[512,256]{1,0:T(8,128)S(1)}, f32[512,256]{1,0:T(8,128)}, u32[]{:S(2)}) copy-start(f32[512,256]{1,0:T(8,128)} %constant.11.clone.table_ref) | copy-start | bytes 1572868
  2.3 29.6 %all-to-all-start = ((bf16[16,72,256]{2,1,0:T(8,128)(2,1)}), bf16[16,72,256]{2,1,0:T(8,128)(2,1)S(1)}, u32[]{:S(2)}, u32[]{:S(2)}) async-start(bf16[16,72,256]{2,1,0:T(8,128)(2,1)} %broadcast_in_dim.5), calls=%async_computation | async-start | bytes 1179648 | tf_op jit(solution)/shard_map/all_to_all | solution.py:126
  14.1 17.8 %copy-start.2 = (bf16[256,512]{1,0:T(8,128)(2,1)S(1)}, bf16[256,512]{1,0:T(8,128)(2,1)}, u32[]{:S(2)}) copy-start(bf16[256,512]{1,0:T(8,128)(2,1)} %constant.12.clone.second_ref) | copy-start | bytes 786436
  14.2 1.3 %collective-permute-start = (bf16[32,256]{1,0:T(8,128)(2,1)S(1)}, bf16[32,256]{1,0:T(8,128)(2,1)S(1)}, u32[]{:S(2)}, u32[]{:S(2)}) collective-permute-start(bf16[32,256]{1,0:T(8,128)(2,1)S(1)} %pad_maximum_fusion.2), channel_id=1, source_target_pairs={{0,1},{1,0},{2,3},{3,2},{4,5},{5,4},{6,7},{7,6},{8,9},{9,8},{10,11... | collective-permute-start | bytes 49160 | tf_op jit(solution)/shard_map/ppermute | solution.py:132
  15.5 6.5 %collective-permute-start.3 = (bf16[2,32,256]{2,1,0:T(8,128)(2,1)S(1)}, bf16[2,32,256]{2,1,0:T(8,128)(2,1)S(1)}, u32[]{:S(2)}, u32[]{:S(2)}) collective-permute-start(bf16[2,32,256]{2,1,0:T(8,128)(2,1)S(1)} %pad_maximum_fusion.1.pair_ref), channel_id=1, source_target_pairs={{0,14},{1,7},{2,12},{3,5},{4,10},{5,3},{6,8},{7,1},{8,6},{9,15},{1... | collective-permute-start | bytes 98312 | tf_op jit(solution)/shard_map/ppermute | solution.py:133
  16.1 6.5 %collective-permute-start.2 = (bf16[2,32,256]{2,1,0:T(8,128)(2,1)S(1)}, bf16[2,32,256]{2,1,0:T(8,128)(2,1)S(1)}, u32[]{:S(2)}, u32[]{:S(2)}) collective-permute-start(bf16[2,32,256]{2,1,0:T(8,128)(2,1)S(1)} %pad_maximum_fusion.1.pair_ref), channel_id=1, source_target_pairs={{0,12},{1,5},{2,14},{3,7},{4,8},{5,1},{6,10},{7,3},{8,4},{9,13},{1... | collective-permute-start | bytes 98312 | tf_op jit(solution)/shard_map/ppermute | solution.py:133
  19.6 5.1 %collective-permute-start.1 = (bf16[2,32,256]{2,1,0:T(8,128)(2,1)S(1)}, bf16[2,32,256]{2,1,0:T(8,128)(2,1)S(1)}, u32[]{:S(2)}, u32[]{:S(2)}) collective-permute-start(bf16[2,32,256]{2,1,0:T(8,128)(2,1)S(1)} %pad_maximum_fusion.1.pair_ref), channel_id=1, source_target_pairs={{0,10},{1,3},{2,8},{3,1},{4,14},{5,7},{6,12},{7,5},{8,2},{9,11},{1... | collective-permute-start | bytes 98312 | tf_op jit(solution)/shard_map/ppermute | solution.py:133
  20.6 4.9 %collective-permute-start.4 = (bf16[2,32,256]{2,1,0:T(8,128)(2,1)S(1)}, bf16[2,32,256]{2,1,0:T(8,128)(2,1)S(1)}, u32[]{:S(2)}, u32[]{:S(2)}) collective-permute-start(bf16[2,32,256]{2,1,0:T(8,128)(2,1)S(1)} %pad_maximum_fusion.1.pair_ref), channel_id=1, source_target_pairs={{0,8},{1,9},{2,10},{3,11},{4,12},{5,13},{6,14},{7,15},{8,0},{9,1},... | collective-permute-start | bytes 98312 | tf_op jit(solution)/shard_map/ppermute | solution.py:134
  24.7 1.4 %collective-permute-start.5 = (bf16[3,2,32,256]{3,2,1,0:T(8,128)(2,1)S(1)}, bf16[3,2,32,256]{3,2,1,0:T(8,128)(2,1)S(1)}, u32[]{:S(2)}, u32[]{:S(2)}) collective-permute-start(bf16[3,2,32,256]{3,2,1,0:T(8,128)(2,1)S(1)} %pad_maximum_fusion.near_ref), channel_id=1, source_target_pairs={{0,1},{1,0},{2,3},{3,2},{4,5},{5,4},{6,7},{7,6},{8,9},{9,8},{10,11... | collective-permute-start | bytes 294920 | tf_op jit(solution)/shard_map/ppermute | solution.py:135
  24.8 7.1 %copy-start = (s32[16]{0:T(128)S(1)}, s32[16]{0:T(128)}, u32[]{:S(2)}) copy-start(s32[16]{0:T(128)} %block_map.1) | copy-start | bytes 196

commit v10 on v9

--- a/solution.py
+++ b/solution.py
@@ -14,7 +14,7 @@
 
 def peer_order(blocks):
     chips = blocks // 2
-    return [2 * (chips - 1 - i % chips) + i // chips for i in range(blocks)]
+    return [2 * (3 * i % chips) + i // chips for i in range(blocks)]
 
 
 def sensor_table(length, pupil):
@@ -46,7 +46,7 @@
             found.append((near_ref[i, r], me ^ (2 * (i + 5 - 4 * core) + r)))
             found.append((far_ref[i, r], me ^ (2 * (i + 1 + 4 * core) + 1 - r)))
     for part, block in found:
-        at = pl.multiple_of(((block & 1) * half_group + half_group - 1 - (block >> 1)) * height, height)
+        at = pl.multiple_of(((block & 1) * half_group + ((3 * (block >> 1)) & (half_group - 1))) * height, height)
         base[pl.ds(at, height), :pupil] = part[:height]
         base[pl.ds(at, height), pupil:] = part[height:]
     point = jnp.concatenate([modes_ref[i][count * height :].astype(jnp.float32)[:1] for i in range(blocks)], axis=0)
@@ -55,7 +55,7 @@
     place = lax.broadcasted_iota(jnp.int32, (blocks, pupil), 1)
     odd = (place & 1) == 1
     block = place // height
-    row = (2 * (half_group - 1 - block % half_group) + block // half_group) * height + place % height
+    row = (2 * (3 * block % half_group) + block // half_group) * height + place % height
 
     def factor(tilt, index):
         angle = tilt * ((index - pupil // 2).astype(jnp.float32) * scale)

time: 36.6 us -> 36.1 us (0.986)
  starting transfers between devices: 18.4 us -> 18 us
    all_to_all x1, starting transfers between devices: 11.8 us -> 11.3 us  [local(): gathered = lax.all_to_all(spread, 'mod', 0, 0, axis_index_groups=[order])]
where the time goes in v10:
time: 36.1 us; the launch traced here: 35.8 us
  starting transfers between devices  18 us (50%)
  waiting for transfers between devices  10.8 us (30%)
  Pallas kernels  4.42 us (12%)
  local copies, waits for them, and re-layouts  1.64 us (5%)
  between operations  0.74 us (2%)
    all_to_all x1, starting transfers between devices, local(): gathered = lax.all_to_all(spread, 'mod', 0, 0, axis_index_groups=[order])  11.3 us
    all_to_all x1, waiting for transfers between devices, local(): gathered = lax.all_to_all(spread, 'mod', 0, 0, axis_index_groups=[order])  5.78 us
    ppermute x3, starting transfers between devices, local(): lax.ppermute(pair, 'mode', pairs(t + 4, t))  5.11 us
    pallas_call x1, Pallas kernels, local(): pl.pallas_call(tangent_kernel, in_specs=[smem, smem] + [vmem] * 7, out_sp...  4.42 us
    ppermute x3, waiting for transfers between devices, local(): lax.ppermute(pair, 'mode', pairs(t + 4, t))  2.69 us
    ppermute x1, starting transfers between devices, local(): fourth = lax.ppermute(pair, 'mode', pairs(4, 4))  1.35 us
    ppermute x1, waiting for transfers between devices, local(): pair = jnp.stack([field, lax.ppermute(field, 'mode', cores)])  1.17 us
    broadcast_in_dim x1, local copies, waits for them, and re-layouts, local(): spread = jnp.broadcast_to(packed[None], (blocks,) + packed.shape)  0.85 us
  transfers between devices with their start and end apart: 7, of which 6 were waited for; matrix products, arithmetic and copies ran while one was open for 0% of the time, Pallas kernels for 0%

profile of v10, /device:TPU:4, one launch (start us, length us, event | category | flops | bytes accessed | tf_op | source)
XLA Modules:
  0.0 35.8 jit_solution(16244611249812484698)
XLA Ops:
  0.7 0.8 %concatenate.21 = bf16[72,256]{1,0:T(8,128)(2,1)S(1)} pad(bf16[64,256]{1,0:T(8,128)(2,1)} %bitcast.12, bf16[]{:T(256)} %bitcast.3), padding=0_8x0_0 | pad | bytes 69634 | tf_op jit(solution)/shard_map/concatenate | solution.py:124
  1.4 0.9 %broadcast_in_dim.5 = bf16[16,72,256]{2,1,0:T(8,128)(2,1)} broadcast(bf16[72,256]{1,0:T(8,128)(2,1)S(1)} %concatenate.21), dimensions={1,2} | broadcast | bytes 626688 | tf_op jit(solution)/shard_map/broadcast_in_dim | solution.py:125
  2.3 0.0 copy-start.3
  2.3 0.0 copy-start.4
  2.3 0.0 copy-start.1
  2.3 11.3 %all-to-all-start = ((bf16[16,72,256]{2,1,0:T(8,128)(2,1)}), bf16[16,72,256]{2,1,0:T(8,128)(2,1)S(1)}, u32[]{:S(2)}, u32[]{:S(2)}) async-start(bf16[16,72,256]{2,1,0:T(8,128)(2,1)} %broadcast_in_dim.5), calls=%async_computation | async-start | bytes 1179648 | tf_op jit(solution)/shard_map/all_to_all | solution.py:126
  13.6 0.0 copy-done.3
  13.6 0.0 copy-done.4
  13.6 0.0 copy-start.2
  13.7 0.1 multiply_convert_fusion.1
  13.7 0.1 collective-permute-start
  13.8 1.2 %collective-permute-done = bf16[32,256]{1,0:T(8,128)(2,1)S(1)} collective-permute-done((bf16[32,256]{1,0:T(8,128)(2,1)S(1)}, bf16[32,256]{1,0:T(8,128)(2,1)S(1)}, u32[]{:S(2)}, u32[]{:S(2)}) %collective-permute-start) | collective-permute-done | bytes 16416 | tf_op jit(solution)/shard_map/ppermute | solution.py:132
  15.0 0.6 %collective-permute-start.3 = (bf16[2,32,256]{2,1,0:T(8,128)(2,1)S(1)}, bf16[2,32,256]{2,1,0:T(8,128)(2,1)S(1)}, u32[]{:S(2)}, u32[]{:S(2)}) collective-permute-start(bf16[2,32,256]{2,1,0:T(8,128)(2,1)S(1)} %pad_maximum_fusion.1.pair_ref), channel_id=1, source_target_pairs={{0,14},{1,7},{2,12},{3,5},{4,10},{5,3},{6,8},{7,1},{8,6},{9,15},{1... | collective-permute-start | bytes 98312 | tf_op jit(solution)/shard_map/ppermute | solution.py:133
  15.7 3.5 %collective-permute-start.2 = (bf16[2,32,256]{2,1,0:T(8,128)(2,1)S(1)}, bf16[2,32,256]{2,1,0:T(8,128)(2,1)S(1)}, u32[]{:S(2)}, u32[]{:S(2)}) collective-permute-start(bf16[2,32,256]{2,1,0:T(8,128)(2,1)S(1)} %pad_maximum_fusion.1.pair_ref), channel_id=1, source_target_pairs={{0,12},{1,5},{2,14},{3,7},{4,8},{5,1},{6,10},{7,3},{8,4},{9,13},{1... | collective-permute-start | bytes 98312 | tf_op jit(solution)/shard_map/ppermute | solution.py:133
  19.2 0.9 %collective-permute-start.1 = (bf16[2,32,256]{2,1,0:T(8,128)(2,1)S(1)}, bf16[2,32,256]{2,1,0:T(8,128)(2,1)S(1)}, u32[]{:S(2)}, u32[]{:S(2)}) collective-permute-start(bf16[2,32,256]{2,1,0:T(8,128)(2,1)S(1)} %pad_maximum_fusion.1.pair_ref), channel_id=1, source_target_pairs={{0,10},{1,3},{2,8},{3,1},{4,14},{5,7},{6,12},{7,5},{8,2},{9,11},{1... | collective-permute-start | bytes 98312 | tf_op jit(solution)/shard_map/ppermute | solution.py:133
  20.1 1.3 %collective-permute-start.4 = (bf16[2,32,256]{2,1,0:T(8,128)(2,1)S(1)}, bf16[2,32,256]{2,1,0:T(8,128)(2,1)S(1)}, u32[]{:S(2)}, u32[]{:S(2)}) collective-permute-start(bf16[2,32,256]{2,1,0:T(8,128)(2,1)S(1)} %pad_maximum_fusion.1.pair_ref), channel_id=1, source_target_pairs={{0,8},{1,9},{2,10},{3,11},{4,12},{5,13},{6,14},{7,15},{8,0},{9,1},... | collective-permute-start | bytes 98312 | tf_op jit(solution)/shard_map/ppermute | solution.py:134
  21.5 0.0 collective-permute-done.3
  21.5 0.7 %collective-permute-done.2 = bf16[2,32,256]{2,1,0:T(8,128)(2,1)S(1)} collective-permute-done((bf16[2,32,256]{2,1,0:T(8,128)(2,1)S(1)}, bf16[2,32,256]{2,1,0:T(8,128)(2,1)S(1)}, u32[]{:S(2)}, u32[]{:S(2)}) %collective-permute-start.2) | collective-permute-done | bytes 32800 | tf_op jit(solution)/shard_map/ppermute | solution.py:133
  22.2 2.0 %collective-permute-done.1 = bf16[2,32,256]{2,1,0:T(8,128)(2,1)S(1)} collective-permute-done((bf16[2,32,256]{2,1,0:T(8,128)(2,1)S(1)}, bf16[2,32,256]{2,1,0:T(8,128)(2,1)S(1)}, u32[]{:S(2)}, u32[]{:S(2)}) %collective-permute-start.1) | collective-permute-done | bytes 32800 | tf_op jit(solution)/shard_map/ppermute | solution.py:133
  24.2 0.1 collective-permute-start.5
  24.3 0.0 copy-start
  24.3 0.1 pad_add_fusion.ids
  24.4 0.5 %collective-permute-done.4.fourth_ref = bf16[2,32,256]{2,1,0:T(8,128)(2,1)S(1)} collective-permute-done((bf16[2,32,256]{2,1,0:T(8,128)(2,1)S(1)}, bf16[2,32,256]{2,1,0:T(8,128)(2,1)S(1)}, u32[]{:S(2)}, u32[]{:S(2)}) %collective-permute-start.4) | collective-permute-done | bytes 32800 | tf_op jit(solution)/shard_map/ppermute | solution.py:134
  24.8 0.7 %collective-permute-done.5.far_ref = bf16[3,2,32,256]{3,2,1,0:T(8,128)(2,1)S(1)} collective-permute-done((bf16[3,2,32,256]{3,2,1,0:T(8,128)(2,1)S(1)}, bf16[3,2,32,256]{3,2,1,0:T(8,128)(2,1)S(1)}, u32[]{:S(2)}, u32[]{:S(2)}) %collective-permute-start.5) | collective-permute-done | bytes 98336 | tf_op jit(solution)/shard_map/ppermute | solution.py:135
  25.6 5.8 %all-to-all-done.modes_ref = bf16[16,72,256]{2,1,0:T(8,128)(2,1)S(1)} async-done(((bf16[16,72,256]{2,1,0:T(8,128)(2,1)}), bf16[16,72,256]{2,1,0:T(8,128)(2,1)S(1)}, u32[]{:S(2)}, u32[]{:S(2)}) %all-to-all-start) | async-done | bytes 589856 | tf_op jit(solution)/shard_map/all_to_all | solution.py:126
  31.4 0.0 copy-done.1
  31.4 0.0 copy-done.2
  31.4 0.0 copy-done
  31.4 4.4 %tangent.1 = f32[32,4,512]{2,1,0:T(4,128)} custom-call(s32[16]{0:T(128)S(1)} %copy-done, s32[2]{0:T(128)S(1)} %pad_add_fusion.ids, bf16[16,72,256]{2,1,0:T(8,128)(2,1)S(1)} %all-to-all-done.modes_ref, bf16[2,32,256]{2,1,0:T(8,128)(2,1)S(1)} %pad_maximum_fusion.1.pair_ref, bf16[3,2,32,256]{3,2,1,0:T(8,128)(2,1)S(1)} %pad_maximum_fusion.near_ref, ...), custom_call_target="tpu_custom_call" | custom-call | flops 2700000000 | bytes 2000000 | tf_op jit(solution)/shard_map/tangent/pallas_call | solution.py:142
  (3 shorter events, 0.0 us)
Async XLA Ops:
  2.3 11.3 %copy-start.3 = (f32[16,256]{1,0:T(8,128)S(1)}, f32[16,256]{1,0:T(8,128)}, u32[]{:S(2)}) copy-start(f32[16,256]{1,0:T(8,128)} %param.9) | copy-start | bytes 49156
  2.3 11.4 %copy-start.4 = (s32[16,256]{1,0:T(8,128)S(1)}, s32[16,256]{1,0:T(8,128)}, u32[]{:S(2)}) copy-start(s32[16,256]{1,0:T(8,128)} %param.8) | copy-start | bytes 49156
  2.3 29.1 %copy-start.1 = (f32[512,256]{1,0:T(8,128)S(1)}, f32[512,256]{1,0:T(8,128)}, u32[]{:S(2)}) copy-start(f32[512,256]{1,0:T(8,128)} %constant.11.clone.table_ref) | copy-start | bytes 1572868
  2.3 29.1 %all-to-all-start = ((bf16[16,72,256]{2,1,0:T(8,128)(2,1)}), bf16[16,72,256]{2,1,0:T(8,128)(2,1)S(1)}, u32[]{:S(2)}, u32[]{:S(2)}) async-start(bf16[16,72,256]{2,1,0:T(8,128)(2,1)} %broadcast_in_dim.5), calls=%async_computation | async-start | bytes 1179648 | tf_op jit(solution)/shard_map/all_to_all | solution.py:126
  13.6 17.7 %copy-start.2 = (bf16[256,512]{1,0:T(8,128)(2,1)S(1)}, bf16[256,512]{1,0:T(8,128)(2,1)}, u32[]{:S(2)}) copy-start(bf16[256,512]{1,0:T(8,128)(2,1)} %constant.12.clone.second_ref) | copy-start | bytes 786436
  13.7 1.3 %collective-permute-start = (bf16[32,256]{1,0:T(8,128)(2,1)S(1)}, bf16[32,256]{1,0:T(8,128)(2,1)S(1)}, u32[]{:S(2)}, u32[]{:S(2)}) collective-permute-start(bf16[32,256]{1,0:T(8,128)(2,1)S(1)} %pad_maximum_fusion.2), channel_id=1, source_target_pairs={{0,1},{1,0},{2,3},{3,2},{4,5},{5,4},{6,7},{7,6},{8,9},{9,8},{10,11... | collective-permute-start | bytes 49160 | tf_op jit(solution)/shard_map/ppermute | solution.py:132
  15.0 6.5 %collective-permute-start.3 = (bf16[2,32,256]{2,1,0:T(8,128)(2,1)S(1)}, bf16[2,32,256]{2,1,0:T(8,128)(2,1)S(1)}, u32[]{:S(2)}, u32[]{:S(2)}) collective-permute-start(bf16[2,32,256]{2,1,0:T(8,128)(2,1)S(1)} %pad_maximum_fusion.1.pair_ref), channel_id=1, source_target_pairs={{0,14},{1,7},{2,12},{3,5},{4,10},{5,3},{6,8},{7,1},{8,6},{9,15},{1... | collective-permute-start | bytes 98312 | tf_op jit(solution)/shard_map/ppermute | solution.py:133
  15.7 6.5 %collective-permute-start.2 = (bf16[2,32,256]{2,1,0:T(8,128)(2,1)S(1)}, bf16[2,32,256]{2,1,0:T(8,128)(2,1)S(1)}, u32[]{:S(2)}, u32[]{:S(2)}) collective-permute-start(bf16[2,32,256]{2,1,0:T(8,128)(2,1)S(1)} %pad_maximum_fusion.1.pair_ref), channel_id=1, source_target_pairs={{0,12},{1,5},{2,14},{3,7},{4,8},{5,1},{6,10},{7,3},{8,4},{9,13},{1... | collective-permute-start | bytes 98312 | tf_op jit(solution)/shard_map/ppermute | solution.py:133
  19.2 5.0 %collective-permute-start.1 = (bf16[2,32,256]{2,1,0:T(8,128)(2,1)S(1)}, bf16[2,32,256]{2,1,0:T(8,128)(2,1)S(1)}, u32[]{:S(2)}, u32[]{:S(2)}) collective-permute-start(bf16[2,32,256]{2,1,0:T(8,128)(2,1)S(1)} %pad_maximum_fusion.1.pair_ref), channel_id=1, source_target_pairs={{0,10},{1,3},{2,8},{3,1},{4,14},{5,7},{6,12},{7,5},{8,2},{9,11},{1... | collective-permute-start | bytes 98312 | tf_op jit(solution)/shard_map/ppermute | solution.py:133
  20.1 4.7 %collective-permute-start.4 = (bf16[2,32,256]{2,1,0:T(8,128)(2,1)S(1)}, bf16[2,32,256]{2,1,0:T(8,128)(2,1)S(1)}, u32[]{:S(2)}, u32[]{:S(2)}) collective-permute-start(bf16[2,32,256]{2,1,0:T(8,128)(2,1)S(1)} %pad_maximum_fusion.1.pair_ref), channel_id=1, source_target_pairs={{0,8},{1,9},{2,10},{3,11},{4,12},{5,13},{6,14},{7,15},{8,0},{9,1},... | collective-permute-start | bytes 98312 | tf_op jit(solution)/shard_map/ppermute | solution.py:134
  24.2 1.4 %collective-permute-start.5 = (bf16[3,2,32,256]{3,2,1,0:T(8,128)(2,1)S(1)}, bf16[3,2,32,256]{3,2,1,0:T(8,128)(2,1)S(1)}, u32[]{:S(2)}, u32[]{:S(2)}) collective-permute-start(bf16[3,2,32,256]{3,2,1,0:T(8,128)(2,1)S(1)} %pad_maximum_fusion.near_ref), channel_id=1, source_target_pairs={{0,1},{1,0},{2,3},{3,2},{4,5},{5,4},{6,7},{7,6},{8,9},{9,8},{10,11... | collective-permute-start | bytes 294920 | tf_op jit(solution)/shard_map/ppermute | solution.py:135
  24.3 7.1 %copy-start = (s32[16]{0:T(128)S(1)}, s32[16]{0:T(128)}, u32[]{:S(2)}) copy-start(s32[16]{0:T(128)} %block_map.1) | copy-start | bytes 196
